TPU v7x, 32 devices: a whole 2x2x4 slice. The times are simulated.
32 devices in a mesh: img: 8 (over z, y), ch: 4 (over x, core).
Axes of the slice: x: 2, y: 2, z: 4, core: 2. Of those that a mesh axis runs over, the one named last changes fastest.
Arguments:
- x_big: bfloat16 [64, 14, 14, 1024], P('img', None, None, 'ch'), may hold values from -6 to 6
- x_small: bfloat16 [64, 10, 10, 1024], P('img', None, None, 'ch'), may hold values from -6 to 6
- cot_big: bfloat16 [64, 7, 7, 2048], P('img', None, None, 'ch'), may hold values from -6 to 6
- cot_small: bfloat16 [64, 5, 5, 2048], P('img', None, None, 'ch'), may hold values from -6 to 6
- counts: int32 [8, 2], replicated, may hold values from 1 to 8, as said below
- w_reduce: bfloat16 [1024, 256], P(None, 'ch'), may hold values from -0.1875 to 0.1875
- w_mix: bfloat16 [3, 3, 256, 256], P(None, None, None, 'ch'), may hold values from -0.125 to 0.125
- w_expand: bfloat16 [256, 1024], P(None, 'ch'), may hold values from -0.375 to 0.375
- w_narrow: bfloat16 [1024, 512], P(None, 'ch'), may hold values from -0.1875 to 0.1875
- w_stride: bfloat16 [3, 3, 512, 512], P(None, None, None, 'ch'), may hold values from -0.09375 to 0.09375
- w_widen: bfloat16 [512, 2048], P(None, 'ch'), may hold values from -0.25 to 0.25
- w_short: bfloat16 [1024, 2048], P(None, 'ch'), may hold values from -0.1875 to 0.1875
- gain_mid3: float32 [2, 256], P(None, 'ch'), may hold values from 0.1 to 1.9
- shift_mid3: float32 [2, 256], P(None, 'ch'), may hold values from -3 to 3
- gain_out3: float32 [1024], P('ch'), may hold values from 0.1 to 1.9
- shift_out3: float32 [1024], P('ch'), may hold values from -3 to 3
- gain_mid4: float32 [2, 512], P(None, 'ch'), may hold values from 0.1 to 1.9
- shift_mid4: float32 [2, 512], P(None, 'ch'), may hold values from -3 to 3
- gain_out4: float32 [2, 2048], P(None, 'ch'), may hold values from 0.1 to 1.9
- shift_out4: float32 [2, 2048], P(None, 'ch'), may hold values from -3 to 3
Outputs:
- out_big: float32 [64, 7, 7, 2048], P('img', None, None, 'ch')
- out_small: float32 [64, 5, 5, 2048], P('img', None, None, 'ch')
- grad_x_big: float32 [64, 14, 14, 1024], P('img', None, None, 'ch')
- grad_x_small: float32 [64, 10, 10, 1024], P('img', None, None, 'ch')
- grad_w_reduce: float32 [1024, 256], P(None, 'ch')
- grad_w_mix: float32 [3, 3, 256, 256], P(None, None, None, 'ch')
- grad_w_expand: float32 [256, 1024], P(None, 'ch')
- grad_w_narrow: float32 [1024, 512], P(None, 'ch')
- grad_w_stride: float32 [3, 3, 512, 512], P(None, None, None, 'ch')
- grad_w_widen: float32 [512, 2048], P(None, 'ch')
- grad_w_short: float32 [1024, 2048], P(None, 'ch')
- grad_gain_mid3: float32 [2, 256], P(None, 'ch')
- grad_shift_mid3: float32 [2, 256], P(None, 'ch')
- grad_gain_out3: float32 [1024], P('ch')
- grad_shift_out3: float32 [1024], P('ch')
- grad_gain_mid4: float32 [2, 512], P(None, 'ch')
- grad_shift_mid4: float32 [2, 512], P(None, 'ch')
- grad_gain_out4: float32 [2, 2048], P(None, 'ch')
- grad_shift_out4: float32 [2, 2048], P(None, 'ch')
Inputs may be any that keep to these rules, and one draw needn't show every extreme that they name: `counts`: column 0 lies between 1 and 8, column 1 between 1 and 8; in every draw some index is full in column 0 and some in column 1. The live views of a device are its first slots.
All inputs are finite; a program needn't handle non-finite values.
Results may differ from a plain program's by a relative error of at most 0.03.
Values may be sent and summed in bfloat16 or wider, within the bound.
No kernel may reach another device: no remote copies, remote signals or barrier semaphores. Data moves between devices by JAX's collectives and lax.ppermute only.
A program may use at most 192 MiB of HBM per device.

v0:
```python
import functools
import math

import jax
import jax.numpy as jnp
from jax import lax
from jax.experimental import pallas as pl
from jax.experimental.pallas import tpu as pltpu
from jax.sharding import PartitionSpec as P

EPS = 1e-05
G0 = 0.7978845608028654
G1 = G0 * 0.044715
F32 = jnp.float32
BF16 = jnp.bfloat16
VIEWS = 8

ANY = pl.BlockSpec(memory_space=pl.ANY)
HBM = pl.BlockSpec(memory_space=pltpu.HBM)
VMEM = pl.BlockSpec(memory_space=pltpu.VMEM)
SMEM = pl.BlockSpec(memory_space=pltpu.SMEM)


def sds(shape, dtype=F32):
    return jax.ShapeDtypeStruct(tuple(shape), dtype)


class Flow:
    WHOLE = ("w", "w4", "all", "chip", "w_in", "w_ahead", "w_back")

    def __init__(self, kind, base=0, shape=None, which=0):
        self.kind, self.base, self.shape, self.which = kind, base, shape, which

    def keys(self, geo, shape):
        parts = (0, 1)
        if self.kind in ("big", "big_px"):
            parts = (0,)
        if self.kind in ("small", "small_px"):
            parts = (1,)
        if self.kind not in ("lead",) + self.WHOLE:
            return [(part, n) for part in parts for n in range(len(geo.groups[part]))]
        if self.kind == "lead":
            return list(range(shape[0]))
        return [None]

    def buffer(self, geo, shapes, dtype):
        if self.kind == "x":
            return pltpu.VMEM((4, geo.rows, shapes[0][1]), dtype)
        if self.kind == "w":
            return pltpu.VMEM(self.shape, dtype)
        if self.kind in ("chip", "w4"):
            return pltpu.VMEM(self.shape, dtype)
        c = shapes[0][-1]
        if self.kind.startswith("w_"):
            return pltpu.VMEM({"w_in": (4, c, c), "w_ahead": (3, c, 3 * c), "w_back": (9, c, c)}[self.kind], dtype)
        return pltpu.VMEM(tuple(shapes[0]), dtype)

    def pairs(self, geo, q, hbm, buf, key):
        if self.kind == "w":
            rows, n = buf.shape[0], buf.shape[1] // 4
            found = []
            for p in range(4):
                for b in range(n // 128):
                    at = pl.ds(pl.multiple_of((q ^ p) * n + 128 * b, 128), 128)
                    found.append((hbm[p].at[pl.ds(self.base + rows * b, rows)], buf.at[:, at]))
            return found
        if self.kind.startswith("w_"):
            c = buf.shape[1]
            n = c // 4
            found = []
            for p in range(4):
                at = pl.ds(pl.multiple_of((q ^ p) * n, n), n)
                for t in range(4 if self.kind == "w_in" else 9):
                    src = hbm[p].at[pl.ds(self.base + n * t, n)]
                    if self.kind == "w_ahead":
                        found.append((src, buf.at[t // 3, at, pl.ds(t % 3 * c, c)]))
                    else:
                        found.append((src, buf.at[t, at]))
            return found
        if self.kind == "chip":
            return [(hbm[0].at[(q >> 1) ^ self.which, pl.ds(self.base, buf.shape[0])], buf)]
        if self.kind == "w4":
            n = buf.shape[1] // 4
            found = []
            for chip in range(2):
                for other in range(2):
                    at = pl.multiple_of((2 * chip + ((q & 1) ^ other)) * n, n)
                    found.append((hbm[other].at[chip], buf.at[:, pl.ds(at, n)]))
            return found
        if key is None:
            return [(hbm[0], buf)]
        if self.kind == "lead":
            return [(hbm[0].at[key], buf.at[key])]
        part, group = key
        i, end = geo.groups[part][group]
        pix, npx, row, nrows = geo.step(part, i)
        npx, nrows, first = npx * (end - i), nrows * (end - i), pix - geo.parts[part][1]
        if self.kind == "px":
            at = pl.ds(pix, npx)
        elif self.kind == "rows":
            at = pl.ds(row, nrows)
        elif self.kind in ("big_px", "small_px"):
            at = pl.ds(first, npx)
        elif self.kind == "x":
            local = pl.ds(first * VIEWS, nrows)
            return [
                (hbm[4 * part + p].at[local], buf.at[q ^ p, pl.ds(row, nrows)]) for p in range(4)
            ]
        else:
            at = pl.ds(i, end - i)
            return [(hbm[0].at[:, :, at], buf.at[:, :, at])]
        return [(hbm[0].at[at], buf.at[at])]


class Moves:
    def __init__(self, geo, q, ahead):
        self.geo, self.q, self.flows, self.kept, self.ahead = geo, q, [], [], ahead

    def add(self, flow, hbm, buf, sem, inward):
        self.flows.append((flow, hbm, buf, sem, inward))

    def copies(self, entry, key):
        flow, hbm, buf, sem, inward = entry
        if flow.kind in flow.WHOLE:
            at = 0
        elif flow.kind == "lead":
            at = key
        elif flow.kind in ("px", "rows", "x"):
            at = (0, len(self.geo.groups[0]))[key[0]] + key[1]
        else:
            at = key[1]
        pairs = flow.pairs(self.geo, self.q, hbm, buf, key)
        return [
            pltpu.make_async_copy(*((a, b) if inward else (b, a)), sem.at[n, at])
            for n, (a, b) in enumerate(pairs)
        ]

    def entries(self, inward, key):
        for entry in self.flows:
            flow = entry[0]
            if entry[4] != inward:
                continue
            if key is None:
                fits = flow.kind in flow.WHOLE
            elif isinstance(key, int):
                fits = flow.kind == "lead" and key < entry[1][0].shape[0]
            else:
                kinds = ("px", "rows", "x") + (("big", "big_px"), ("small", "small_px"))[key[0]]
                fits = flow.kind in kinds
            if fits:
                yield entry

    def start(self, inward, key):
        for entry in self.entries(inward, key):
            for c in self.copies(entry, key):
                c.start()

    def wait(self, inward, key):
        for entry in self.entries(inward, key):
            for c in self.copies(entry, key):
                c.wait()

    def begin(self, hold):
        self.order = [(part, n) for part in range(2) for n in range(len(self.geo.groups[part]))]
        if hold:
            self.start(True, None)
            return
        self.start(True, self.order[0])
        self.start(True, None)
        for key in self.order[1 : self.ahead]:
            self.start(True, key)
        for n in range(self.ahead):
            self.start_lead(n)
        streams = any(e[4] and e[0].kind not in ("lead",) + Flow.WHOLE for e in self.flows)
        if not streams:
            for c in self.kept:
                c.start()

    def start_steps(self):
        for key in self.order:
            self.start(True, key)

    def start_lead(self, n):
        for entry in self.flows:
            if entry[4] and entry[0].kind == "lead" and n < entry[1][0].shape[0]:
                for c in self.copies(entry, n):
                    c.start()

    def ready(self):
        self.wait(True, None)

    def arrive(self, *key):
        if len(key) == 1:
            self.wait(True, key[0])
            self.start_lead(key[0] + self.ahead)
            return
        self.wait(True, key)
        at = self.order.index(key)
        if at + self.ahead < len(self.order):
            self.start(True, self.order[at + self.ahead])
        streams = any(e[4] and e[0].kind not in ("lead",) + Flow.WHOLE for e in self.flows)
        if at == 0 and streams:
            for c in self.kept:
                c.start()

    def leave(self, *key):
        self.start(False, key if len(key) > 1 else key[0])

    def send(self, *refs):
        for entry in self.entries(False, None):
            if any(entry[2] is r for r in refs):
                for c in self.copies(entry, None):
                    c.start()

    def finish(self):
        for entry in self.flows:
            if not entry[4]:
                shape = entry[1][0].shape
                for key in entry[0].keys(self.geo, shape):
                    for c in self.copies(entry, key):
                        c.wait()
        for c in self.kept:
            c.wait()


class Keep:
    kind = "keep"

    def __init__(self, source):
        self.source = source


def fast(shape, dtype=F32):
    return pltpu.VMEM(tuple(shape), dtype)


def scoped_bytes(v):
    return math.prod(v.shape) * jnp.dtype(v.dtype).itemsize


def in_hbm(v):
    return pltpu.with_memory_space_constraint(v, pltpu.HBM)


def call(name, kernel, ins, outs, scratch=(), cost=None, order=False, geo=None, slack=14, ahead=3, hold=False, staying=0):
    if order:
        inner, n_in, n_out = kernel, len(ins), len(outs)

        def kernel(*refs):
            rest = refs[n_in:]
            return inner(*refs[:n_in], *rest[n_out:], *rest[:n_out])

    outs = [o if isinstance(o, tuple) else (o, VMEM) for o in outs]
    arrays, specs, moved = [], [], []
    for a, spec in ins:
        group = a if isinstance(a, list) else [a]
        flow = isinstance(spec, Flow)
        arrays += [in_hbm(v) for v in group] if flow else group
        specs += [HBM if flow else spec] * len(group)
        moved.append((spec if flow else None, len(group), [v.shape for v in group], group[0].dtype))
    out_shapes, out_specs = [], []
    for shape, spec in outs:
        flow = isinstance(spec, (Flow, Keep))
        out_shapes.append(pltpu.HBM(shape.shape, shape.dtype) if flow else shape)
        out_specs.append(HBM if flow else spec)
        moved.append((spec if flow else None, 1, [shape.shape], shape.dtype))
    extra = []
    for flow, _, shapes, dtype in moved:
        if isinstance(flow, Keep):
            extra += [pltpu.SemaphoreType.DMA((1,))]
        elif flow:
            keys = len(flow.keys(geo, shapes[0]))
            copies = {"x": 4, "w": 4, "w4": 4, "w_in": 16, "w_ahead": 36, "w_back": 36}.get(flow.kind, 1)
            if flow.kind == "w":
                copies = flow.shape[1] // 128
            extra += [flow.buffer(geo, shapes, dtype), pltpu.SemaphoreType.DMA((copies, keys))]
    body = kernel
    if extra:

        def body(*refs):
            n_io = sum(n for _, n, _, _ in moved)
            given, own, rest = list(refs[:n_io]), refs[n_io : n_io + len(scratch)], refs[n_io + len(scratch) :]
            rest = list(rest)
            moves = Moves(geo, given[0][0], ahead)
            args = []
            for n, (flow, count, _, _) in enumerate(moved):
                group, given = given[:count], given[count:]
                if not flow:
                    args += group
                    continue
                if isinstance(flow, Keep):
                    moves.kept.append(pltpu.make_async_copy(args[flow.source], group[0], rest[0].at[0]))
                    rest = rest[1:]
                    continue
                buf, sem = rest[:2]
                rest = rest[2:]
                moves.add(flow, group, buf, sem, n < len(ins))
                args.append(buf)
            moves.begin(hold)
            kernel(moves, *args, *own)
            moves.finish()

    scratch = list(scratch)
    def held(v):
        pinned = "vmem" in str(getattr(v, "memory_space", "")).lower()
        return 0 if pinned else scoped_bytes(v)

    need = sum(held(jax.typeof(a)) for a, spec in zip(arrays, specs) if spec is VMEM)
    need += sum(held(o) for o, spec in zip(out_shapes, out_specs) if spec is VMEM)
    need += sum(
        scoped_bytes(v)
        for v in scratch + extra
        if getattr(v, "memory_space", None) == pltpu.VMEM
    )
    need -= staying
    result = pl.pallas_call(
        body,
        out_shape=out_shapes,
        in_specs=specs,
        out_specs=out_specs,
        scratch_shapes=scratch + extra,
        compiler_params=pltpu.CompilerParams(vmem_limit_bytes=need + need // 16 + (slack << 20)),
        cost_estimate=cost,
        name=name,
    )(*arrays)
    return list(result)


def vm(*arrays):
    return [(a, VMEM) for a in arrays]


def nn(a, b):
    return lax.dot_general(a, b, (((1,), (0,)), ((), ())), preferred_element_type=F32)


def nt(a, b):
    return lax.dot_general(a, b, (((1,), (1,)), ((), ())), preferred_element_type=F32)


def tn(a, b):
    return lax.dot_general(a, b, (((0,), (0,)), ((), ())), preferred_element_type=F32)


def gelu(t):
    half = 0.5 * t
    return half + half * jnp.tanh(t * (G0 + G1 * (t * t)))


def gelu_both(t):
    sq = t * t
    half = 0.5 * t
    th = jnp.tanh(t * (G0 + G1 * sq))
    return half + half * th, 0.5 + 0.5 * th + half * (1.0 - th * th) * (G0 + (3.0 * G1) * sq)


def gelu_slope(t):
    sq = t * t
    th = jnp.tanh(t * (G0 + G1 * sq))
    return 0.5 * (1.0 + th) + (0.5 * t) * (1.0 - th * th) * (G0 + (3.0 * G1) * sq)


def live_rows(count, chans):
    return (lax.broadcasted_iota(jnp.int32, (VIEWS, chans), 0) < count).astype(F32)


def rows_sum(v):
    return jnp.sum(v, axis=0, keepdims=True)


def merged(sa, sb, na, nb):
    total = na + nb
    mean = (na * sa[0:1] + nb * sb[0:1]) / total
    diff = sb[0:1] - sa[0:1]
    square = sa[1:2] + sb[1:2] + diff * diff * (na * nb / total)
    return mean, lax.rsqrt(square / total + EPS)


def as_rows(v):
    return v.reshape(v.shape[0] * v.shape[1], v.shape[2])


def as_pix_rows(v):
    return v.reshape(v.shape[0] * v.shape[1], VIEWS, v.shape[3])


def as_pix(v):
    return v.reshape(v.shape[0] // VIEWS, VIEWS, v.shape[1])


class Geo:
    def __init__(self, hb, hs):
        self.hb, self.hs = hb, hs
        self.pb, self.ps = hb * hb, hs * hs
        self.px = self.pb + self.ps
        self.rows = self.px * VIEWS
        self.qb, self.qs = self.pb // 4, self.ps // 4
        self.px4 = self.qb + self.qs
        self.rows4 = self.px4 * VIEWS
        self.parts = ((hb, 0), (hs, self.pb))
        self.groups = [self.cuts(hb // 2, 1), self.cuts(hs // 2, 2)]
        self.spans = [[list(range(n))[: n // 2], list(range(n))[n // 2 :]] for n in map(len, self.groups)]
        self.bands = [[(0, hb // 2), (hb // 2, hb)], [(0, hs)]]

    @staticmethod
    def cuts(steps, first):
        at = sorted({0, steps} | set(range(first, steps, 2)))
        return list(zip(at[:-1], at[1:]))

    @staticmethod
    def aligned(n):
        return n if isinstance(n, int) else pl.multiple_of(n, 16)

    def step(self, part, i):
        side, start = self.parts[part]
        npx = 2 * side
        return start + i * npx, npx, self.aligned((start + i * npx) * VIEWS), npx * VIEWS

    def staged(self, io, before, product, carries):
        out = []
        for part in range(2):
            carry = carries[part]
            for span in self.spans[part]:
                lo, hi = self.groups[part][span[0]][0], self.groups[part][span[-1]][1]
                for n in span:
                    io.arrive(part, n)
                pix, npx, row, nrows = self.step(part, lo)
                if before:

                    def early(i, c, part=part):
                        before(part, i, *self.step(part, i))
                        return c

                    lax.fori_loop(lo, hi, early, 0)
                carry = product(part, pix, npx * (hi - lo), row, nrows * (hi - lo), carry)
                for n in span:
                    io.leave(part, n)
            out.append(carry)
        return out

    def loop(self, body, carries, arrive=None, leave=None):
        out = []
        for part in range(2):

            def run(i, carry, part=part):
                for n, (lo, hi) in enumerate(self.groups[part]):
                    if arrive:
                        pl.when(i == lo)(functools.partial(arrive.arrive, part, n))
                carry = body(part, i, *self.step(part, i), carry)
                for n, (lo, hi) in enumerate(self.groups[part]):
                    if leave:
                        pl.when(i == hi - 1)(functools.partial(leave.leave, part, n))
                return carry

            out.append(lax.fori_loop(0, self.groups[part][-1][1], run, carries[part]))
        return out


def finish_stats(geo, ref, sums, lives, count, out, quarter=None):
    mean = (rows_sum(sums[0] * lives[0]) + rows_sum(sums[1] * lives[1])) / count

    def body(part, i, pix, npx, row, nrows, carry):
        dev = ref[pl.ds(pix, npx)] - mean
        return carry + jnp.sum(dev * dev, axis=0)

    zero = jnp.zeros(sums[0].shape, F32)
    sq = geo.loop(body, [zero, zero])
    out[0:1] = mean
    out[1:2] = rows_sum(sq[0] * lives[0]) + rows_sum(sq[1] * lives[1])


def block_stats(geo, value, lives, count):
    big, small = value[: geo.qb], value[geo.qb :]
    mean = (
        rows_sum(jnp.sum(big, axis=0) * lives[0]) + rows_sum(jnp.sum(small, axis=0) * lives[1])
    ) / count
    db, ds = big - mean, small - mean
    square = rows_sum(jnp.sum(db * db, axis=0) * lives[0]) + rows_sum(
        jnp.sum(ds * ds, axis=0) * lives[1]
    )
    return mean, square


def k_reduce(geo, io, me, nf, xs, wt, pre, stats):
    io.ready()
    chans = wt.shape[1]
    lives = [live_rows(me[1], chans), live_rows(me[2], chans)]

    def product(part, pix, npx, row, nrows, carry):
        acc = None
        for j in range(4):
            d = nt(xs[j, row : row + nrows, :], wt[j])
            acc = d if acc is None else acc + d
        z = as_pix(acc)
        pre[pix : pix + npx] = z
        return carry + jnp.sum(z, axis=0)

    zero = jnp.zeros((VIEWS, chans), F32)
    sums = geo.staged(io, None, product, [zero, zero])
    finish_stats(geo, pre, sums, lives, nf[0], stats)


def k_counts(ni, sizes, counts, me, nf3, cnt3, nf4, cnt4):
    img = lax.axis_index("img")
    levels = ni.bit_length() - 1
    me[0] = lax.axis_index("ch").astype(jnp.int32)
    me[1] = counts[img, 0]
    me[2] = counts[img, 1]
    me[3] = img
    for (big, small), nf, cnt in zip(sizes, (nf3, nf4), (cnt3, cnt4)):

        def group(shift, index):
            def add(i, total):
                at = index * (1 << shift) + i
                return total + counts[at, 0] * big + counts[at, 1] * small

            return lax.fori_loop(0, 1 << shift, add, jnp.int32(0)).astype(F32)

        nf[0] = group(0, img)
        for m in range(2):
            nf[1 + m] = group(levels - 1, (img >> (levels - 1)) ^ m)
        row, k = 0, 0
        while k < levels - 1:
            bits = 2 if k == 0 else 1
            for m in range(8):
                cnt[row + m] = group(k, (img >> k) ^ m) if m < 1 << bits else jnp.float32(0.0)
            row, k = row + 8, k + bits


def k_pack_params(gm3, sm3, go3, so3, gm4, sm4, go4, so4, out, rows):
    rows[...] = jnp.zeros(rows.shape, F32)
    rows[0:2, 0:64] = gm3[...]
    rows[2:4, 0:64] = sm3[...]
    for b in range(2):
        lanes = slice(128 * b, 128 * b + 128)
        rows[4 + b : 5 + b] = go3[:, lanes]
        rows[6 + b : 7 + b] = so3[:, lanes]
    rows[8:10] = gm4[...]
    rows[10:12] = sm4[...]
    for n in range(2):
        for b in range(4):
            lanes = slice(128 * b, 128 * b + 128)
            rows[12 + 4 * n + b : 13 + 4 * n + b] = go4[n : n + 1, lanes]
            rows[20 + 4 * n + b : 21 + 4 * n + b] = so4[n : n + 1, lanes]
    v = rows[...]
    high = v.astype(BF16)
    rest = v - high.astype(F32)
    mid = rest.astype(BF16)
    low = (rest - mid.astype(F32)).astype(BF16)
    out[0:32, 0:128] = high
    out[0:32, 128:256] = mid
    out[32:64, 0:128] = low
    out[32:64, 128:256] = jnp.zeros_like(low)


def k_unpack_params(base, me, p0, p1, p2, p3, gs1, gs2, gs3, gs4, gs5, gs6, buf, sem):
    copies = [
        pltpu.make_async_copy(p.at[pl.ds(base, 64)], buf.at[n], sem.at[n])
        for n, p in enumerate((p0, p1, p2, p3))
    ]
    for c in copies:
        c.start()
    for c in copies:
        c.wait()
    rows = []
    for n in range(4):
        v = buf[n].astype(F32)
        rows.append(v[0:32, 0:128] + v[0:32, 128:256] + v[32:64, 0:128])
    odd = me[0] & 1
    for chip in range(2):
        mine, other = rows[2 * chip][:, 0:64], rows[2 * chip + 1][:, 0:64]
        both = jnp.where(
            odd == 0,
            jnp.concatenate([mine, other], axis=1),
            jnp.concatenate([other, mine], axis=1),
        )
        at = pl.ds(pl.multiple_of(((me[0] >> 1) ^ chip) * 128, 128), 128)
        for n, gs in enumerate((gs1, gs2)):
            gs[0:1, at] = both[n : n + 1]
            gs[1:2, at] = both[2 + n : 3 + n]
    for p, v in enumerate(rows):
        for b in range(2):
            at = pl.ds(pl.multiple_of((me[0] ^ p) * 256 + 128 * b, 128), 128)
            gs3[0:1, at] = v[4 + b : 5 + b]
            gs3[1:2, at] = v[6 + b : 7 + b]
        at = pl.ds(pl.multiple_of((me[0] ^ p) * 128, 128), 128)
        for n, gs in enumerate((gs4, gs5)):
            gs[0:1, at] = v[8 + n : 9 + n]
            gs[1:2, at] = v[10 + n : 11 + n]
    for chip in range(2):
        v = rows[2 * chip]
        for n in range(2):
            for b in range(4):
                lanes = slice(128 * b, 128 * b + 128)
                gs6[chip, 2 * n : 2 * n + 1, lanes] = v[12 + 4 * n + b : 13 + 4 * n + b]
                gs6[chip, 2 * n + 1 : 2 * n + 2, lanes] = v[20 + 4 * n + b : 21 + 4 * n + b]


def k_merge(first, n, cnt, *refs):
    arrays, out = refs[:n], refs[n]
    for at in range(0, out.shape[-2], 2):
        mean_at, sq_at = (..., slice(at, at + 1), slice(None)), (..., slice(at + 1, at + 2), slice(None))
        groups = [(cnt[first + m], a[mean_at], a[sq_at]) for m, a in enumerate(arrays)]
        while len(groups) > 1:
            pairs = []
            for (na, ma, qa), (nb, mb, qb) in zip(groups[::2], groups[1::2]):
                total = na + nb
                diff = mb - ma
                pairs.append(
                    (total, (na * ma + nb * mb) / total, qa + qb + diff * diff * (na * nb / total))
                )
            groups = pairs
        out[mean_at], out[sq_at] = groups[0][1], groups[0][2]


def k_add(n, *refs):
    values = [r[...] for r in refs[:n]]
    while len(values) > 1:
        values = [a + b for a, b in zip(values[::2], values[1::2])]
    refs[n][...] = values[0]


def side_shift(v, by):
    zero = jnp.zeros((v.shape[0], 1) + v.shape[2:], v.dtype)
    if by > 0:
        return jnp.concatenate([zero, v[:, :-1]], axis=1)
    return jnp.concatenate([v[:, 1:], zero], axis=1)


def store_shifted(buf, row, nrows, side, v, order):
    img = v.reshape(2, side, VIEWS, v.shape[-1])
    chans = v.shape[-1]
    forms = [side_shift(img, 1), img, side_shift(img, -1)]
    for lane, k in enumerate(order):
        flat = forms[k].reshape(nrows, chans).astype(BF16)
        buf[pl.ds(row, nrows), lane * chans : (lane + 1) * chans] = flat


def put_phases(ref, i, v):
    for k in range(4):
        ref[k // 2, k % 2, i] = v[k // 2, :, k % 2]


def get_phases(ref, i):
    rows = [jnp.stack([ref[r, 0, i], ref[r, 1, i]], axis=1) for r in range(2)]
    return jnp.stack(rows)


def zero_edges(buf, edge):
    total = buf.shape[0]
    buf[0:edge, :] = jnp.zeros((edge, buf.shape[1]), BF16)
    buf[total - edge : total, :] = jnp.zeros((edge, buf.shape[1]), BF16)


def k_mix(geo, io, me, nf, pre1, sa, sb, gs, w, pre2, wb, ws, stats, dev, center):
    chans = pre1.shape[-1]
    lives = [live_rows(me[1], chans), live_rows(me[2], chans)]
    mean, inv = merged(sa[...], sb[...], nf[1], nf[2])
    scale, shift = gs[0:1] * inv, gs[1:2]
    bufs = (wb, ws)
    for part, (side, _) in enumerate(geo.parts):
        zero_edges(bufs[part], side * VIEWS)

    def act(part, i, pix, npx, row, nrows, carry):
        a = gelu((pre1[pl.ds(pix, npx)] - mean) * scale + shift)
        own = (pre1[pl.ds(pix, npx), :, lanes] - center[:, lanes]) * lives[part][:, 0:128]
        dev[pl.ds(row, nrows), :] = as_rows(own).astype(BF16)
        side = geo.parts[part][0]
        at = pl.multiple_of(side * VIEWS + i * nrows, 16)
        store_shifted(bufs[part], at, nrows, side, a, (0, 1, 2))
        return carry

    lanes, _ = own_block(me)
    center[...] = mean
    geo.loop(act, [0, 0], io)
    io.send(wb, ws, dev)
    io.ready()

    sums = [jnp.zeros((VIEWS, chans), F32)] * 2
    for part, (side, start) in enumerate(geo.parts):
        for lo, hi in geo.bands[part]:
            acc = None
            for r in range(3):
                at = (lo + r) * side * VIEWS
                d = nt(bufs[part][at : at + (hi - lo) * side * VIEWS, :], w[r])
                acc = d if acc is None else acc + d
            z = as_pix(acc)
            pre2[start + lo * side : start + hi * side] = z
            sums[part] = sums[part] + jnp.sum(z, axis=0)
    finish_stats(geo, pre2, sums, lives, nf[0], stats)


def k_expand(geo, io, me, nf, pre2, sa, sb, gs, w, pre3, act2, stats):
    chans = w.shape[1]
    lives = [live_rows(me[1], chans), live_rows(me[2], chans)]
    mean, inv = merged(sa[...], sb[...], nf[1], nf[2])
    scale, shift = gs[0:1] * inv, gs[1:2]

    def before(part, i, pix, npx, row, nrows):
        a = as_rows(gelu((pre2[pl.ds(pix, npx)] - mean) * scale + shift)).astype(BF16)
        act2[pl.ds(row, nrows), :] = a

    def product(part, pix, npx, row, nrows, carry):
        total = []
        for j in range(4):
            at = slice(256 * j, 256 * j + 256)
            z = as_pix(nn(act2[row : row + nrows, :], w[:, at]))
            pre3[pix : pix + npx, :, at] = z
            total.append(jnp.sum(z, axis=0))
        return carry + jnp.concatenate(total, axis=1)

    io.ready()
    zero = jnp.zeros((VIEWS, chans), F32)
    sums = geo.staged(io, before, product, [zero, zero])
    finish_stats(geo, pre3, sums, lives, nf[0], stats)


def k_narrow(geo, io, me, nf, pre3, xs, sa, sb, gs, w, pre4b, pre4s, mid, mids, stats, dev3, slope3, mid_even):
    chans = w.shape[1]
    lives = [live_rows(me[1], chans), live_rows(me[2], chans)]
    mean, inv = merged(sa[...], sb[...], nf[1], nf[2])
    scale, shift = gs[0:1] * inv, gs[1:2]
    pre4 = (pre4b, pre4s)

    def body(part, i, pix, npx, row, nrows, carry):
        side = geo.parts[part][0]
        half = side // 2
        for j in range(4):
            at = slice(256 * j, 256 * j + 256)
            dev = pre3[pl.ds(pix, npx), :, at] - mean[:, at]
            x = as_pix(xs[j, pl.ds(row, nrows), :].astype(F32))
            a, slope = gelu_both(dev * scale[:, at] + shift[:, at] + x)
            mid[pl.ds(row, nrows), at] = as_rows(a).astype(BF16)
            dev3[pl.ds(row, nrows), at] = as_rows(dev).astype(BF16)
            slope3[pl.ds(row, nrows), at] = as_rows(slope).astype(BF16)
            even = a.reshape(2, half, 2, VIEWS, 256)[0, :, 0]
            mid_even[pl.ds((0, geo.qb)[part] + half * i, half), :, at] = even
        z = nn(mid[pl.ds(row, nrows), :], w[...])
        put_phases(pre4[part], i, z.reshape(2, half, 2, VIEWS, chans))
        return carry + jnp.sum(as_pix(z), axis=0)

    io.ready()
    zero = jnp.zeros((VIEWS, chans), F32)
    sums = geo.loop(body, [zero, zero], io, io)
    mean4 = (rows_sum(sums[0] * lives[0]) + rows_sum(sums[1] * lives[1])) / nf[0]
    mids[...] = as_rows(mid_even[...]).astype(BF16)
    io.send(mids)
    sq = []
    for part in range(2):

        def dev2(i, carry, part=part):
            for k in range(4):
                d = pre4[part][k // 2, k % 2, i] - mean4
                carry = carry + jnp.sum(d * d, axis=0)
            return carry

        sq.append(lax.fori_loop(0, geo.parts[part][0] // 2, dev2, zero))
    stats[0:1] = mean4
    stats[1:2] = rows_sum(sq[0] * lives[0]) + rows_sum(sq[1] * lives[1])


def k_short(geo, io, me, nf, mids, w0, w1, side, stats):
    io.ready()
    chans = w0.shape[1]
    lives = [live_rows(me[1], chans), live_rows(me[2], chans)]
    for j, w in enumerate((w0, w1)):
        z = as_pix(nn(mids[...], w[...]))
        side[j] = z
        io.leave(j)
        mean, square = block_stats(geo, z, lives, nf[0])
        stats[j] = jnp.concatenate([mean, square], axis=0)


def k_stride(geo, io, me, nf, n4, pre4b, pre4s, sa, sb, gs, w, pre5, cols, stats, sb_act, ss_act):
    chans = pre4b.shape[-1]
    lives = [live_rows(me[1], chans), live_rows(me[2], chans)]
    mean, inv = merged(sa[...], sb[...], n4[1], n4[2])
    scale, shift = gs[0:1] * inv, gs[1:2]
    srcs, dsts = (pre4b, pre4s), (sb_act, ss_act)

    def act(part, i, pix, npx, row, nrows, carry):
        for k in range(4):
            at = (k // 2, k % 2, i)
            dsts[part][at] = gelu((srcs[part][at] - mean) * scale + shift)
        return carry

    geo.loop(act, [0, 0], io)
    for r in range(3):
        for c in range(3):
            flats = []
            for part in range(2):
                half = geo.parts[part][0] // 2
                v = dsts[part][(r + 1) % 2, (c + 1) % 2]
                if c == 0:
                    v = side_shift(v, 1)
                if r == 0:
                    v = jnp.concatenate([jnp.zeros((1,) + v.shape[1:], F32), v[:-1]], axis=0)
                flats.append(v.reshape(half * half * VIEWS, chans))
            t = 3 * r + c
            cols[t] = jnp.concatenate(flats, axis=0).astype(BF16)
            io.leave(t)
    io.ready()
    acc = None
    for t in range(9):
        d = nn(cols[t], w[t * chans : (t + 1) * chans, :])
        acc = d if acc is None else acc + d
    z = as_pix(acc)
    pre5[...] = z
    m5, s5 = block_stats(geo, z, lives, nf[0])
    stats[0:1] = m5
    stats[1:2] = s5


def k_widen(geo, io, me, nf, pre5, sa, sb, gs, w0, w1, st_side, pre6, act5, stats):
    chans = w0.shape[1]
    lives = [live_rows(me[1], chans), live_rows(me[2], chans)]
    mean, inv = merged(sa[...], sb[...], nf[1], nf[2])
    scale, shift = gs[0:1] * inv, gs[1:2]
    act5[...] = as_rows(gelu((pre5[...] - mean) * scale + shift)).astype(BF16)
    io.ready()
    for j, w in enumerate((w0, w1)):
        z = as_pix(nn(act5[...], w[...]))
        pre6[j] = z
        io.leave(j)
        m6, s6 = block_stats(geo, z, lives, nf[0])
        stats[j] = jnp.concatenate([m6, s6, st_side[j]], axis=0)


def k_total(geo, io, me, nf, pre6, side, sa, sb, gs, cb0, cb1, cs0, cs1, out_b, out_s, dt, sums):
    chans = pre6.shape[-1]
    lives = [live_rows(me[1], chans), live_rows(me[2], chans)]
    cots = ((cb0, cb1), (cs0, cs1))
    spans = ((0, geo.qb), (geo.qb, geo.px4))
    outs = (out_b, out_s)
    io.ready()
    for j in range(2):
        io.arrive(j)
        a, b, g = sa[j], sb[j], gs[j]
        m6, r6 = merged(a[0:2], b[0:2], nf[1], nf[2])
        ms, rs = merged(a[2:4], b[2:4], nf[1], nf[2])
        acc = [None, None, None]
        for part, (lo, hi) in enumerate(spans):
            d6 = pre6[j, lo:hi] - m6
            dd = side[j, lo:hi] - ms
            total = d6 * (g[0:1] * r6) + g[1:2] + (dd * (g[2:3] * rs) + g[3:4])
            live = lives[part]
            if j == 0:
                outs[part][...] = gelu(total) * live
            grad = gelu_slope(total) * (as_pix(cots[part][j][...].astype(F32)) * live)
            dt[j, lo:hi] = grad
            terms = [jnp.sum(v, axis=0) for v in (grad, grad * d6, grad * dd)]
            acc = [t if s is None else s + t for s, t in zip(acc, terms)]
        io.leave(j)
        if j == 0:
            io.send(out_b, out_s)
        sums[j] = jnp.concatenate(
            [rows_sum(acc[0]), rows_sum(acc[1]) * r6, rows_sum(acc[2]) * rs], axis=0
        )


def back_coefs(lives, s1, s2, inv, gain, count):
    c1 = gain * inv
    c2 = [live * (c1 * s1 / count) for live in lives]
    c3 = [live * (c1 * inv * s2 / count) for live in lives]
    return c1, c2, c3


def k_back_wide(geo, io, me, nf, dt, pre6, side, sa, sb, gs, ga, gb, w0, w1, part5, dz6, dzs, tot):
    chans = pre6.shape[-1]
    lives = [live_rows(me[1], chans), live_rows(me[2], chans)]
    total = nf[1] + nf[2]
    spans = ((0, geo.qb), (geo.qb, geo.px4))
    acc = None
    io.ready()
    for j, w in enumerate((w0, w1)):
        io.arrive(j)
        a, b, g = sa[j], sb[j], gs[j]
        s = ga[j] + gb[j]
        tot[j] = s
        m6, r6 = merged(a[0:2], b[0:2], nf[1], nf[2])
        ms, rs = merged(a[2:4], b[2:4], nf[1], nf[2])
        k1, k2, k3 = back_coefs(lives, s[0:1], s[1:2], r6, g[0:1], total)
        h1, h2, h3 = back_coefs(lives, s[0:1], s[2:3], rs, g[2:3], total)
        main, short = [], []
        for part, (lo, hi) in enumerate(spans):
            grad = dt[j, lo:hi]
            main.append(grad * k1 - k2[part] - (pre6[j, lo:hi] - m6) * k3[part])
            short.append(grad * h1 - h2[part] - (side[j, lo:hi] - ms) * h3[part])
        z6 = as_rows(jnp.concatenate(main, axis=0)).astype(BF16)
        dzs[j] = as_rows(jnp.concatenate(short, axis=0)).astype(BF16)
        io.leave(j)
        if j == 0:
            dz6[...] = z6
        d = nt(z6, w[...])
        acc = d if acc is None else acc + d
    part5[...] = as_pix(acc)


def k_back_act5(nf, mine, other, pre5, sa5, sb5, gs5, dt5, sums5):
    m5, r5 = merged(sa5[...], sb5[...], nf[1], nf[2])
    dev = pre5[...] - m5
    grad = gelu_slope(dev * (gs5[0:1] * r5) + gs5[1:2]) * (mine[...] + other[...])
    dt5[...] = grad
    sums5[0:1] = rows_sum(jnp.sum(grad, axis=0))
    sums5[1:2] = rows_sum(jnp.sum(grad * dev, axis=0)) * r5


def k_back_short(io, me, dzs, w0, w1, dms):
    io.ready()
    acc = None
    for j, w in enumerate((w0, w1)):
        d = nt(dzs[j], w[...])
        acc = d if acc is None else acc + d
    dms[...] = as_pix(acc).astype(BF16)


def k_back_stride(geo, io, me, nf, dt5, pre5, sa5, sb5, gs5, ga, gb, pre4b, pre4s, sa4, sb4, gs4, n4, w, dt4b, dt4s, dz5, sums4, tot, shifts):
    chans = pre5.shape[-1]
    lives = [live_rows(me[1], chans), live_rows(me[2], chans)]
    s = ga[...] + gb[...]
    tot[...] = s
    m5, r5 = merged(sa5[...], sb5[...], nf[1], nf[2])
    c1, c2, c3 = back_coefs(lives, s[0:1], s[1:2], r5, gs5[0:1], nf[1] + nf[2])
    spans = ((0, geo.qb), (geo.qb, geo.px4))
    imgs = []
    for part, (lo, hi) in enumerate(spans):
        half = geo.parts[part][0] // 2
        z = dt5[lo:hi] * c1 - c2[part] - (pre5[lo:hi] - m5) * c3[part]
        imgs.append(z.reshape(half, half, VIEWS, chans))

    def flat(moved):
        return jnp.concatenate([v.reshape(-1, chans) for v in moved], axis=0).astype(BF16)

    def up(v):
        return jnp.concatenate([v[1:], jnp.zeros((1,) + v.shape[1:], F32)], axis=0)

    shifts[0] = flat(imgs)
    dz5[...] = shifts[0]
    shifts[1] = flat([side_shift(v, -1) for v in imgs])
    shifts[2] = flat([up(v) for v in imgs])
    shifts[3] = flat([up(side_shift(v, -1)) for v in imgs])
    m4, r4 = merged(sa4[...], sb4[...], n4[1], n4[2])
    scale, off = gs4[0:1] * r4, gs4[1:2]
    io.ready()
    plan = {
        (0, 0): ((0, 4),),
        (0, 1): ((0, 5), (1, 3)),
        (1, 0): ((0, 7), (2, 1)),
        (1, 1): ((0, 8), (1, 6), (2, 2), (3, 0)),
    }
    t1, t2 = jnp.zeros((VIEWS, chans), F32), jnp.zeros((VIEWS, chans), F32)
    for (rp, cp), terms in plan.items():
        acc = None
        for k, t in terms:
            d = nt(shifts[k], w[t * chans : (t + 1) * chans, :])
            acc = d if acc is None else acc + d
        for part, (lo, hi) in enumerate(spans):
            half = geo.parts[part][0] // 2
            d = acc[lo * VIEWS : hi * VIEWS].reshape(half, half, VIEWS, chans)
            dev = (pre4b, pre4s)[part][rp, cp] - m4
            grad = gelu_slope(dev * scale + off) * d
            (dt4b, dt4s)[part][rp, cp] = grad
            t1 = t1 + jnp.sum(grad, axis=(0, 1))
            t2 = t2 + jnp.sum(grad * dev, axis=(0, 1))
    io.send(dt4b, dt4s)
    sums4[0:1] = rows_sum(t1)
    sums4[1:2] = rows_sum(t2) * r4


def k_back_narrow(geo, io, me, nf, dt4b, dt4s, pre4b, pre4s, sa4, sb4, gs4, ga, gb, dev3, slope3, sa3, sb3, dms, dmo, w, dt3, dz4, sums3, tot):
    chans = w.shape[1]
    wide = w.shape[0]
    lives = [live_rows(me[1], chans), live_rows(me[2], chans)]
    s = ga[...] + gb[...]
    tot[...] = s
    m4, r4 = merged(sa4[...], sb4[...], nf[1], nf[2])
    c1, c2, c3 = back_coefs(lives, s[0:1], s[1:2], r4, gs4[0:1], nf[1] + nf[2])
    _, r3 = merged(sa3[...], sb3[...], nf[1], nf[2])
    dts, pres = (dt4b, dt4s), (pre4b, pre4s)

    def body(part, i, pix, npx, row, nrows, carry):
        half = geo.parts[part][0] // 2
        dev4 = get_phases(pres[part], i) - m4
        z = get_phases(dts[part], i) * c1 - c2[part] - dev4 * c3[part]
        z = z.reshape(nrows, chans).astype(BF16)
        dz4[pl.ds(row, nrows), :] = z
        at = pl.ds((0, geo.qb)[part] + half * i, half)
        t1, t2 = [], []
        for j in range(4):
            at_j = slice(256 * j, 256 * j + 256)
            d = nt(z, w[at_j, :]).reshape(2, half, 2, VIEWS, 256)
            even = d[0, :, 0] + (dms[at, :, at_j].astype(F32) + dmo[at, :, at_j].astype(F32))
            top = jnp.stack([even, d[0, :, 1]], axis=1)
            d = jnp.concatenate([as_pix_rows(top), as_pix_rows(d[1])], axis=0)
            dev = as_pix(dev3[pl.ds(row, nrows), at_j].astype(F32))
            grad = as_pix(slope3[pl.ds(row, nrows), at_j].astype(F32)) * d
            dt3[pl.ds(row, nrows), at_j] = as_rows(grad).astype(BF16)
            t1.append(jnp.sum(grad, axis=0))
            t2.append(jnp.sum(grad * dev, axis=0))
        return carry[0] + jnp.concatenate(t1, axis=1), carry[1] + jnp.concatenate(t2, axis=1)

    io.ready()
    zero = jnp.zeros((VIEWS, wide), F32)
    (a1, a2), (b1, b2) = geo.loop(body, [(zero, zero), (zero, zero)], io, io)
    sums3[0:1] = rows_sum(a1 + b1)
    sums3[1:2] = rows_sum(a2 + b2) * r3


def k_back_expand(geo, io, me, nf, dt3, dev3, sa3, sb3, gs3, ga, gb, pre2, sa2, sb2, gs2, w, dt2, dz3, dt3q, sums2, tot, zbuf_b, zbuf_s):
    wide, chans = w.shape[1], w.shape[0]
    lives = [live_rows(me[1], wide), live_rows(me[2], wide)]
    s = ga[...] + gb[...]
    tot[...] = s
    _, r3 = merged(sa3[...], sb3[...], nf[1], nf[2])
    c1, c2, c3 = back_coefs(lives, s[0:1], s[1:2], r3, gs3[0:1], nf[1] + nf[2])
    m2, r2 = merged(sa2[...], sb2[...], nf[1], nf[2])
    scale, off = gs2[0:1] * r2, gs2[1:2]
    mine = pl.ds(pl.multiple_of(me[0] * 256, 256), 256)

    def body(part, i, pix, npx, row, nrows, carry):
        zbuf = (zbuf_b, zbuf_s)[part]
        dt3q[pl.ds(row, nrows), :] = dt3[pl.ds(row, nrows), mine]
        for j in range(4):
            at = slice(256 * j, 256 * j + 256)
            z = (
                as_pix(dt3[pl.ds(row, nrows), at].astype(F32)) * c1[:, at]
                - c2[part][:, at]
                - as_pix(dev3[pl.ds(row, nrows), at].astype(F32)) * c3[part][:, at]
            )
            zbuf[:, at] = as_rows(z).astype(BF16)
        dz3[pl.ds(row, nrows), :] = zbuf[:, mine]
        d = as_pix(nt(zbuf[...], w[...]))
        dev = pre2[pl.ds(pix, npx)] - m2
        grad = gelu_slope(dev * scale + off) * d
        dt2[pl.ds(pix, npx)] = grad
        return carry[0] + jnp.sum(grad, axis=0), carry[1] + jnp.sum(grad * dev, axis=0)

    io.ready()
    zero = jnp.zeros((VIEWS, chans), F32)
    (a1, a2), (b1, b2) = geo.loop(body, [(zero, zero), (zero, zero)], io, io)
    sums2[0:1] = rows_sum(a1 + b1)
    sums2[1:2] = rows_sum(a2 + b2) * r2


def k_back_mix(geo, io, me, nf, dt2, pre2, sa2, sb2, gs2, ga, gb, pre1, sa1, sb1, gs1, w, dt1, dz2, sums1, tot, dt1q, zb, zs):
    chans = pre2.shape[-1]
    lives = [live_rows(me[1], chans), live_rows(me[2], chans)]
    s = ga[...] + gb[...]
    tot[...] = s
    m2, r2 = merged(sa2[...], sb2[...], nf[1], nf[2])
    c1, c2, c3 = back_coefs(lives, s[0:1], s[1:2], r2, gs2[0:1], nf[1] + nf[2])
    m1, r1 = merged(sa1[...], sb1[...], nf[1], nf[2])
    scale, off = gs1[0:1] * r1, gs1[1:2]
    bufs = (zb, zs)
    for part, (side, _) in enumerate(geo.parts):
        zero_edges(bufs[part], side * VIEWS)

    def back(part, i, pix, npx, row, nrows, carry):
        z = dt2[pl.ds(pix, npx)] * c1 - c2[part] - (pre2[pl.ds(pix, npx)] - m2) * c3[part]
        dz2[pl.ds(row, nrows), :] = as_rows(z).astype(BF16)
        side = geo.parts[part][0]
        at = pl.multiple_of(side * VIEWS + i * nrows, 16)
        store_shifted(bufs[part], at, nrows, side, z, (2, 1, 0))
        return carry

    lanes, _ = own_block(me)
    geo.loop(back, [0, 0], io)
    io.send(dz2)
    io.ready()

    for part, (side, start) in enumerate(geo.parts):
        for lo, hi in geo.bands[part]:
            acc = None
            for r in range(3):
                at = (lo + 2 - r) * side * VIEWS
                taps = w[3 * r : 3 * r + 3].reshape(3 * chans, chans)
                d = nn(bufs[part][at : at + (hi - lo) * side * VIEWS, :], taps)
                acc = d if acc is None else acc + d
            dt1[start + lo * side : start + hi * side] = as_pix(acc)

    def finish(part, i, pix, npx, row, nrows, carry):
        dev = pre1[pl.ds(pix, npx)] - m1
        grad = gelu_slope(dev * scale + off) * dt1[pl.ds(pix, npx)]
        dt1[pl.ds(pix, npx)] = grad
        dt1q[pl.ds(row, nrows), :] = as_rows(dt1[pl.ds(pix, npx), :, lanes]).astype(BF16)
        return carry[0] + jnp.sum(grad, axis=0), carry[1] + jnp.sum(grad * dev, axis=0)

    zero = jnp.zeros((VIEWS, chans), F32)
    (a1, a2), (b1, b2) = geo.loop(finish, [(zero, zero), (zero, zero)], None, io)
    sums1[0:1] = rows_sum(a1 + b1)
    sums1[1:2] = rows_sum(a2 + b2) * r1


def k_back_reduce(geo, io, me, nf, dt1, pre1, sa1, sb1, gs1, ga, gb, dt3q, wt, gxb, gxs, tot, coef):
    chans = pre1.shape[-1]
    lives = [live_rows(me[1], chans), live_rows(me[2], chans)]
    s = ga[...] + gb[...]
    tot[...] = s
    m1, r1 = merged(sa1[...], sb1[...], nf[1], nf[2])
    c1, c2, c3 = back_coefs(lives, s[0:1], s[1:2], r1, gs1[0:1], nf[1] + nf[2])
    io.ready()
    total = nf[1] + nf[2]
    coef[0:1] = c1
    coef[1:2] = c1 * s[0:1] / total
    coef[2:3] = c1 * r1 * s[1:2] / total

    def body(part, i, pix, npx, row, nrows, carry):
        z = dt1[pl.ds(pix, npx)] * c1 - c2[part] - (pre1[pl.ds(pix, npx)] - m1) * c3[part]
        z = as_rows(z).astype(BF16)
        g = as_pix(nn(z, wt[me[0]])) + as_pix(dt3q[pl.ds(row, nrows), :].astype(F32))
        (gxb, gxs)[part][pl.ds(pix - (0, geo.pb)[part], npx)] = g
        return carry

    geo.loop(body, [0, 0], io, io)


def k_dw_wide(act5, dz6, mids, dzs, dwide, dshort):
    dwide[...] = tn(act5[...], dz6[...]).astype(BF16)
    dshort[...] = tn(mids[...], dzs[0]).astype(BF16)


def lane_blocks(v):
    return [v[:, 128 * b : 128 * b + 128] for b in range(v.shape[1] // 128)]


def put_halves(me, full, keep, send):
    bit = me[3] & 1
    keep[...] = full[bit].astype(BF16)
    send[...] = full[1 - bit].astype(BF16)


def k_dw_stride(io, me, cols, dz5, keep, send, full):
    mine = pl.ds(pl.multiple_of(me[0] * 128, 128), 128)
    z = dz5[:, mine]
    rows = full.shape[1]
    for t in range(9):
        io.arrive(t)
        dw = tn(cols[t], z)
        lo = 0
        while lo < 512:
            half, at = divmod(t * 512 + lo, rows)
            n = min(512 - lo, rows - at)
            full[half, at : at + n] = dw[lo : lo + n]
            lo += n
    put_halves(me, full, keep, send)


def k_dw_mid(me, mid, dz4, act2, dz3, keep, send, full):
    mine = pl.ds(pl.multiple_of(me[0] * 128, 128), 128)
    blocks = [tn(mid[...], dz4[:, mine])] + lane_blocks(tn(act2[...], dz3[...]))
    full[...] = jnp.concatenate(blocks, axis=0).reshape(full.shape)
    put_halves(me, full, keep, send)


def own_block(me):
    lanes = pl.ds(pl.multiple_of((me[0] >> 1) * 128, 128), 128)
    return lanes, pl.ds(pl.multiple_of((me[0] & 1) * 64, 64), 64)


def k_dev_products(geo, io, me, devq, xs, out, part):
    lives = [live_rows(me[1], 256), live_rows(me[2], 256)]
    _, mine = own_block(me)
    io.ready()

    def body(step, i, pix, npx, row, nrows, carry):
        return [
            carry[j] + jnp.sum(as_pix(xs[j, pl.ds(row, nrows), :].astype(F32)), axis=0) for j in range(4)
        ]

    zero = [jnp.zeros((VIEWS, 256), F32)] * 4
    big, small = geo.loop(body, [zero, zero], io)
    sums = [jnp.broadcast_to(rows_sum(b * lives[0] + s * lives[1]), (8, 256)) for b, s in zip(big, small)]
    for j in range(4):
        part[...] = tn(devq[...], xs[j])
        out[:, 256 * j : 256 * j + 256] = jnp.concatenate([part[mine, :], sums[j]], axis=0).astype(BF16)


def k_dw_last(geo, io, me, wb, ws, dz2, xs, dt1q, keep, send, full, part, flat):
    lanes, mine = own_block(me)
    io.ready()
    io.start_steps()
    nb, ns = geo.pb * VIEWS, geo.ps * VIEWS
    at = 0
    for r in range(3):
        ob, os = r * geo.hb * VIEWS, r * geo.hs * VIEWS
        full[...] = tn(dz2[0:nb, lanes], wb[ob : ob + nb, :]) + tn(
            dz2[nb : nb + ns, lanes], ws[os : os + ns, :]
        )
        for block in lane_blocks(full[mine, :]):
            flat[at : at + 64] = block
            at += 64
    geo.loop(lambda step, i, pix, npx, row, nrows, carry: carry, [0, 0], io)
    for j in range(4):
        part[:, 256 * j : 256 * j + 256] = tn(dt1q[...], xs[j])
    flat[at:] = jnp.concatenate(lane_blocks(part[mine, :]), axis=0)
    half = keep.shape[0]
    bit = me[3] & 1
    keep[...] = flat[pl.ds(pl.multiple_of(bit * half, 8), half)].astype(BF16)
    send[...] = flat[pl.ds(pl.multiple_of((1 - bit) * half, 8), half)].astype(BF16)


def k_out_first(io, me, wide, short, a, b, dwide, dshort, dstride):
    bit = me[3] & 1
    for n in range(4):
        io.arrive(n)
        if n < 2:
            dwide[n] = wide[n].astype(F32)
        dshort[n] = short[n].astype(F32)
        io.leave(n)
    io.ready()
    dstride[bit] = a[0].astype(F32)
    dstride[1 - bit] = b[0].astype(F32)
    io.send(dstride)


def k_small_outputs(me, t1, t2, t3, t4, t5, t6, late, gm3, sm3, go3, so3, gm4, sm4, go4, so4):
    lanes, _ = own_block(me)
    half = me[0] & 1
    for n, t in enumerate((t1, t2)):
        block = t[:, lanes]
        mine = jnp.where(half == 0, block[:, 0:64], block[:, 64:128])
        gm3[n : n + 1] = mine[1:2]
        sm3[n : n + 1] = mine[0:1]
    wide = pl.ds(pl.multiple_of(me[0] * 256, 256), 256)
    go3[...] = t3[1:2, wide]
    so3[...] = t3[0:1, wide]
    mid = pl.ds(pl.multiple_of(me[0] * 128, 128), 128)
    for n, t in enumerate((t4, t5)):
        gm4[n : n + 1] = t[1:2, mid]
        sm4[n : n + 1] = t[0:1, mid]
    go4[...] = t6[1:3]
    so4[0:1] = t6[0:1]
    so4[1:2] = t6[0:1]


def k_sum_split(shift, size, n_in, me, *refs):
    total = refs[n_in]
    acc = refs[0][...].astype(F32)
    for r in refs[1:n_in]:
        acc = acc + r[...].astype(F32)
    total[...] = acc
    where = (me[3] >> shift) & (size - 1)
    for m, out in enumerate(refs[n_in + 1 :]):
        out[...] = total[where ^ m].astype(BF16)


def k_sum(n_in, *refs):
    acc = refs[0][...].astype(F32)
    for r in refs[1:n_in]:
        acc = acc + r[...].astype(F32)
    refs[n_in][...] = acc.astype(BF16)


def k_join(shift, size, me, *refs):
    where = (me[3] >> shift) & (size - 1)
    for m in range(size):
        refs[size][where ^ m] = refs[m][...]


def k_unpack(plan, me, a, b, *refs):
    full = refs[-1]
    bit = me[3] & 1
    full[bit] = a[...].reshape(full.shape[1:]).astype(F32)
    full[1 - bit] = b[...].reshape(full.shape[1:]).astype(F32)
    flat = full[...].reshape(2 * full.shape[1], 128)
    at = 0
    for out, (lead, rows, cols) in zip(refs, plan):
        for t in range(lead):
            for block in range(cols // 128):
                v = flat[at : at + rows]
                lanes = slice(128 * block, 128 * block + 128)
                if lead > 1:
                    out[t, :, lanes] = v
                else:
                    out[:, lanes] = v
                at += rows


def k_out_last(me, a, b, dev, coef, dmix, dreduce, full):
    bit = me[3] & 1
    full[bit] = a[...].reshape(full.shape[1:]).astype(F32)
    full[1 - bit] = b[...].reshape(full.shape[1:]).astype(F32)
    flat = full[...].reshape(2 * full.shape[1], 128)
    at = 0
    for t in range(9):
        for block in range(2):
            dmix[t, :, 128 * block : 128 * block + 128] = flat[at : at + 64]
            at += 64
    fix = dev[64:65].astype(F32) * coef[1] + dev[0:64].astype(F32) * coef[2]
    for block in range(8):
        lanes = slice(128 * block, 128 * block + 128)
        dreduce[:, lanes] = flat[at : at + 64] * coef[0] - fix[:, lanes]
        at += 64


def per_device(
    ni,
    nc,
    x_big,
    x_small,
    cot_big,
    cot_small,
    counts,
    w_reduce,
    w_mix,
    w_expand,
    w_narrow,
    w_stride,
    w_widen,
    w_short,
    gain_mid3,
    shift_mid3,
    gain_out3,
    shift_out3,
    gain_mid4,
    shift_mid4,
    gain_out4,
    shift_out4,
):
    assert nc == 4 and ni >= 8 and x_big.shape[0] == VIEWS and x_small.shape[0] == VIEWS
    geo = Geo(x_big.shape[1], x_small.shape[1])
    img = lax.axis_index("img")
    q = lax.axis_index("ch").astype(jnp.int32)
    levels = ni.bit_length() - 1
    me, nf3, cnt3, nf4, cnt4 = call(
        "counts",
        functools.partial(k_counts, ni, ((geo.pb, geo.ps), (geo.qb, geo.qs))),
        [(counts, SMEM)],
        [(sds((4,), jnp.int32), SMEM)]
        + [(sds((n,)), SMEM) for n in (3, 8 * (levels - 2)) * 2],
        slack=1,
    )

    smem = [(me, SMEM)]

    def over_img(v, k):
        return lax.ppermute(v, "img", [(i, i ^ (1 << k)) for i in range(ni)])

    def over_ch(v, k):
        return lax.ppermute(v, "ch", [(i, i ^ k) for i in range(nc)])

    rounds, at = [], 0
    while at < levels:
        rounds.append((at, min(2, levels - at) if at == 0 else 1))
        at += rounds[-1][1]

    def peers(v, shift, bits):
        out = []
        for m in range(1, 1 << bits):
            out.append(lax.ppermute(v, "img", [(i, i ^ (m << shift)) for i in range(ni)]))
        return out

    def sync(v, combine, wait=(), free=()):
        wait, free = dict(wait), dict(free)
        freed = []
        for k, (shift, bits) in enumerate(rounds):
            if k in wait:
                v = lax.optimization_barrier((v,) + tuple(wait[k]))[0]
            others = peers(v, shift, bits)
            if k in free:
                held = lax.optimization_barrier(tuple(others) + tuple(free[k]))
                others = list(held[: len(others)])
                freed += held[len(others) :]
            if k == len(rounds) - 1:
                return (v, others[0]) + ((freed,) if free else ())
            v = combine(k, [v] + others)

    last = len(rounds) - 1

    def sync_stats(stats, cnt, wait=(), free=()):
        def combine(k, arrays):
            (v,) = call(
                "merge",
                functools.partial(k_merge, 8 * k, len(arrays)),
                [(cnt, SMEM)] + vm(*arrays),
                [sds(stats.shape)],
                slack=1,
            )
            return v

        return sync(stats, combine, wait, free)

    def sync_sums(sums, wait=(), free=()):
        def combine(k, arrays):
            (v,) = call("add", functools.partial(k_add, len(arrays)), vm(*arrays), [sds(sums.shape)], slack=1)
            return v

        return sync(sums, combine, wait, free)

    pairs = [(at, 1) for at in range(levels)]
    fours = [(0, 1)]
    while fours[-1][0] + fours[-1][1] < levels:
        done = fours[-1][0] + fours[-1][1]
        fours.append((done, min(2, levels - done)))

    def to_peers(parts, group):
        shift, bits = group
        out = []
        for m in range(1, 1 << bits):
            perm = [(i, i ^ (m << shift)) for i in range(ni)]
            out.append(lax.ppermute(parts[m if len(parts) > 1 else 0], "img", perm))
        return out

    def sum_split(name, arrays, group):
        shift, bits = group
        size = 1 << bits
        shape = arrays[0].shape
        view = (size, shape[0] // size) + shape[1:]
        return call(
            name,
            functools.partial(k_sum_split, shift, size, len(arrays)),
            smem + vm(*[a.reshape(view) for a in arrays]),
            [sds(view[1:], BF16)] * size,
            [pltpu.VMEM(view, F32)],
            order=True,
        )

    def join(name, parts, group):
        shift, bits = group
        size = 1 << bits
        (full,) = call(
            name,
            functools.partial(k_join, shift, size),
            smem + vm(*parts),
            [sds((size,) + parts[0].shape, BF16)],
        )
        return full.reshape((-1,) + parts[0].shape[1:])

    class Train:
        def __init__(self, name, groups, parts):
            self.name, self.groups, self.parts, self.at, self.summing = name, groups, parts, 0, True

        def sends(self):
            return self.parts[1:] if self.summing else self.parts

        def launch(self, sends):
            parts = self.parts[:1] + list(sends) if self.summing else list(sends)
            self.received = to_peers(parts, self.groups[self.at])

        def advance(self):
            name = "%s_%d" % (self.name, self.at)
            arrays = self.parts[:1] + self.received
            if self.summing and self.at + 1 < len(self.groups):
                self.at += 1
                self.parts = sum_split(name, arrays, self.groups[self.at])
            elif self.summing:
                self.summing = False
                self.parts = call(
                    name + "s",
                    functools.partial(k_sum, len(arrays)),
                    vm(*arrays),
                    [sds(arrays[0].shape, BF16)],
                    slack=2,
                )
            else:
                self.parts = [join(name + "j", arrays, self.groups[self.at])]
                self.at -= 1

        def to_last(self):
            while self.summing or self.at > 0:
                self.advance()
                self.launch(self.sends())

        def finish(self):
            self.to_last()
            return self.parts[0], self.received[0]

    def quarters(v):
        p1 = over_ch(v, 1)
        p2 = over_ch(v, 2)
        return [v, p1, p2, over_ch(p2, 1)]

    def after(marker, *arrays):
        return list(lax.optimization_barrier((marker,) + arrays))

    def sent(v):
        return [v, over_ch(v, 1), over_ch(v, 2)]

    def passed_on(g):
        return g + [over_ch(g[2], 1)]

    def rows_of(v):
        return jnp.transpose(v, (1, 2, 0, 3)).reshape(-1, v.shape[3])

    m3, c3 = 4 * w_reduce.shape[1], w_reduce.shape[0]
    m4, c4q = w_widen.shape
    first = [rows_of(x_small)]
    first.append(jnp.transpose(w_mix, (0, 1, 3, 2)).reshape(-1, m3))
    first += [w_reduce.T[:, j * m3 : (j + 1) * m3] for j in range(c3 // m3)]
    mix_at, reduce_at = first[0].shape[0], first[0].shape[0] + first[1].shape[0]
    held = (gain_mid3, shift_mid3, gain_out3[None], shift_out3[None], gain_mid4, shift_mid4, gain_out4, shift_out4)
    first += call(
        "pack_params",
        k_pack_params,
        vm(*held),
        [sds((64, 256), BF16)],
        [pltpu.VMEM((32, 128), F32)],
        slack=2,
    )
    params_at = sum(v.shape[0] for v in first[:-1])
    xb = quarters(rows_of(x_big))
    xb[1], me, *first = lax.optimization_barrier((xb[1], me, *first))
    smem = [(me, SMEM)]
    xsm = sent(jnp.concatenate(first))
    xb[3], xsm[2] = after(xb[3], xsm[2])
    xsm = passed_on(xsm)
    gs1, gs2, gs3, gs4, gs5, gs6 = call(
        "unpack_params",
        functools.partial(k_unpack_params, params_at),
        smem + [(in_hbm(v), HBM) for v in xsm],
        [sds((2, n)) for n in (m3, m3, c3, m4, m4)] + [sds((2, 4, c4q))],
        [pltpu.VMEM((4, 64, 256), BF16), pltpu.SemaphoreType.DMA((4,))],
        slack=2,
    )

    def blocks128(v):
        return [v[:, 128 * b : 128 * b + 128] for b in range(v.shape[1] // 128)]

    w_mid = jnp.concatenate(blocks128(w_expand) + blocks128(w_narrow))
    last_in = jnp.concatenate([w_short, w_widen, rows_of(cot_big), rows_of(cot_small)])
    wst = w_stride.reshape(-1, w_stride.shape[3])
    xsm[3], w_mid, last_in, wst = after(xsm[3], w_mid, last_in, wst)
    chip_pairs = [[0, 2], [1, 3]]
    wst = lax.all_gather(wst, "ch", axis_index_groups=chip_pairs)
    last_in = lax.all_gather(last_in, "ch", axis_index_groups=chip_pairs)

    n3, n4 = [(nf3, SMEM)], [(nf4, SMEM)]

    def k(fn):
        return functools.partial(fn, geo)

    hb, hs = geo.hb, geo.hs
    sb4, ss4 = (2, 2, hb // 2, hb // 2, VIEWS, m4), (2, 2, hs // 2, hs // 2, VIEWS, m4)
    wb_shape, ws_shape = ((hb + 2) * hb * VIEWS, 3 * m3), ((hs + 2) * hs * VIEWS, 3 * m3)

    def flow(kind, *arrays):
        return [(a, Flow(kind)) for a in arrays]

    def out(kind, shape, dtype=F32):
        return (sds(shape, dtype), Flow(kind))

    x_all = [(xb + xsm, Flow("x"))]
    w_in, w_ahead, w_back = [
        [(xsm, Flow(kind, base))]
        for kind, base in (("w_in", reduce_at), ("w_ahead", mix_at), ("w_back", mix_at))
    ]
    run = functools.partial(call, geo=geo)
    px1, px3, px4 = (geo.px, VIEWS, m3), (geo.px, VIEWS, c3), (geo.px4, VIEWS, m4)

    pre1, st = run(
        "reduce",
        k(k_reduce),
        smem + n3 + x_all + w_in,
        [fast(px1), sds((2, m3))],
    )
    st, w_mid = after(st, w_mid)
    w_mid = sent(w_mid)
    a1, b1 = sync_stats(st, cnt3)
    pre2, winb, wins, st, devq, keep1 = run(
        "mix",
        k(k_mix),
        smem + n3 + vm(pre1, a1, b1, gs1) + w_ahead,
        [
            fast(px1),
            out("all", wb_shape, BF16),
            out("all", ws_shape, BF16),
            sds((2, m3)),
            out("all", (geo.rows, 128), BF16),
            (sds(px1), Keep(2)),
        ],
        [pltpu.VMEM((1, m3), F32)],
    )
    st, w_mid[2] = after(st, w_mid[2])
    w_mid = passed_on(w_mid)
    w_expand_all = [(w_mid, Flow("w", 0, (m3, c3)))]
    w_narrow_all = [(w_mid, Flow("w", m3 * (c3 // 4 // 128), (c3, m4)))]
    a2, b2 = sync_stats(st, cnt3)
    pre3, act2, st, keep2 = run(
        "expand",
        k(k_expand),
        smem + n3 + vm(pre2, a2, b2, gs2) + w_expand_all,
        [
            fast(px3),
            out("rows", (geo.rows, m3), BF16),
            sds((2, c3)),
            (sds(px1), Keep(2)),
        ],
    )
    a3, b3 = sync_stats(st, cnt3)
    pre4b, pre4s, mid, mids, st, dev3, slope3 = run(
        "narrow",
        k(k_narrow),
        smem + n3 + vm(pre3) + x_all + vm(a3, b3, gs3) + w_narrow_all,
        [
            out("big", sb4),
            out("small", ss4),
            out("rows", (geo.rows, c3), BF16),
            fast((geo.rows4, c3), BF16),
            sds((2, m4)),
            out("rows", (geo.rows, c3), BF16),
            out("rows", (geo.rows, c3), BF16),
        ],
        [pltpu.VMEM((geo.px4, VIEWS, c3), F32)],
        slack=6,
        staying=4 * math.prod(px3),
    )
    st, wst = after(st, wst)
    wst = [wst, over_ch(wst, 1)]
    a4, b4 = sync_stats(st, cnt3)
    w_stride_all = [(wst, Flow("w4", 0, (9 * m4, m4)))]
    pre5, cols, st = run(
        "stride",
        k(k_stride),
        smem
        + n4
        + n3
        + flow("big", pre4b)
        + flow("small", pre4s)
        + vm(a4, b4, gs4)
        + w_stride_all,
        [
            sds(px4),
            out("lead", (9, geo.rows4, m4), BF16),
            sds((2, m4)),
        ],
        [pltpu.VMEM(sb4, F32), pltpu.VMEM(ss4, F32)],
    )
    (dev,) = run(
        "dev_products",
        k(k_dev_products),
        smem + flow("all", devq) + x_all,
        [sds((m3 // 4 + 8, c3), BF16)],
        [pltpu.VMEM((128, c3 // 4), F32)],
        ahead=8,
    )
    a5, b5, (dev,) = sync_stats(st, cnt4, free={last: [dev]})
    a5, last_in, mids = after(a5, last_in, mids)
    at_w, at_b, at_s = c3, c3 + m4, c3 + m4 + geo.qb * VIEWS

    def from_chips(base, rows):
        return [(last_in, Flow("chip", base, (rows, c4q), j)) for j in range(2)]

    wsh, wwi = from_chips(0, c3), from_chips(at_w, m4)
    cots = from_chips(at_b, geo.qb * VIEWS) + from_chips(at_s, geo.qs * VIEWS)
    side, st_side = run(
        "short",
        k(k_short),
        smem + n4 + vm(mids) + wsh,
        [fast((2, geo.px4, VIEWS, c4q)), sds((2, 2, c4q))],
    )
    pre6, act5, st = run(
        "widen",
        k(k_widen),
        smem + n4 + vm(pre5, a5, b5, gs5) + wwi + vm(st_side),
        [
            fast((2, geo.px4, VIEWS, c4q)),
            sds((geo.rows4, m4), BF16),
            sds((2, 4, c4q)),
        ],
    )
    a6, b6 = sync_stats(st, cnt4)
    out_b, out_s, dt6, sums = run(
        "total",
        k(k_total),
        smem + n4 + vm(pre6, side, a6, b6, gs6) + cots,
        [
            out("all", (geo.qb, VIEWS, c4q)),
            out("all", (geo.qs, VIEWS, c4q)),
            fast((2, geo.px4, VIEWS, c4q)),
            sds((2, 3, c4q)),
        ],
    )
    ga6, gb6 = sync_sums(sums)
    part5, dz6, dzs, t6 = run(
        "back_wide",
        k(k_back_wide),
        smem
        + n4
        + vm(dt6, pre6, side, a6, b6, gs6, ga6, gb6)
        + wwi,
        [
            sds(px4),
            sds((geo.rows4, c4q), BF16),
            sds((2, geo.rows4, c4q), BF16),
            sds((2, 3, c4q)),
        ],
    )
    other5 = over_ch(part5, 1)
    dt5, sums = call(
        "back_act5",
        k_back_act5,
        n4 + vm(part5, other5, pre5, a5, b5, gs5),
        [sds(px4), sds((2, m4))],
    )
    (dms,) = run(
        "back_short", k_back_short, smem + vm(dzs) + wsh, [sds((geo.px4, VIEWS, c3), BF16)]
    )
    dmo = over_ch(dms, 1)
    dwide, dshort = call(
        "dw_wide",
        k_dw_wide,
        vm(act5, dz6, mids, dzs),
        [sds((m4, c4q), BF16), sds((c3, c4q), BF16)],
    )
    ga5, gb5, (dwide, dshort) = sync_sums(sums, free={0: [dwide, dshort]})
    dt4b, dt4s, dz5, sums, t5 = run(
        "back_stride",
        k(k_back_stride),
        smem
        + n4
        + vm(dt5, pre5, a5, b5, gs5, ga5, gb5)
        + flow("all", pre4b, pre4s)
        + vm(a4, b4, gs4)
        + n3
        + w_stride_all,
        [fast(sb4), fast(ss4), sds((geo.rows4, m4), BF16), sds((2, m4)), sds((2, m4))],
        [pltpu.VMEM((4, geo.rows4, m4), BF16)],
    )

    def halves(rows):
        return [sds((rows // 2, 128), BF16)] * 2, pltpu.VMEM((2, rows // 2, 128), F32)

    outs, full = halves(9 * m4)
    parts = run("dw_stride", k_dw_stride, smem + flow("lead", cols) + vm(dz5), outs, [full])
    stride_train = Train("stride", pairs, parts)
    ga4, gb4, sends = sync_sums(sums, free={0: stride_train.sends()})
    stride_train.launch(sends)
    dt3, dz4, sums, t4 = run(
        "back_narrow",
        k(k_back_narrow),
        smem
        + n3
        + vm(dt4b, dt4s)
        + flow("big", pre4b)
        + flow("small", pre4s)
        + vm(a4, b4, gs4, ga4, gb4)
        + flow("rows", dev3, slope3)
        + vm(a3, b3, dms, dmo)
        + w_narrow_all,
        [
            fast((geo.rows, c3), BF16),
            out("rows", (geo.rows, m4), BF16),
            sds((2, c3)),
            sds((2, m4)),
        ],
    )
    came = stride_train.received
    stride_train.advance()
    ga3, gb3, sends = sync_sums(sums, wait={0: came}, free={last: stride_train.sends()})
    stride_train.launch(sends)
    dt2, dz3, dt3q, sums, t3 = run(
        "back_expand",
        k(k_back_expand),
        smem
        + n3
        + vm(dt3)
        + flow("rows", dev3)
        + vm(a3, b3, gs3, ga3, gb3)
        + flow("px", keep2)
        + vm(a2, b2, gs2)
        + w_expand_all,
        [
            fast(px1),
            out("rows", (geo.rows, c3 // 4), BF16),
            out("rows", (geo.rows, c3 // 4), BF16),
            sds((2, m3)),
            sds((2, c3)),
        ],
        [
            pltpu.VMEM((2 * hb * VIEWS, c3), BF16),
            pltpu.VMEM((2 * hs * VIEWS, c3), BF16),
        ],
    )
    came = stride_train.received
    stride_train.advance()
    outs, full = halves(c3 + (c3 // 4 // 128) * m3)
    parts = call("dw_mid", k_dw_mid, smem + vm(mid, dz4, act2, dz3), outs, [full])
    mid_train = Train("mid", pairs, parts)
    ga2, gb2, (mid_send, *sends) = sync_sums(
        sums, wait={0: came}, free={0: mid_train.sends(), last: stride_train.sends()}
    )
    mid_train.launch([mid_send])
    stride_train.launch(sends)
    dt1, dz2, sums, t2, dt1q = run(
        "back_mix",
        k(k_back_mix),
        smem
        + n3
        + vm(dt2)
        + flow("px", keep2)
        + vm(a2, b2, gs2, ga2, gb2)
        + flow("px", keep1)
        + vm(a1, b1, gs1)
        + w_back,
        [
            out("px", px1),
            out("all", (geo.rows, m3), BF16),
            sds((2, m3)),
            sds((2, m3)),
            out("rows", (geo.rows, 128), BF16),
        ],
        [pltpu.VMEM(wb_shape, BF16), pltpu.VMEM(ws_shape, BF16)],
    )
    came = stride_train.received + mid_train.received
    stride_train.advance()
    mid_train.advance()
    mix_rows = 9 * m3 // 128 * (m3 // 4)
    rows_last = mix_rows + c3 // 128 * (m3 // 4)
    outs, _ = halves(rows_last)
    parts = run(
        "dw_last",
        k(k_dw_last),
        smem + flow("all", winb, wins, dz2) + x_all + flow("all", dt1q),
        outs,
        [
            pltpu.VMEM((128, 3 * m3), F32),
            pltpu.VMEM((128, c3), F32),
            pltpu.VMEM((rows_last, 128), F32),
        ],
        ahead=8,
        hold=True,
    )
    last_train = Train("last", fours, parts)
    dwide, dshort, dev = lax.psum((dwide, dshort, dev), "img")
    wide = [dwide, dshort, dev]
    ga1, gb1, (last_send, mid_send, *sends) = sync_sums(
        sums,
        wait={last: came + wide},
        free={last: last_train.sends() + mid_train.sends() + stride_train.sends()},
    )
    last_train.launch([last_send])
    mid_train.launch([mid_send])
    stride_train.launch(sends)
    dwide, dshort, dev = wide
    gxb, gxs, t1, coef = run(
        "back_reduce",
        k(k_back_reduce),
        smem
        + n3
        + flow("px", dt1, keep1)
        + vm(a1, b1, gs1, ga1, gb1)
        + flow("rows", dt3q)
        + w_in,
        [
            out("big_px", (geo.pb, VIEWS, c3 // 4)),
            out("small_px", (geo.ps, VIEWS, c3 // 4)),
            sds((2, m3)),
            sds((3, m3)),
        ],
    )
    def unpack(name, a, b, plan):
        shapes = [((lead,) if lead > 1 else ()) + (rows, cols) for lead, rows, cols in plan]
        return call(
            name,
            functools.partial(k_unpack, plan),
            smem + vm(a, b),
            [sds(shape) for shape in shapes],
            [pltpu.VMEM((2,) + a.shape, F32)],
        )

    trains = (last_train, mid_train, stride_train)
    gxb, dwide, dshort, dev, coef, *came = after(
        gxb, dwide, dshort, dev, coef, *[train.received[0] for train in trains]
    )
    for train, first in zip(trains, came):
        train.received[0] = first
    halves_in = [v.reshape(1, 9 * m4 // 2, 128) for v in stride_train.finish()]
    dwide, dshort, dstride = run(
        "out_first",
        k_out_first,
        smem
        + flow("lead", dwide.reshape(2, m4 // 2, c4q), dshort.reshape(4, c3 // 4, c4q))
        + flow("all", *halves_in),
        [
            out("lead", (2, m4 // 2, c4q)),
            out("lead", (4, c3 // 4, c4q)),
            out("all", (2, 9 * m4 // 2, 128)),
        ],
        ahead=4,
    )
    mid_train.to_last()
    last_train.to_last()
    dstride, mid_train.received[0], last_train.received[0] = after(
        dstride, mid_train.received[0], last_train.received[0]
    )
    dnarrow, dexpand = unpack(
        "out_mid", *mid_train.finish(), [(1, c3, m4 // 4), (1, m3, c3 // 4)]
    )
    coef = lax.dynamic_slice_in_dim(coef, q * (m3 // 4), m3 // 4, 1)[:, :, None]
    mine, other = last_train.finish()
    dmix, dreduce = call(
        "out_last",
        k_out_last,
        smem + vm(mine, other, dev, coef),
        [sds((9, m3 // 4, m3)), sds((m3 // 4, c3))],
        [pltpu.VMEM((2,) + mine.shape, F32)],
    )

    def views_first(v, side):
        return jnp.transpose(v.reshape(side, side, VIEWS, v.shape[2]), (2, 0, 1, 3))

    small = call(
        "small_outputs",
        k_small_outputs,
        smem + vm(t1, t2, t3, t4, t5, t6[0], gxs[0]),
        [sds((2, m3 // 4))] * 2
        + [sds((1, c3 // 4))] * 2
        + [sds((2, m4 // 4))] * 2
        + [sds((2, c4q))] * 2,
        slack=4,
    )
    small[2], small[3] = small[2][0], small[3][0]
    return (
        views_first(out_b, hb // 2),
        views_first(out_s, hs // 2),
        views_first(gxb, hb),
        views_first(gxs, hs),
        dreduce.T,
        jnp.transpose(dmix.reshape(3, 3, m3 // 4, m3), (0, 1, 3, 2)),
        dexpand,
        dnarrow,
        dstride.reshape(3, 3, m4, m4 // 4),
        dwide.reshape(m4, c4q),
        dshort.reshape(c3, c4q),
        *small,
    )


def solution(mesh):
    act = P("img", None, None, "ch")
    flat, taps, vec = P(None, "ch"), P(None, None, None, "ch"), P("ch")
    in_specs = (act,) * 4 + (P(), flat, taps, flat, flat, taps, flat, flat)
    in_specs += (flat, flat, vec, vec, flat, flat, flat, flat)
    out_specs = (act,) * 4 + (flat, taps, flat, flat, taps, flat, flat)
    out_specs += (flat, flat, vec, vec, flat, flat, flat, flat)
    return jax.shard_map(
        functools.partial(per_device, mesh.shape["img"], mesh.shape["ch"]),
        mesh=mesh,
        in_specs=in_specs,
        out_specs=out_specs,
        check_vma=False,
    )
```

profile of v0, /device:TPU:0, one launch (start us, length us, event | category | flops | bytes accessed | tf_op | source)
XLA Modules:
  0.0 385.2 jit_solution(17082929540539196754)
XLA Ops:
  7.8 2.6 collective-permute-start.1
  21.4 7.8 %collective-permute-done.1.refs_4_.refs_5_.refs_6_ = bf16[1568,256]{1,0:T(8,128)(2,1)S(1)} collective-permute-done((bf16[1568,256]{1,0:T(8,128)(2,1)}, bf16[1568,256]{1,0:T(8,128)(2,1)S(1)}, u32[]{:S(2)}, u32[]{:S(2)}) %collective-permute-start.1) | collective-permute-done | bytes 802848 | tf_op jit(solution)/shard_map/ppermute | solution.py:1340
  29.3 2.3 collective-permute-done.2.refs_5_.refs_6_.refs_7_
  31.6 16.0 %collective-permute-done.3.refs_8_.refs_12_.p2.refs_9_.refs_15_.refs_10_ = bf16[1696,256]{1,0:T(8,128)(2,1)S(1)} collective-permute-done((bf16[1696,256]{1,0:T(8,128)(2,1)S(1)}, bf16[1696,256]{1,0:T(8,128)(2,1)S(1)}, u32[]{:S(2)}, u32[]{:S(2)}) %collective-permute-start.3) | collective-permute-done | bytes 868384 | tf_op jit(solution)/shard_map/ppermute | solution.py:1340
  54.6 6.8 %reduce.1 = (f32[296,8,256]{2,1,0:T(8,128)S(1)}, f32[2,256]{1,0:T(2,128)S(1)}) custom-call(s32[4]{0:T(128)S(1)} %get-tuple-element.187.refs_0_.me, f32[3]{0:T(128)S(1)} %get-tuple-element.189.refs_1_.refs_2_.refs_14_, bf16[1568,256]{1,0:T(8,128)(2,1)} %bitcast.105, bf16[1568,256]{1,0:T(8,128)(2,1)} %copy-done.21, bf16[1568,256]{1,0:T(8,128)(2,1)} %copy-done.22, ...), custom_call_target="tpu_custom_call" | custom-call | tf_op jit(solution)/shard_map/reduce/pallas_call | solution.py:316
  68.3 2.5 collective-permute-done.8.refs_3_
  71.5 2.7 collective-permute-start.9
  76.0 6.4 %mix.1 = (f32[296,8,256]{2,1,0:T(8,128)S(1)}, bf16[1792,768]{1,0:T(8,128)(2,1)}, bf16[960,768]{1,0:T(8,128)(2,1)}, f32[2,256]{1,0:T(2,128)S(1)}, bf16[2368,128]{1,0:T(8,128)(2,1)}, /*index=5*/f32[296,8,256]{2,1,0:T(8,128)}) custom-call(s32[4]{0:T(128)S(1)} %get-tuple-element.187.refs_0_.me, f32[3]{0:T(128)S(1)} %get-tuple-element.189.refs_1_.refs_2_.refs_14_, ...), custom_call_target="tpu_custom_call" | custom-call | tf_op jit(solution)/shard_map/mix/pallas_call | solution.py:316
  87.0 2.5 collective-permute-done.13.refs_3_
  90.1 2.7 collective-permute-start.14
  95.4 6.7 %expand.1 = (f32[296,8,1024]{2,1,0:T(8,128)S(1)}, bf16[2368,256]{1,0:T(8,128)(2,1)}, f32[2,1024]{1,0:T(2,128)S(1)}, f32[296,8,256]{2,1,0:T(8,128)}) custom-call(s32[4]{0:T(128)S(1)} %get-tuple-element.187.refs_0_.me, f32[3]{0:T(128)S(1)} %get-tuple-element.189.refs_1_.refs_2_.refs_14_, f32[296,8,256]{2,1,0:T(8,128)S(1)} %get-tuple-element.207.refs_2_, ...), custom_call_target="tpu_custom_call" | custom-call | tf_op jit(solution)/shard_map/expand/pallas_call | solution.py:316
  108.9 2.6 collective-permute-start.20
  113.5 13.9 %narrow.1 = (f32[2,2,7,7,8,512]{5,4,3,2,1,0:T(8,128)}, f32[2,2,5,5,8,512]{5,4,3,2,1,0:T(8,128)}, bf16[2368,1024]{1,0:T(8,128)(2,1)}, bf16[592,1024]{1,0:T(8,128)...) custom-call(s32[4]{0:T(128)S(1)} %get-tuple-element.187.refs_0_.me, ...), custom_call_target="tpu_custom_call" | custom-call | tf_op jit(solution)/shard_map/narrow/pallas_call | solution.py:316
  132.1 2.5 collective-permute-done.23.refs_3_
  135.2 2.7 collective-permute-start.24
  141.2 9.1 %stride.1 = (f32[74,8,512]{2,1,0:T(8,128)S(1)}, bf16[9,592,512]{2,1,0:T(8,128)(2,1)}, f32[2,512]{1,0:T(2,128)S(1)}) custom-call(s32[4]{0:T(128)S(1)} %get-tuple-element.187.refs_0_.me, f32[3]{0:T(128)S(1)} %get-tuple-element.188.refs_1_.nf, f32[3]{0:T(128)S(1)} %get-tuple-element.189.refs_1_.refs_2_.refs_14_, ...), custom_call_target="tpu_custom_call" | custom-call | tf_op jit(solution)/shard_map/stride/pallas_call | solution.py:316
  157.1 2.6 collective-permute-start.29
  159.7 6.2 %dev_products.1 = bf16[72,1024]{1,0:T(8,128)(2,1)} custom-call(s32[4]{0:T(128)S(1)} %get-tuple-element.187.refs_0_.me, bf16[2368,128]{1,0:T(8,128)(2,1)} %get-tuple-element.229.refs_1_, bf16[1568,256]{1,0:T(8,128)(2,1)} %bitcast.107, bf16[1568,256]{1,0:T(8,128)(2,1)} %copy-done.21, bf16[1568,256]{1,0:T(8,128)(2,1)} %copy-done.22, ...), custom_call_target="tpu_custom_call" | custom-call | tf_op jit(solution)/shard_map/dev_products/pallas_call | solution.py:316
  165.9 3.8 short.1
  169.8 2.8 widen.1
  177.3 2.5 collective-permute-done.32.refs_3_
  180.8 4.4 %collective-permute-done.33.refs_5_.refs_6_ = f32[2,4,512]{2,1,0:T(4,128)S(1)} collective-permute-done((f32[2,4,512]{2,1,0:T(4,128)S(1)}, f32[2,4,512]{2,1,0:T(4,128)S(1)}, u32[]{:S(2)}, u32[]{:S(2)}) %collective-permute-start.33) | collective-permute-done | bytes 16416 | tf_op jit(solution)/shard_map/ppermute | solution.py:1350
  185.1 6.7 %total.1 = (f32[49,8,512]{2,1,0:T(8,128)}, f32[25,8,512]{2,1,0:T(8,128)}, f32[2,74,8,512]{3,2,1,0:T(8,128)S(1)}, f32[2,3,512]{2,1,0:T(4,128)S(1)}) custom-call(s32[4]{0:T(128)S(1)} %get-tuple-element.187.refs_0_.me, f32[3]{0:T(128)S(1)} %get-tuple-element.188.refs_1_.nf, f32[2,74,8,512]{3,2,1,0:T(8,128)S(1)} %get-tuple-element.235.refs_2_.refs_3_, ...), custom_call_target="tpu_custom_call" | custom-call | tf_op jit(solution)/shard_map/total/pallas_call | solution.py:316
  198.5 4.2 %collective-permute-done.37.refs_9_ = f32[2,3,512]{2,1,0:T(4,128)S(1)} collective-permute-done((f32[2,3,512]{2,1,0:T(4,128)S(1)}, f32[2,3,512]{2,1,0:T(4,128)S(1)}, u32[]{:S(2)}, u32[]{:S(2)}) %collective-permute-start.37) | collective-permute-done | bytes 12320 | tf_op jit(solution)/shard_map/ppermute | solution.py:1350
  202.7 3.0 back_wide.1
  205.8 2.9 collective-permute-done.38.other
  208.6 2.7 back_act5.1
  214.9 3.6 back_short.1.refs_15_
  218.6 2.4 dw_wide.1
  221.5 4.1 %collective-permute-done.42.refs_8_ = f32[2,512]{1,0:T(2,128)S(1)} collective-permute-done((f32[2,512]{1,0:T(2,128)S(1)}, f32[2,512]{1,0:T(2,128)S(1)}, u32[]{:S(2)}, u32[]{:S(2)}) %collective-permute-start.42) | collective-permute-done | bytes 4128 | tf_op jit(solution)/shard_map/ppermute | solution.py:1350
  226.9 10.2 %back_stride.1 = (f32[2,2,7,7,8,512]{5,4,3,2,1,0:T(8,128)S(1)}, f32[2,2,5,5,8,512]{5,4,3,2,1,0:T(8,128)S(1)}, bf16[592,512]{1,0:T(8,128)(2,1)S(1)}, f32[2,512]{1,0:T(2,128)S(1)}, f32[2,512]{1,0:T(2,128)S(1)}) custom-call(s32[4]{0:T(128)S(1)} %get-tuple-element.187.refs_0_.me, f32[3]{0:T(128)S(1)} %get-tuple-element.188.refs_1_.nf, ...), custom_call_target="tpu_custom_call" | custom-call | tf_op jit(solution)/shard_map/back_stride/pallas_call | solution.py:316
  240.6 5.9 %dw_stride.1 = (bf16[2304,128]{1,0:T(8,128)(2,1)S(1)}, bf16[2304,128]{1,0:T(8,128)(2,1)S(1)}) custom-call(s32[4]{0:T(128)S(1)} %get-tuple-element.187.refs_0_.me, bf16[9,592,512]{2,1,0:T(8,128)(2,1)} %get-tuple-element.257.refs_1_, bf16[592,512]{1,0:T(8,128)(2,1)S(1)} %get-tuple-element.258.refs_2_), custom_call_target="tpu_custom_call" | custom-call | tf_op jit(solution)/shard_map/dw_stride/pallas_call | solution.py:316
  248.2 4.1 %collective-permute-done.46.refs_10_ = f32[2,512]{1,0:T(2,128)S(1)} collective-permute-done((f32[2,512]{1,0:T(2,128)S(1)}, f32[2,512]{1,0:T(2,128)S(1)}, u32[]{:S(2)}, u32[]{:S(2)}) %collective-permute-start.46) | collective-permute-done | bytes 4128 | tf_op jit(solution)/shard_map/ppermute | solution.py:1350
  252.3 11.4 %back_narrow.1 = (bf16[2368,1024]{1,0:T(8,128)(2,1)S(1)}, bf16[2368,512]{1,0:T(8,128)(2,1)}, f32[2,1024]{1,0:T(2,128)S(1)}, f32[2,512]{1,0:T(2,128)S(1)}) custom-call(s32[4]{0:T(128)S(1)} %get-tuple-element.187.refs_0_.me, f32[3]{0:T(128)S(1)} %get-tuple-element.189.refs_1_.refs_2_.refs_14_, f32[2,2,7,7,8,512]{5,4,3,2,1,0:T(8,128)S(1)} %get-tuple-element.254.refs_2_, ...), custom_call_target="tpu_custom_call" | custom-call | tf_op jit(solution)/shard_map/back_narrow/pallas_call | solution.py:316
  272.0 3.1 collective-permute-done.52.refs_8_
  275.8 8.7 %back_expand.1 = (f32[296,8,256]{2,1,0:T(8,128)S(1)}, bf16[2368,256]{1,0:T(8,128)(2,1)}, bf16[2368,256]{1,0:T(8,128)(2,1)}, f32[2,256]{1,0:T(2,128)S(1)}, f32[2,1024]{1,0:T(2,128)S(1)}) custom-call(s32[4]{0:T(128)S(1)} %get-tuple-element.187.refs_0_.me, f32[3]{0:T(128)S(1)} %get-tuple-element.189.refs_1_.refs_2_.refs_14_, ...), custom_call_target="tpu_custom_call" | custom-call | tf_op jit(solution)/shard_map/back_expand/pallas_call | solution.py:316
  289.4 2.6 dw_mid.1
  295.5 2.4 collective-permute-done.57.refs_8_
  299.4 11.4 %back_mix.1 = (f32[296,8,256]{2,1,0:T(8,128)}, bf16[2368,256]{1,0:T(8,128)(2,1)}, f32[2,256]{1,0:T(2,128)S(1)}, f32[2,256]{1,0:T(2,128)S(1)}, bf16[2368,128]{1,0:T(8,128)(2,1)}) custom-call(s32[4]{0:T(128)S(1)} %get-tuple-element.187.refs_0_.me, f32[3]{0:T(128)S(1)} %get-tuple-element.189.refs_1_.refs_2_.refs_14_, ...), custom_call_target="tpu_custom_call" | custom-call | tf_op jit(solution)/shard_map/back_mix/pallas_call | solution.py:316
  317.2 2.8 all-reduce.3.cloned.1.call-done
  320.0 8.8 %dw_last.1 = (bf16[832,128]{1,0:T(8,128)(2,1)S(1)}, bf16[832,128]{1,0:T(8,128)(2,1)S(1)}) custom-call(s32[4]{0:T(128)S(1)} %get-tuple-element.187.refs_0_.me, bf16[1792,768]{1,0:T(8,128)(2,1)} %get-tuple-element.297.refs_1_, bf16[960,768]{1,0:T(8,128)(2,1)} %get-tuple-element.298.refs_2_, bf16[2368,256]{1,0:T(8,128)(2,1)} %get-tuple-element.299.refs_3_, ...), custom_call_target="tpu_custom_call" | custom-call | tf_op jit(solution)/shard_map/dw_last/pallas_call | solution.py:316
  331.0 2.9 collective-permute-start.66
  333.9 6.1 %back_reduce.1 = (f32[196,8,256]{2,1,0:T(8,128)}, f32[100,8,256]{2,1,0:T(8,128)}, f32[2,256]{1,0:T(2,128)S(1)}, f32[3,256]{1,0:T(4,128)S(1)}) custom-call(s32[4]{0:T(128)S(1)} %get-tuple-element.187.refs_0_.me, f32[3]{0:T(128)S(1)} %get-tuple-element.189.refs_1_.refs_2_.refs_14_, f32[296,8,256]{2,1,0:T(8,128)} %get-tuple-element.289.refs_2_, ...), custom_call_target="tpu_custom_call" | custom-call | tf_op jit(solution)/shard_map/back_reduce/pallas_call | solution.py:316
  348.5 2.8 collective-permute-done.75.refs_1_
  351.3 3.5 collective-permute-start.76
  356.2 2.4 collective-permute-start.71
  361.6 2.9 collective-permute-done.72.refs_3_
  370.8 4.4 %out_first.1 = (f32[2,256,512]{2,1,0:T(8,128)}, f32[4,256,512]{2,1,0:T(8,128)}, f32[2,2304,128]{2,1,0:T(8,128)}) custom-call(s32[4]{0:T(128)S(1)} %get-tuple-element.187.refs_0_.me, bf16[2,256,512]{2,1,0:T(8,128)(2,1)} %bitcast.115, bf16[4,256,512]{2,1,0:T(8,128)(2,1)} %bitcast.113, bf16[1,2304,128]{2,1,0:T(8,128)(2,1)} %bitcast.70, ...), custom_call_target="tpu_custom_call" | custom-call | tf_op jit(solution)/shard_map/out_first/pallas_call | solution.py:316
  (265 shorter events, 132.5 us)
Async XLA Ops:
  7.2 120.3 %all-gather.5.cloned.1.call-start = ((), (), s32[]{:S(2)}) async-start(), calls=%async_computation | async-start | bytes 3538944 | tf_op jit(solution)/shard_map/all_gather | solution.py:1524
  7.2 11.7 %collective-permute-start = (bf16[1568,256]{1,0:T(8,128)(2,1)}, bf16[1568,256]{1,0:T(8,128)(2,1)S(1)}, u32[]{:S(2)}, u32[]{:S(2)}) collective-permute-start(bf16[1568,256]{1,0:T(8,128)(2,1)} %bitcast.103), channel_id=1, source_target_pairs={{0,1},{1,0},{2,3},{3,2},{4,5},{5,4},{6,7},{7,6},{8,9},{9,8},{10,11... | collective-permute-start | bytes 2408456 | tf_op jit(solution)/shard_map/ppermute | solution.py:1340
  7.8 21.5 %collective-permute-start.1 = (bf16[1568,256]{1,0:T(8,128)(2,1)}, bf16[1568,256]{1,0:T(8,128)(2,1)S(1)}, u32[]{:S(2)}, u32[]{:S(2)}) collective-permute-start(bf16[1568,256]{1,0:T(8,128)(2,1)} %bitcast.104), channel_id=1, source_target_pairs={{0,2},{1,3},{2,0},{3,1},{4,6},{5,7},{6,4},{7,5},{8,10},{9,11},{10,... | collective-permute-start | bytes 2408456 | tf_op jit(solution)/shard_map/ppermute | solution.py:1340
  21.3 26.3 %collective-permute-start.3 = (bf16[1696,256]{1,0:T(8,128)(2,1)S(1)}, bf16[1696,256]{1,0:T(8,128)(2,1)S(1)}, u32[]{:S(2)}, u32[]{:S(2)}) collective-permute-start(bf16[1696,256]{1,0:T(8,128)(2,1)S(1)} %constant_dynamic-update-slice_fusion.refs_6_.refs_10_.p0.refs_7_.refs_13_.refs_8_), channel_id=1, source_target_pairs={{0,2},{1,3},{2,0},{3,1},{4,6},{5,7},{6,4},{7,5},{8,10},{9,11},{10,... | collective-permute-start | bytes 2605064 | tf_op jit(solution)/shard_map/ppermute | solution.py:1340
  50.3 115.6 %all-gather.7.cloned.1.call-start = ((), (), s32[]{:S(2)}) async-start(), calls=%async_computation.1 | async-start | bytes 6537216 | tf_op jit(solution)/shard_map/all_gather | solution.py:1525
  51.1 268.9 %all-reduce.3.cloned.1.call-start = ((), (), s32[]{:S(2)}) async-start(), calls=%async_computation.2 | async-start | bytes 3440640 | tf_op jit(solution)/shard_map/psum | solution.py:1824
  61.4 21.0 %collective-permute-start.10 = (bf16[1536,128]{1,0:T(8,128)(2,1)S(1)}, bf16[1536,128]{1,0:T(8,128)(2,1)S(1)}, u32[]{:S(2)}, u32[]{:S(2)}) collective-permute-start(bf16[1536,128]{1,0:T(8,128)(2,1)S(1)} %pad_maximum_fusion.1.refs_6_.refs_14_.refs_17_.refs_13_), channel_id=1, source_target_pairs={{0,2},{1,3},{2,0},{3,1},{4,6},{5,7},{6,4},{7,5},{8,10},{9,11},{10,... | collective-permute-start | bytes 1179656 | tf_op jit(solution)/shard_map/ppermute | solution.py:1340
  74.1 18.7 %collective-permute-start.15 = (bf16[1536,128]{1,0:T(8,128)(2,1)S(1)}, bf16[1536,128]{1,0:T(8,128)(2,1)S(1)}, u32[]{:S(2)}, u32[]{:S(2)}) collective-permute-start(bf16[1536,128]{1,0:T(8,128)(2,1)S(1)} %pad_maximum_fusion.1.refs_6_.refs_14_.refs_17_.refs_13_), channel_id=1, source_target_pairs={{0,1},{1,0},{2,3},{3,2},{4,5},{5,4},{6,7},{7,6},{8,9},{9,8},{10,11... | collective-permute-start | bytes 1179656 | tf_op jit(solution)/shard_map/ppermute | solution.py:1340
  82.4 12.3 %collective-permute-start.16 = (bf16[1536,128]{1,0:T(8,128)(2,1)S(1)}, bf16[1536,128]{1,0:T(8,128)(2,1)S(1)}, u32[]{:S(2)}, u32[]{:S(2)}) collective-permute-start(bf16[1536,128]{1,0:T(8,128)(2,1)S(1)} %collective-permute-done.10.refs_8_.refs_16_.refs_19_.refs_15_), channel_id=1, source_target_pairs={{0,1},{1,0},{2,3},{3,2},{4,5},{5,4},{6,7},{7,6},{8,9},{9,8},{10,11... | collective-permute-start | bytes 1179656 | tf_op jit(solution)/shard_map/ppermute | solution.py:1340
  108.9 4.6 %collective-permute-start.20 = (f32[2,1024]{1,0:T(2,128)S(1)}, f32[2,1024]{1,0:T(2,128)S(1)}, u32[]{:S(2)}, u32[]{:S(2)}) collective-permute-start(f32[2,1024]{1,0:T(2,128)S(1)} %merge.8.refs_11_.refs_13_.refs_4_), channel_id=1, source_target_pairs={{0,16},{4,20},{8,24},{12,28},{16,0},{20,4},{24,8},{28,12},{1,17},{... | collective-permute-start | bytes 24584 | tf_op jit(solution)/shard_map/ppermute | solution.py:1350
  127.5 12.3 %collective-permute-start.25 = (bf16[2,4608,128]{2,1,0:T(8,128)(2,1)}, bf16[2,4608,128]{2,1,0:T(8,128)(2,1)S(1)}, u32[]{:S(2)}, u32[]{:S(2)}) collective-permute-start(bf16[2,4608,128]{2,1,0:T(8,128)(2,1)} %bitcast.109), channel_id=1, source_target_pairs={{0,1},{1,0},{2,3},{3,2},{4,5},{5,4},{6,7},{7,6},{8,9},{9,8},{10,11... | collective-permute-start | bytes 7077896 | tf_op jit(solution)/shard_map/ppermute | solution.py:1340
  157.1 12.6 %collective-permute-start.29 = (f32[2,512]{1,0:T(2,128)S(1)}, f32[2,512]{1,0:T(2,128)S(1)}, u32[]{:S(2)}, u32[]{:S(2)}) collective-permute-start(f32[2,512]{1,0:T(2,128)S(1)} %merge.10.refs_3_.sa5.refs_4_), channel_id=1, source_target_pairs={{0,16},{4,20},{8,24},{12,28},{16,0},{20,4},{24,8},{28,12},{1,17},{... | collective-permute-start | bytes 12296 | tf_op jit(solution)/shard_map/ppermute | solution.py:1350
  175.2 4.6 %collective-permute-start.32 = (f32[2,4,512]{2,1,0:T(4,128)S(1)}, f32[2,4,512]{2,1,0:T(4,128)S(1)}, u32[]{:S(2)}, u32[]{:S(2)}) collective-permute-start(f32[2,4,512]{2,1,0:T(4,128)S(1)} %get-tuple-element.237.refs_0_), channel_id=1, source_target_pairs={{0,12},{4,8},{8,4},{12,0},{16,28},{20,24},{24,20},{28,16},{1,13},{... | collective-permute-start | bytes 49160 | tf_op jit(solution)/shard_map/ppermute | solution.py:1350
  180.4 4.7 %collective-permute-start.33 = (f32[2,4,512]{2,1,0:T(4,128)S(1)}, f32[2,4,512]{2,1,0:T(4,128)S(1)}, u32[]{:S(2)}, u32[]{:S(2)}) collective-permute-start(f32[2,4,512]{2,1,0:T(4,128)S(1)} %merge.11.refs_4_.refs_5_), channel_id=1, source_target_pairs={{0,16},{4,20},{8,24},{12,28},{16,0},{20,4},{24,8},{28,12},{1,17},{... | collective-permute-start | bytes 49160 | tf_op jit(solution)/shard_map/ppermute | solution.py:1350
  193.4 4.6 %collective-permute-start.36 = (f32[2,3,512]{2,1,0:T(4,128)S(1)}, f32[2,3,512]{2,1,0:T(4,128)S(1)}, u32[]{:S(2)}, u32[]{:S(2)}) collective-permute-start(f32[2,3,512]{2,1,0:T(4,128)S(1)} %get-tuple-element.242.refs_0_), channel_id=1, source_target_pairs={{0,12},{4,8},{8,4},{12,0},{16,28},{20,24},{24,20},{28,16},{1,13},{... | collective-permute-start | bytes 36872 | tf_op jit(solution)/shard_map/ppermute | solution.py:1350
  198.0 4.7 %collective-permute-start.37 = (f32[2,3,512]{2,1,0:T(4,128)S(1)}, f32[2,3,512]{2,1,0:T(4,128)S(1)}, u32[]{:S(2)}, u32[]{:S(2)}) collective-permute-start(f32[2,3,512]{2,1,0:T(4,128)S(1)} %add.17.refs_8_), channel_id=1, source_target_pairs={{0,16},{4,20},{8,24},{12,28},{16,0},{20,4},{24,8},{28,12},{1,17},{... | collective-permute-start | bytes 36872 | tf_op jit(solution)/shard_map/ppermute | solution.py:1350
  211.3 9.6 %collective-permute-start.39 = (f32[2,512]{1,0:T(2,128)S(1)}, f32[2,512]{1,0:T(2,128)S(1)}, u32[]{:S(2)}, u32[]{:S(2)}) collective-permute-start(f32[2,512]{1,0:T(2,128)S(1)} %get-tuple-element.245.refs_0_), channel_id=1, source_target_pairs={{0,4},{4,0},{8,12},{12,8},{16,20},{20,16},{24,28},{28,24},{1,5},{5... | collective-permute-start | bytes 12296 | tf_op jit(solution)/shard_map/ppermute | solution.py:1350
  212.3 8.6 %collective-permute-start.40 = (f32[2,512]{1,0:T(2,128)S(1)}, f32[2,512]{1,0:T(2,128)S(1)}, u32[]{:S(2)}, u32[]{:S(2)}) collective-permute-start(f32[2,512]{1,0:T(2,128)S(1)} %get-tuple-element.245.refs_0_), channel_id=1, source_target_pairs={{0,8},{4,12},{8,0},{12,4},{16,24},{20,28},{24,16},{28,20},{1,9},{5... | collective-permute-start | bytes 12296 | tf_op jit(solution)/shard_map/ppermute | solution.py:1350
  214.0 7.0 %collective-permute-start.41 = (f32[2,512]{1,0:T(2,128)S(1)}, f32[2,512]{1,0:T(2,128)S(1)}, u32[]{:S(2)}, u32[]{:S(2)}) collective-permute-start(f32[2,512]{1,0:T(2,128)S(1)} %get-tuple-element.245.refs_0_), channel_id=1, source_target_pairs={{0,12},{4,8},{8,4},{12,0},{16,28},{20,24},{24,20},{28,16},{1,13},{... | collective-permute-start | bytes 12296 | tf_op jit(solution)/shard_map/ppermute | solution.py:1350
  218.5 29.7 %collective-permute-start.47 = (bf16[74,8,1024]{2,1,0:T(8,128)(2,1)S(1)}, bf16[74,8,1024]{2,1,0:T(8,128)(2,1)}, u32[]{:S(2)}, u32[]{:S(2)}) collective-permute-start(bf16[74,8,1024]{2,1,0:T(8,128)(2,1)S(1)} %back_short.1.refs_15_), channel_id=1, source_target_pairs={{0,1},{1,0},{2,3},{3,2},{4,5},{5,4},{6,7},{7,6},{8,9},{9,8},{10,11... | collective-permute-start | bytes 3637256 | tf_op jit(solution)/shard_map/ppermute | solution.py:1340
  237.1 9.4 %collective-permute-start.43 = (f32[2,512]{1,0:T(2,128)S(1)}, f32[2,512]{1,0:T(2,128)S(1)}, u32[]{:S(2)}, u32[]{:S(2)}) collective-permute-start(f32[2,512]{1,0:T(2,128)S(1)} %get-tuple-element.256.refs_0_), channel_id=1, source_target_pairs={{0,4},{4,0},{8,12},{12,8},{16,20},{20,16},{24,28},{28,24},{1,5},{5... | collective-permute-start | bytes 12296 | tf_op jit(solution)/shard_map/ppermute | solution.py:1350
  238.3 8.2 %collective-permute-start.44 = (f32[2,512]{1,0:T(2,128)S(1)}, f32[2,512]{1,0:T(2,128)S(1)}, u32[]{:S(2)}, u32[]{:S(2)}) collective-permute-start(f32[2,512]{1,0:T(2,128)S(1)} %get-tuple-element.256.refs_0_), channel_id=1, source_target_pairs={{0,8},{4,12},{8,0},{12,4},{16,24},{20,28},{24,16},{28,20},{1,9},{5... | collective-permute-start | bytes 12296 | tf_op jit(solution)/shard_map/ppermute | solution.py:1350
  239.9 6.6 %collective-permute-start.45 = (f32[2,512]{1,0:T(2,128)S(1)}, f32[2,512]{1,0:T(2,128)S(1)}, u32[]{:S(2)}, u32[]{:S(2)}) collective-permute-start(f32[2,512]{1,0:T(2,128)S(1)} %get-tuple-element.256.refs_0_), channel_id=1, source_target_pairs={{0,12},{4,8},{8,4},{12,0},{16,28},{20,24},{24,20},{28,16},{1,13},{... | collective-permute-start | bytes 12296 | tf_op jit(solution)/shard_map/ppermute | solution.py:1350
  246.5 17.3 %collective-permute-start.48 = (bf16[2304,128]{1,0:T(8,128)(2,1)S(1)}, bf16[2304,128]{1,0:T(8,128)(2,1)S(1)}, u32[]{:S(2)}, u32[]{:S(2)}) collective-permute-start(bf16[2304,128]{1,0:T(8,128)(2,1)S(1)} %get-tuple-element.267), channel_id=1, source_target_pairs={{0,4},{4,0},{8,12},{12,8},{16,20},{20,16},{24,28},{28,24},{1,5},{5... | collective-permute-start | bytes 1769480 | tf_op jit(solution)/shard_map/ppermute | solution.py:1401
  270.4 4.7 %collective-permute-start.52 = (f32[2,1024]{1,0:T(2,128)S(1)}, f32[2,1024]{1,0:T(2,128)S(1)}, u32[]{:S(2)}, u32[]{:S(2)}) collective-permute-start(f32[2,1024]{1,0:T(2,128)S(1)} %add.20.refs_7_), channel_id=1, source_target_pairs={{0,16},{4,20},{8,24},{12,28},{16,0},{20,4},{24,8},{28,12},{1,17},{... | collective-permute-start | bytes 24584 | tf_op jit(solution)/shard_map/ppermute | solution.py:1350
  275.1 9.5 %collective-permute-start.53 = (bf16[1152,128]{1,0:T(8,128)(2,1)S(1)}, bf16[1152,128]{1,0:T(8,128)(2,1)S(1)}, u32[]{:S(2)}, u32[]{:S(2)}) collective-permute-start(bf16[1152,128]{1,0:T(8,128)(2,1)S(1)} %get-tuple-element.275), channel_id=1, source_target_pairs={{0,8},{4,12},{8,0},{12,4},{16,24},{20,28},{24,16},{28,20},{1,9},{5... | collective-permute-start | bytes 884744 | tf_op jit(solution)/shard_map/ppermute | solution.py:1401
  284.6 7.4 %collective-permute-start.54 = (f32[2,256]{1,0:T(2,128)S(1)}, f32[2,256]{1,0:T(2,128)S(1)}, u32[]{:S(2)}, u32[]{:S(2)}) collective-permute-start(f32[2,256]{1,0:T(2,128)S(1)} %get-tuple-element.276.refs_0_), channel_id=1, source_target_pairs={{0,4},{4,0},{8,12},{12,8},{16,20},{20,16},{24,28},{28,24},{1,5},{5... | collective-permute-start | bytes 6152 | tf_op jit(solution)/shard_map/ppermute | solution.py:1350
  285.9 6.1 %collective-permute-start.55 = (f32[2,256]{1,0:T(2,128)S(1)}, f32[2,256]{1,0:T(2,128)S(1)}, u32[]{:S(2)}, u32[]{:S(2)}) collective-permute-start(f32[2,256]{1,0:T(2,128)S(1)} %get-tuple-element.276.refs_0_), channel_id=1, source_target_pairs={{0,8},{4,12},{8,0},{12,4},{16,24},{20,28},{24,16},{28,20},{1,9},{5... | collective-permute-start | bytes 6152 | tf_op jit(solution)/shard_map/ppermute | solution.py:1350
  287.4 4.7 %collective-permute-start.56 = (f32[2,256]{1,0:T(2,128)S(1)}, f32[2,256]{1,0:T(2,128)S(1)}, u32[]{:S(2)}, u32[]{:S(2)}) collective-permute-start(f32[2,256]{1,0:T(2,128)S(1)} %get-tuple-element.276.refs_0_), channel_id=1, source_target_pairs={{0,12},{4,8},{8,4},{12,0},{16,28},{20,24},{24,20},{28,16},{1,13},{... | collective-permute-start | bytes 6152 | tf_op jit(solution)/shard_map/ppermute | solution.py:1350
  292.0 25.2 %collective-permute-start.62 = (bf16[768,128]{1,0:T(8,128)(2,1)S(1)}, bf16[768,128]{1,0:T(8,128)(2,1)S(1)}, u32[]{:S(2)}, u32[]{:S(2)}) collective-permute-start(bf16[768,128]{1,0:T(8,128)(2,1)S(1)} %get-tuple-element.292), channel_id=1, source_target_pairs={{0,4},{4,0},{8,12},{12,8},{16,20},{20,16},{24,28},{28,24},{1,5},{5... | collective-permute-start | bytes 589832 | tf_op jit(solution)/shard_map/ppermute | solution.py:1401
  298.0 19.3 %collective-permute-start.61 = (bf16[576,128]{1,0:T(8,128)(2,1)S(1)}, bf16[576,128]{1,0:T(8,128)(2,1)S(1)}, u32[]{:S(2)}, u32[]{:S(2)}) collective-permute-start(bf16[576,128]{1,0:T(8,128)(2,1)S(1)} %get-tuple-element.291), channel_id=1, source_target_pairs={{0,16},{4,20},{8,24},{12,28},{16,0},{20,4},{24,8},{28,12},{1,17},{... | collective-permute-start | bytes 442376 | tf_op jit(solution)/shard_map/ppermute | solution.py:1401
  320.0 9.5 %collective-permute-start.63 = (f32[2,256]{1,0:T(2,128)S(1)}, f32[2,256]{1,0:T(2,128)S(1)}, u32[]{:S(2)}, u32[]{:S(2)}) collective-permute-start(f32[2,256]{1,0:T(2,128)S(1)} %add.22.refs_7_), channel_id=1, source_target_pairs={{0,16},{4,20},{8,24},{12,28},{16,0},{20,4},{24,8},{28,12},{1,17},{... | collective-permute-start | bytes 6152 | tf_op jit(solution)/shard_map/ppermute | solution.py:1350
  329.5 11.1 %collective-permute-start.64 = (bf16[832,128]{1,0:T(8,128)(2,1)S(1)}, bf16[832,128]{1,0:T(8,128)(2,1)S(1)}, u32[]{:S(2)}, u32[]{:S(2)}) collective-permute-start(bf16[832,128]{1,0:T(8,128)(2,1)S(1)} %get-tuple-element.309), channel_id=1, source_target_pairs={{0,4},{4,0},{8,12},{12,8},{16,20},{20,16},{24,28},{28,24},{1,5},{5... | collective-permute-start | bytes 638984 | tf_op jit(solution)/shard_map/ppermute | solution.py:1401
  331.0 9.6 %collective-permute-start.66 = (bf16[576,128]{1,0:T(8,128)(2,1)S(1)}, bf16[576,128]{1,0:T(8,128)(2,1)S(1)}, u32[]{:S(2)}, u32[]{:S(2)}) collective-permute-start(bf16[576,128]{1,0:T(8,128)(2,1)S(1)} %stride_2s.1.refs_0_), channel_id=1, source_target_pairs={{0,16},{4,20},{8,24},{12,28},{16,0},{20,4},{24,8},{28,12},{1,17},{... | collective-permute-start | bytes 442376 | tf_op jit(solution)/shard_map/ppermute | solution.py:1401
  333.9 6.1 %collective-permute-start.65 = (bf16[384,128]{1,0:T(8,128)(2,1)S(1)}, bf16[384,128]{1,0:T(8,128)(2,1)S(1)}, u32[]{:S(2)}, u32[]{:S(2)}) collective-permute-start(bf16[384,128]{1,0:T(8,128)(2,1)S(1)} %get-tuple-element.310), channel_id=1, source_target_pairs={{0,8},{4,12},{8,0},{12,4},{16,24},{20,28},{24,16},{28,20},{1,9},{5... | collective-permute-start | bytes 294920 | tf_op jit(solution)/shard_map/ppermute | solution.py:1401
  341.2 13.6 %collective-permute-start.73 = (bf16[1152,128]{1,0:T(8,128)(2,1)S(1)}, bf16[1152,128]{1,0:T(8,128)(2,1)S(1)}, u32[]{:S(2)}, u32[]{:S(2)}) collective-permute-start(bf16[1152,128]{1,0:T(8,128)(2,1)S(1)} %bitcast.71), channel_id=1, source_target_pairs={{0,8},{4,12},{8,0},{12,4},{16,24},{20,28},{24,16},{28,20},{1,9},{5... | collective-permute-start | bytes 884744 | tf_op jit(solution)/shard_map/ppermute | solution.py:1401
  343.3 8.0 %collective-permute-start.75 = (bf16[192,128]{1,0:T(8,128)(2,1)S(1)}, bf16[192,128]{1,0:T(8,128)(2,1)S(1)}, u32[]{:S(2)}, u32[]{:S(2)}) collective-permute-start(bf16[192,128]{1,0:T(8,128)(2,1)S(1)} %get-tuple-element.327), channel_id=1, source_target_pairs={{0,16},{4,20},{8,24},{12,28},{16,0},{20,4},{24,8},{28,12},{1,17},{... | collective-permute-start | bytes 147464 | tf_op jit(solution)/shard_map/ppermute | solution.py:1401
  344.0 12.0 %collective-permute-start.67 = (bf16[208,128]{1,0:T(8,128)(2,1)S(1)}, bf16[208,128]{1,0:T(8,128)(2,1)S(1)}, u32[]{:S(2)}, u32[]{:S(2)}) collective-permute-start(bf16[208,128]{1,0:T(8,128)(2,1)S(1)} %get-tuple-element.317), channel_id=1, source_target_pairs={{0,8},{4,12},{8,0},{12,4},{16,24},{20,28},{24,16},{28,20},{1,9},{5... | collective-permute-start | bytes 159752 | tf_op jit(solution)/shard_map/ppermute | solution.py:1401
  346.0 10.1 %collective-permute-start.68 = (bf16[208,128]{1,0:T(8,128)(2,1)S(1)}, bf16[208,128]{1,0:T(8,128)(2,1)S(1)}, u32[]{:S(2)}, u32[]{:S(2)}) collective-permute-start(bf16[208,128]{1,0:T(8,128)(2,1)S(1)} %get-tuple-element.318), channel_id=1, source_target_pairs={{0,16},{4,20},{8,24},{12,28},{16,0},{20,4},{24,8},{28,12},{1,17},{... | collective-permute-start | bytes 159752 | tf_op jit(solution)/shard_map/ppermute | solution.py:1401
  347.6 8.5 %collective-permute-start.69 = (bf16[208,128]{1,0:T(8,128)(2,1)S(1)}, bf16[208,128]{1,0:T(8,128)(2,1)S(1)}, u32[]{:S(2)}, u32[]{:S(2)}) collective-permute-start(bf16[208,128]{1,0:T(8,128)(2,1)S(1)} %get-tuple-element.319), channel_id=1, source_target_pairs={{0,24},{4,28},{8,16},{12,20},{16,8},{20,12},{24,0},{28,4},{1,25},{... | collective-permute-start | bytes 159752 | tf_op jit(solution)/shard_map/ppermute | solution.py:1401
  351.3 9.3 %collective-permute-start.76 = (bf16[192,128]{1,0:T(8,128)(2,1)S(1)}, bf16[192,128]{1,0:T(8,128)(2,1)S(1)}, u32[]{:S(2)}, u32[]{:S(2)}) collective-permute-start(bf16[192,128]{1,0:T(8,128)(2,1)S(1)} %mid_2s.1.refs_0_), channel_id=1, source_target_pairs={{0,16},{4,20},{8,24},{12,28},{16,0},{20,4},{24,8},{28,12},{1,17},{... | collective-permute-start | bytes 147464 | tf_op jit(solution)/shard_map/ppermute | solution.py:1401
  355.4 14.6 %collective-permute-start.74 = (bf16[2304,128]{1,0:T(8,128)(2,1)S(1)}, bf16[2304,128]{1,0:T(8,128)(2,1)S(1)}, u32[]{:S(2)}, u32[]{:S(2)}) collective-permute-start(bf16[2304,128]{1,0:T(8,128)(2,1)S(1)} %bitcast.69), channel_id=1, source_target_pairs={{0,4},{4,0},{8,12},{12,8},{16,20},{20,16},{24,28},{28,24},{1,5},{5... | collective-permute-start | bytes 1769480 | tf_op jit(solution)/shard_map/ppermute | solution.py:1401
  356.1 5.5 %collective-permute-start.70 = (bf16[208,128]{1,0:T(8,128)(2,1)S(1)}, bf16[208,128]{1,0:T(8,128)(2,1)S(1)}, u32[]{:S(2)}, u32[]{:S(2)}) collective-permute-start(bf16[208,128]{1,0:T(8,128)(2,1)S(1)} %last_1s.1.refs_0_), channel_id=1, source_target_pairs={{0,8},{4,12},{8,0},{12,4},{16,24},{20,28},{24,16},{28,20},{1,9},{5... | collective-permute-start | bytes 159752 | tf_op jit(solution)/shard_map/ppermute | solution.py:1401
  356.2 5.4 %collective-permute-start.71 = (bf16[208,128]{1,0:T(8,128)(2,1)S(1)}, bf16[208,128]{1,0:T(8,128)(2,1)S(1)}, u32[]{:S(2)}, u32[]{:S(2)}) collective-permute-start(bf16[208,128]{1,0:T(8,128)(2,1)S(1)} %last_1s.1.refs_0_), channel_id=1, source_target_pairs={{0,16},{4,20},{8,24},{12,28},{16,0},{20,4},{24,8},{28,12},{1,17},{... | collective-permute-start | bytes 159752 | tf_op jit(solution)/shard_map/ppermute | solution.py:1401
  358.6 5.9 %collective-permute-start.72 = (bf16[208,128]{1,0:T(8,128)(2,1)S(1)}, bf16[208,128]{1,0:T(8,128)(2,1)S(1)}, u32[]{:S(2)}, u32[]{:S(2)}) collective-permute-start(bf16[208,128]{1,0:T(8,128)(2,1)S(1)} %last_1s.1.refs_0_), channel_id=1, source_target_pairs={{0,24},{4,28},{8,16},{12,20},{16,8},{20,12},{24,0},{28,4},{1,25},{... | collective-permute-start | bytes 159752 | tf_op jit(solution)/shard_map/ppermute | solution.py:1401
  361.1 5.0 %collective-permute-start.77 = (bf16[384,128]{1,0:T(8,128)(2,1)S(1)}, bf16[384,128]{1,0:T(8,128)(2,1)S(1)}, u32[]{:S(2)}, u32[]{:S(2)}) collective-permute-start(bf16[384,128]{1,0:T(8,128)(2,1)S(1)} %bitcast.79), channel_id=1, source_target_pairs={{0,8},{4,12},{8,0},{12,4},{16,24},{20,28},{24,16},{28,20},{1,9},{5... | collective-permute-start | bytes 294920 | tf_op jit(solution)/shard_map/ppermute | solution.py:1401
  365.1 10.2 %collective-permute-start.79 = (bf16[832,128]{1,0:T(8,128)(2,1)S(1)}, bf16[832,128]{1,0:T(8,128)(2,1)S(1)}, u32[]{:S(2)}, u32[]{:S(2)}) collective-permute-start(bf16[832,128]{1,0:T(8,128)(2,1)S(1)} %bitcast.73), channel_id=1, source_target_pairs={{0,4},{4,0},{8,12},{12,8},{16,20},{20,16},{24,28},{28,24},{1,5},{5... | collective-permute-start | bytes 638984 | tf_op jit(solution)/shard_map/ppermute | solution.py:1401
  366.6 8.6 %collective-permute-start.78 = (bf16[768,128]{1,0:T(8,128)(2,1)S(1)}, bf16[768,128]{1,0:T(8,128)(2,1)S(1)}, u32[]{:S(2)}, u32[]{:S(2)}) collective-permute-start(bf16[768,128]{1,0:T(8,128)(2,1)S(1)} %bitcast.75), channel_id=1, source_target_pairs={{0,4},{4,0},{8,12},{12,8},{16,20},{20,16},{24,28},{28,24},{1,5},{5... | collective-permute-start | bytes 589832 | tf_op jit(solution)/shard_map/ppermute | solution.py:1401
  (72 other events, 532.2 us)
Sparse Core Ops, SparseCore 0:
  50.5 46.0 all-gather.4
  98.1 58.6 all-gather.6
  221.1 98.8 all-reduce.2
where the time goes:
time: 389 us; the launch traced here: 385 us
  Pallas kernels  160 us (41%)
  waiting for transfers between devices  99 us (25%)
  starting transfers between devices  91.5 us (24%)
  local copies, waits for them, and re-layouts  18 us (5%)
  between operations  14.8 us (4%)
    pallas_call x53, Pallas kernels, call(): pl.pallas_call(body, out_shape=out_shapes, in_specs=specs, out_specs=out_...  160 us
    ppermute x48, starting transfers between devices, peers(): out.append(lax.ppermute(v, 'img', [(i, i ^ m << shift) for i in range(ni)]))  59.4 us
    ppermute x48, waiting for transfers between devices, peers(): out.append(lax.ppermute(v, 'img', [(i, i ^ m << shift) for i in range(ni)]))  57.3 us
    ppermute x12, waiting for transfers between devices, over_ch(): return lax.ppermute(v, 'ch', [(i, i ^ k) for i in range(nc)])  31.1 us
    ppermute x20, starting transfers between devices, to_peers(): out.append(lax.ppermute(parts[m if len(parts) > 1 else 0], 'img', perm))  26.1 us
    unnamed x81, local copies, waits for them, and re-layouts  15.1 us
  transfers between devices with their start and end apart: 83, of which 49 were waited for; matrix products, arithmetic and copies ran while one was open for 2% of the time, Pallas kernels for 37%

commit v1 on v0

--- a/solution.py
+++ b/solution.py
@@ -826,7 +826,7 @@
         stats[j] = jnp.concatenate([m6, s6, st_side[j]], axis=0)
 
 
-def k_total(geo, io, me, nf, pre6, side, sa, sb, gs, cb0, cb1, cs0, cs1, out_b, out_s, dt, sums):
+def k_total(geo, io, me, nf, pre6, side, sa, sb, gs, cb0, cb1, cs0, cs1, out_b, out_s, dt, sums, cot):
     chans = pre6.shape[-1]
     lives = [live_rows(me[1], chans), live_rows(me[2], chans)]
     cots = ((cb0, cb1), (cs0, cs1))
@@ -838,18 +838,26 @@
         a, b, g = sa[j], sb[j], gs[j]
         m6, r6 = merged(a[0:2], b[0:2], nf[1], nf[2])
         ms, rs = merged(a[2:4], b[2:4], nf[1], nf[2])
-        acc = [None, None, None]
+        k6, ks = g[0:1] * r6, g[2:3] * rs
+        off = g[1:2] + g[3:4]
+        acc = [jnp.zeros((VIEWS, chans), F32)] * 3
         for part, (lo, hi) in enumerate(spans):
-            d6 = pre6[j, lo:hi] - m6
-            dd = side[j, lo:hi] - ms
-            total = d6 * (g[0:1] * r6) + g[1:2] + (dd * (g[2:3] * rs) + g[3:4])
-            live = lives[part]
-            if j == 0:
-                outs[part][...] = gelu(total) * live
-            grad = gelu_slope(total) * (as_pix(cots[part][j][...].astype(F32)) * live)
-            dt[j, lo:hi] = grad
-            terms = [jnp.sum(v, axis=0) for v in (grad, grad * d6, grad * dd)]
-            acc = [t if s is None else s + t for s, t in zip(acc, terms)]
+            half = geo.parts[part][0] // 2
+            cot[lo:hi] = as_pix(cots[part][j][...].astype(F32))
+
+            def row(i, carry, part=part, lo=lo, half=half):
+                at = pl.ds(lo + i * half, half)
+                d6 = pre6[j, at] - m6
+                dd = side[j, at] - ms
+                value, slope = gelu_both(d6 * k6 + (dd * ks + off))
+                if j == 0:
+                    outs[part][pl.ds(i * half, half)] = value * lives[part]
+                grad = slope * (cot[at] * lives[part])
+                dt[j, at] = grad
+                terms = [jnp.sum(v, axis=0) for v in (grad, grad * d6, grad * dd)]
+                return [s + t for s, t in zip(carry, terms)]
+
+            acc = lax.fori_loop(0, half, row, acc)
         io.leave(j)
         if j == 0:
             io.send(out_b, out_s)
@@ -1502,7 +1510,13 @@
     xb[1], me, *first = lax.optimization_barrier((xb[1], me, *first))
     smem = [(me, SMEM)]
     xsm = sent(jnp.concatenate(first))
-    xb[3], xsm[2] = after(xb[3], xsm[2])
+    def blocks128(v):
+        return [v[:, 128 * b : 128 * b + 128] for b in range(v.shape[1] // 128)]
+
+    w_mid = jnp.concatenate(blocks128(w_expand) + blocks128(w_narrow))
+    last_in = jnp.concatenate([w_short, w_widen, rows_of(cot_big), rows_of(cot_small)])
+    wst = w_stride.reshape(-1, w_stride.shape[3])
+    xb[3], xsm[2], w_mid, last_in, wst = after(xb[3], xsm[2], w_mid, last_in, wst)
     xsm = passed_on(xsm)
     gs1, gs2, gs3, gs4, gs5, gs6 = call(
         "unpack_params",
@@ -1513,13 +1527,6 @@
         slack=2,
     )
 
-    def blocks128(v):
-        return [v[:, 128 * b : 128 * b + 128] for b in range(v.shape[1] // 128)]
-
-    w_mid = jnp.concatenate(blocks128(w_expand) + blocks128(w_narrow))
-    last_in = jnp.concatenate([w_short, w_widen, rows_of(cot_big), rows_of(cot_small)])
-    wst = w_stride.reshape(-1, w_stride.shape[3])
-    xsm[3], w_mid, last_in, wst = after(xsm[3], w_mid, last_in, wst)
     chip_pairs = [[0, 2], [1, 3]]
     wst = lax.all_gather(wst, "ch", axis_index_groups=chip_pairs)
     last_in = lax.all_gather(last_in, "ch", axis_index_groups=chip_pairs)
@@ -1669,6 +1676,7 @@
             fast((2, geo.px4, VIEWS, c4q)),
             sds((2, 3, c4q)),
         ],
+        [pltpu.VMEM((geo.px4, VIEWS, c4q), F32)],
     )
     ga6, gb6 = sync_sums(sums)
     part5, dz6, dzs, t6 = run(
@@ -1723,7 +1731,7 @@
     outs, full = halves(9 * m4)
     parts = run("dw_stride", k_dw_stride, smem + flow("lead", cols) + vm(dz5), outs, [full])
     stride_train = Train("stride", pairs, parts)
-    ga4, gb4, sends = sync_sums(sums, free={0: stride_train.sends()})
+    ga4, gb4, sends = sync_sums(sums, free={last: stride_train.sends()})
     stride_train.launch(sends)
     dt3, dz4, sums, t4 = run(
         "back_narrow",
@@ -1746,7 +1754,7 @@
     )
     came = stride_train.received
     stride_train.advance()
-    ga3, gb3, sends = sync_sums(sums, wait={0: came}, free={last: stride_train.sends()})
+    ga3, gb3, sends = sync_sums(sums, wait={last: came}, free={last: stride_train.sends()})
     stride_train.launch(sends)
     dt2, dz3, dt3q, sums, t3 = run(
         "back_expand",
@@ -1777,7 +1785,7 @@
     parts = call("dw_mid", k_dw_mid, smem + vm(mid, dz4, act2, dz3), outs, [full])
     mid_train = Train("mid", pairs, parts)
     ga2, gb2, (mid_send, *sends) = sync_sums(
-        sums, wait={0: came}, free={0: mid_train.sends(), last: stride_train.sends()}
+        sums, wait={last: came}, free={0: mid_train.sends(), last: stride_train.sends()}
     )
     mid_train.launch([mid_send])
     stride_train.launch(sends)
@@ -1825,7 +1833,7 @@
     wide = [dwide, dshort, dev]
     ga1, gb1, (last_send, mid_send, *sends) = sync_sums(
         sums,
-        wait={last: came + wide},
+        wait={last: came},
         free={last: last_train.sends() + mid_train.sends() + stride_train.sends()},
     )
     last_train.launch([last_send])

time: 389 us -> 382 us (0.982)
  waiting for transfers between devices: 99 us -> 88.6 us
  starting transfers between devices: 91.5 us -> 96 us
    ppermute x12, waiting for transfers between devices: 31.1 us -> 26.8 us  [over_ch(): return lax.ppermute(v, 'ch', [(i, i ^ k) for i in range(nc)])]
    unnamed x81 -> x77, local copies, waits for them, and re-layouts: 15.1 us -> 16.1 us
  transfers between devices with their start and end apart: 83 -> 83, of which waited for: 49 -> 49; matrix products, arithmetic and copies ran while one was open for 2% -> 2% of each run, Pallas kernels for 37% -> 38%
where the time goes in v1:
time: 382 us; the launch traced here: 378 us
  Pallas kernels  158 us (41%)
  starting transfers between devices  96 us (25%)
  waiting for transfers between devices  88.6 us (23%)
  local copies, waits for them, and re-layouts  18.8 us (5%)
  between operations  14.8 us (4%)
    pallas_call x53, Pallas kernels, call(): pl.pallas_call(body, out_shape=out_shapes, in_specs=specs, out_specs=out_...  158 us
    ppermute x48, starting transfers between devices, peers(): out.append(lax.ppermute(v, 'img', [(i, i ^ m << shift) for i in range(ni)]))  62.7 us
    ppermute x48, waiting for transfers between devices, peers(): out.append(lax.ppermute(v, 'img', [(i, i ^ m << shift) for i in range(ni)]))  54.4 us
    ppermute x12, waiting for transfers between devices, over_ch(): return lax.ppermute(v, 'ch', [(i, i ^ k) for i in range(nc)])  26.8 us
    ppermute x20, starting transfers between devices, to_peers(): out.append(lax.ppermute(parts[m if len(parts) > 1 else 0], 'img', perm))  26.7 us
    unnamed x77, local copies, waits for them, and re-layouts  16.1 us
  transfers between devices with their start and end apart: 83, of which 49 were waited for; matrix products, arithmetic and copies ran while one was open for 2% of the time, Pallas kernels for 38%

profile of v1, /device:TPU:0, one launch (start us, length us, event | category | flops | bytes accessed | tf_op | source)
XLA Modules:
  0.0 378.1 jit_solution(13975048775604339801)
XLA Ops:
  7.8 2.6 collective-permute-start.1
  21.4 8.0 %collective-permute-done.1.refs_4_.refs_5_.refs_6_ = bf16[1568,256]{1,0:T(8,128)(2,1)} collective-permute-done((bf16[1568,256]{1,0:T(8,128)(2,1)}, bf16[1568,256]{1,0:T(8,128)(2,1)}, u32[]{:S(2)}, u32[]{:S(2)}) %collective-permute-start.1) | collective-permute-done | bytes 802848 | tf_op jit(solution)/shard_map/ppermute | solution.py:1348
  32.0 15.6 %collective-permute-done.3.refs_8_.refs_12_.p2.refs_9_.refs_15_.refs_10_ = bf16[1696,256]{1,0:T(8,128)(2,1)S(1)} collective-permute-done((bf16[1696,256]{1,0:T(8,128)(2,1)S(1)}, bf16[1696,256]{1,0:T(8,128)(2,1)S(1)}, u32[]{:S(2)}, u32[]{:S(2)}) %collective-permute-start.3) | collective-permute-done | bytes 868384 | tf_op jit(solution)/shard_map/ppermute | solution.py:1348
  53.1 6.7 %reduce.1 = (f32[296,8,256]{2,1,0:T(8,128)S(1)}, f32[2,256]{1,0:T(2,128)S(1)}) custom-call(s32[4]{0:T(128)S(1)} %get-tuple-element.184.refs_0_.me, f32[3]{0:T(128)S(1)} %get-tuple-element.186.refs_1_.refs_2_.refs_14_, bf16[1568,256]{1,0:T(8,128)(2,1)} %bitcast.105, bf16[1568,256]{1,0:T(8,128)(2,1)} %copy-done.21, ...), custom_call_target="tpu_custom_call" | custom-call | tf_op jit(solution)/shard_map/reduce/pallas_call | solution.py:316
  66.7 2.5 collective-permute-done.8.refs_3_
  69.9 2.7 collective-permute-start.9
  74.4 6.4 %mix.1 = (f32[296,8,256]{2,1,0:T(8,128)S(1)}, bf16[1792,768]{1,0:T(8,128)(2,1)}, bf16[960,768]{1,0:T(8,128)(2,1)}, f32[2,256]{1,0:T(2,128)S(1)}, bf16[2368,128]{1,0:T(8,128)(2,1)}, /*index=5*/f32[296,8,256]{2,1,0:T(8,128)}) custom-call(s32[4]{0:T(128)S(1)} %get-tuple-element.184.refs_0_.me, f32[3]{0:T(128)S(1)} %get-tuple-element.186.refs_1_.refs_2_.refs_14_, ...), custom_call_target="tpu_custom_call" | custom-call | tf_op jit(solution)/shard_map/mix/pallas_call | solution.py:316
  85.3 2.5 collective-permute-done.13.refs_3_
  88.5 2.7 collective-permute-start.14
  93.7 6.6 %expand.1 = (f32[296,8,1024]{2,1,0:T(8,128)S(1)}, bf16[2368,256]{1,0:T(8,128)(2,1)}, f32[2,1024]{1,0:T(2,128)S(1)}, f32[296,8,256]{2,1,0:T(8,128)}) custom-call(s32[4]{0:T(128)S(1)} %get-tuple-element.184.refs_0_.me, f32[3]{0:T(128)S(1)} %get-tuple-element.186.refs_1_.refs_2_.refs_14_, f32[296,8,256]{2,1,0:T(8,128)S(1)} %get-tuple-element.203.refs_2_, ...), custom_call_target="tpu_custom_call" | custom-call | tf_op jit(solution)/shard_map/expand/pallas_call | solution.py:316
  104.6 2.1 collective-permute-done.19.refs_3_
  107.3 2.6 collective-permute-start.20
  112.0 13.9 %narrow.1 = (f32[2,2,7,7,8,512]{5,4,3,2,1,0:T(8,128)}, f32[2,2,5,5,8,512]{5,4,3,2,1,0:T(8,128)}, bf16[2368,1024]{1,0:T(8,128)(2,1)}, bf16[592,1024]{1,0:T(8,128)...) custom-call(s32[4]{0:T(128)S(1)} %get-tuple-element.184.refs_0_.me, ...), custom_call_target="tpu_custom_call" | custom-call | tf_op jit(solution)/shard_map/narrow/pallas_call | solution.py:316
  130.4 2.5 collective-permute-done.23.refs_3_
  133.5 2.7 collective-permute-start.24
  139.5 9.1 %stride.1 = (f32[74,8,512]{2,1,0:T(8,128)S(1)}, bf16[9,592,512]{2,1,0:T(8,128)(2,1)}, f32[2,512]{1,0:T(2,128)S(1)}) custom-call(s32[4]{0:T(128)S(1)} %get-tuple-element.184.refs_0_.me, f32[3]{0:T(128)S(1)} %get-tuple-element.185.refs_1_.nf, f32[3]{0:T(128)S(1)} %get-tuple-element.186.refs_1_.refs_2_.refs_14_, ...), custom_call_target="tpu_custom_call" | custom-call | tf_op jit(solution)/shard_map/stride/pallas_call | solution.py:316
  152.8 2.1 collective-permute-done.28.refs_3_
  155.5 2.6 collective-permute-start.29
  158.1 6.5 %dev_products.1 = bf16[72,1024]{1,0:T(8,128)(2,1)} custom-call(s32[4]{0:T(128)S(1)} %get-tuple-element.184.refs_0_.me, bf16[2368,128]{1,0:T(8,128)(2,1)} %get-tuple-element.225.refs_1_, bf16[1568,256]{1,0:T(8,128)(2,1)} %bitcast.107, bf16[1568,256]{1,0:T(8,128)(2,1)} %copy-done.21, bf16[1568,256]{1,0:T(8,128)(2,1)} %collective-permute-done.1.refs_4_.refs_5_.refs_6_, ...), custom_call_target="tpu_custom_call" | custom-call | tf_op jit(solution)/shard_map/dev_products/pallas_call | solution.py:316
  164.7 3.8 %short.1 = (f32[2,74,8,512]{3,2,1,0:T(8,128)S(1)}, f32[2,2,512]{2,1,0:T(2,128)S(1)}) custom-call(s32[4]{0:T(128)S(1)} %get-tuple-element.184.refs_0_.me, f32[3]{0:T(128)S(1)} %get-tuple-element.185.refs_1_.nf, bf16[592,1024]{1,0:T(8,128)(2,1)S(1)} %get-tuple-element.229.refs_2_.mids, bf16[2,2128,512]{2,1,0:T(8,128)(2,1)} %bitcast.91, ...), custom_call_target="tpu_custom_call" | custom-call | tf_op jit(solution)/shard_map/short/pallas_call | solution.py:316
  168.5 2.8 widen.1
  175.9 2.5 collective-permute-done.32.refs_3_
  179.4 4.4 %collective-permute-done.33.refs_5_.refs_6_ = f32[2,4,512]{2,1,0:T(4,128)S(1)} collective-permute-done((f32[2,4,512]{2,1,0:T(4,128)S(1)}, f32[2,4,512]{2,1,0:T(4,128)S(1)}, u32[]{:S(2)}, u32[]{:S(2)}) %collective-permute-start.33) | collective-permute-done | bytes 16416 | tf_op jit(solution)/shard_map/ppermute | solution.py:1358
  183.8 4.9 %total.1 = (f32[49,8,512]{2,1,0:T(8,128)}, f32[25,8,512]{2,1,0:T(8,128)}, f32[2,74,8,512]{3,2,1,0:T(8,128)S(1)}, f32[2,3,512]{2,1,0:T(4,128)S(1)}) custom-call(s32[4]{0:T(128)S(1)} %get-tuple-element.184.refs_0_.me, f32[3]{0:T(128)S(1)} %get-tuple-element.185.refs_1_.nf, f32[2,74,8,512]{3,2,1,0:T(8,128)S(1)} %get-tuple-element.231.refs_2_.refs_3_, ...), custom_call_target="tpu_custom_call" | custom-call | tf_op jit(solution)/shard_map/total/pallas_call | solution.py:316
  193.0 2.0 collective-permute-done.36.refs_3_
  195.4 4.3 %collective-permute-done.37.refs_9_ = f32[2,3,512]{2,1,0:T(4,128)S(1)} collective-permute-done((f32[2,3,512]{2,1,0:T(4,128)S(1)}, f32[2,3,512]{2,1,0:T(4,128)S(1)}, u32[]{:S(2)}, u32[]{:S(2)}) %collective-permute-start.37) | collective-permute-done | bytes 12320 | tf_op jit(solution)/shard_map/ppermute | solution.py:1358
  199.7 3.0 back_wide.1
  202.7 3.6 back_short.1.refs_15_
  206.9 2.5 back_act5.1
  213.9 2.4 dw_wide.1
  217.7 4.2 %collective-permute-done.42.refs_8_ = f32[2,512]{1,0:T(2,128)S(1)} collective-permute-done((f32[2,512]{1,0:T(2,128)S(1)}, f32[2,512]{1,0:T(2,128)S(1)}, u32[]{:S(2)}, u32[]{:S(2)}) %collective-permute-start.42) | collective-permute-done | bytes 4128 | tf_op jit(solution)/shard_map/ppermute | solution.py:1358
  223.3 10.2 %back_stride.1 = (f32[2,2,7,7,8,512]{5,4,3,2,1,0:T(8,128)S(1)}, f32[2,2,5,5,8,512]{5,4,3,2,1,0:T(8,128)S(1)}, bf16[592,512]{1,0:T(8,128)(2,1)S(1)}, f32[2,512]{1,0:T(2,128)S(1)}, f32[2,512]{1,0:T(2,128)S(1)}) custom-call(s32[4]{0:T(128)S(1)} %get-tuple-element.184.refs_0_.me, f32[3]{0:T(128)S(1)} %get-tuple-element.185.refs_1_.nf, ...), custom_call_target="tpu_custom_call" | custom-call | tf_op jit(solution)/shard_map/back_stride/pallas_call | solution.py:316
  240.4 6.0 %dw_stride.1 = (bf16[2304,128]{1,0:T(8,128)(2,1)S(1)}, bf16[2304,128]{1,0:T(8,128)(2,1)S(1)}) custom-call(s32[4]{0:T(128)S(1)} %get-tuple-element.184.refs_0_.me, bf16[9,592,512]{2,1,0:T(8,128)(2,1)} %get-tuple-element.253.refs_1_, bf16[592,512]{1,0:T(8,128)(2,1)S(1)} %get-tuple-element.254.refs_2_), custom_call_target="tpu_custom_call" | custom-call | tf_op jit(solution)/shard_map/dw_stride/pallas_call | solution.py:316
  247.1 11.0 %back_narrow.1 = (bf16[2368,1024]{1,0:T(8,128)(2,1)S(1)}, bf16[2368,512]{1,0:T(8,128)(2,1)}, f32[2,1024]{1,0:T(2,128)S(1)}, f32[2,512]{1,0:T(2,128)S(1)}) custom-call(s32[4]{0:T(128)S(1)} %get-tuple-element.184.refs_0_.me, f32[3]{0:T(128)S(1)} %get-tuple-element.186.refs_1_.refs_2_.refs_14_, f32[2,2,7,7,8,512]{5,4,3,2,1,0:T(8,128)S(1)} %get-tuple-element.250.refs_2_, ...), custom_call_target="tpu_custom_call" | custom-call | tf_op jit(solution)/shard_map/back_narrow/pallas_call | solution.py:316
  265.0 2.6 collective-permute-start.52
  271.1 8.7 %back_expand.1 = (f32[296,8,256]{2,1,0:T(8,128)S(1)}, bf16[2368,256]{1,0:T(8,128)(2,1)}, bf16[2368,256]{1,0:T(8,128)(2,1)}, f32[2,256]{1,0:T(2,128)S(1)}, f32[2,1024]{1,0:T(2,128)S(1)}) custom-call(s32[4]{0:T(128)S(1)} %get-tuple-element.184.refs_0_.me, f32[3]{0:T(128)S(1)} %get-tuple-element.186.refs_1_.refs_2_.refs_14_, ...), custom_call_target="tpu_custom_call" | custom-call | tf_op jit(solution)/shard_map/back_expand/pallas_call | solution.py:316
  284.6 2.6 dw_mid.1
  287.9 2.7 collective-permute-start.57
  292.5 2.7 collective-permute-start.61
  295.3 11.4 %back_mix.1 = (f32[296,8,256]{2,1,0:T(8,128)}, bf16[2368,256]{1,0:T(8,128)(2,1)}, f32[2,256]{1,0:T(2,128)S(1)}, f32[2,256]{1,0:T(2,128)S(1)}, bf16[2368,128]{1,0:T(8,128)(2,1)}) custom-call(s32[4]{0:T(128)S(1)} %get-tuple-element.184.refs_0_.me, f32[3]{0:T(128)S(1)} %get-tuple-element.186.refs_1_.refs_2_.refs_14_, ...), custom_call_target="tpu_custom_call" | custom-call | tf_op jit(solution)/shard_map/back_mix/pallas_call | solution.py:316
  314.1 8.8 %dw_last.1 = (bf16[832,128]{1,0:T(8,128)(2,1)S(1)}, bf16[832,128]{1,0:T(8,128)(2,1)S(1)}) custom-call(s32[4]{0:T(128)S(1)} %get-tuple-element.184.refs_0_.me, bf16[1792,768]{1,0:T(8,128)(2,1)} %get-tuple-element.288.refs_1_, bf16[960,768]{1,0:T(8,128)(2,1)} %get-tuple-element.289.refs_2_, bf16[2368,256]{1,0:T(8,128)(2,1)} %get-tuple-element.290.refs_3_, ...), custom_call_target="tpu_custom_call" | custom-call | tf_op jit(solution)/shard_map/dw_last/pallas_call | solution.py:316
  324.7 2.8 collective-permute-start.66
  327.8 5.9 %back_reduce.1 = (f32[196,8,256]{2,1,0:T(8,128)}, f32[100,8,256]{2,1,0:T(8,128)}, f32[2,256]{1,0:T(2,128)S(1)}, f32[3,256]{1,0:T(4,128)S(1)}) custom-call(s32[4]{0:T(128)S(1)} %get-tuple-element.184.refs_0_.me, f32[3]{0:T(128)S(1)} %get-tuple-element.186.refs_1_.refs_2_.refs_14_, f32[296,8,256]{2,1,0:T(8,128)} %get-tuple-element.283.refs_2_, ...), custom_call_target="tpu_custom_call" | custom-call | tf_op jit(solution)/shard_map/back_reduce/pallas_call | solution.py:316
  336.8 3.0 collective-permute-start.75
  342.5 2.4 collective-permute-start.69
  348.6 2.9 collective-permute-start.71
  353.7 3.8 %collective-permute-done.72.refs_3_ = bf16[208,128]{1,0:T(8,128)(2,1)S(1)} collective-permute-done((bf16[208,128]{1,0:T(8,128)(2,1)S(1)}, bf16[208,128]{1,0:T(8,128)(2,1)S(1)}, u32[]{:S(2)}, u32[]{:S(2)}) %collective-permute-start.72) | collective-permute-done | bytes 53280 | tf_op jit(solution)/shard_map/ppermute | solution.py:1409
  363.7 4.4 %out_first.1 = (f32[2,256,512]{2,1,0:T(8,128)}, f32[4,256,512]{2,1,0:T(8,128)}, f32[2,2304,128]{2,1,0:T(8,128)}) custom-call(s32[4]{0:T(128)S(1)} %get-tuple-element.184.refs_0_.me, bf16[2,256,512]{2,1,0:T(8,128)(2,1)} %bitcast.115, bf16[4,256,512]{2,1,0:T(8,128)(2,1)} %bitcast.113, bf16[1,2304,128]{2,1,0:T(8,128)(2,1)} %bitcast.70, ...), custom_call_target="tpu_custom_call" | custom-call | tf_op jit(solution)/shard_map/out_first/pallas_call | solution.py:316
  (261 shorter events, 130.3 us)
Async XLA Ops:
  7.2 118.8 %all-gather.5.cloned.1.call-start = ((), (), s32[]{:S(2)}) async-start(), calls=%async_computation | async-start | bytes 3538944 | tf_op jit(solution)/shard_map/all_gather | solution.py:1531
  7.2 11.7 %collective-permute-start = (bf16[1568,256]{1,0:T(8,128)(2,1)}, bf16[1568,256]{1,0:T(8,128)(2,1)S(1)}, u32[]{:S(2)}, u32[]{:S(2)}) collective-permute-start(bf16[1568,256]{1,0:T(8,128)(2,1)} %bitcast.103), channel_id=1, source_target_pairs={{0,1},{1,0},{2,3},{3,2},{4,5},{5,4},{6,7},{7,6},{8,9},{9,8},{10,11... | collective-permute-start | bytes 2408456 | tf_op jit(solution)/shard_map/ppermute | solution.py:1348
  7.8 21.6 %collective-permute-start.1 = (bf16[1568,256]{1,0:T(8,128)(2,1)}, bf16[1568,256]{1,0:T(8,128)(2,1)}, u32[]{:S(2)}, u32[]{:S(2)}) collective-permute-start(bf16[1568,256]{1,0:T(8,128)(2,1)} %bitcast.104), channel_id=1, source_target_pairs={{0,2},{1,3},{2,0},{3,1},{4,6},{5,7},{6,4},{7,5},{8,10},{9,11},{10,... | collective-permute-start | bytes 2408456 | tf_op jit(solution)/shard_map/ppermute | solution.py:1348
  21.3 26.3 %collective-permute-start.3 = (bf16[1696,256]{1,0:T(8,128)(2,1)S(1)}, bf16[1696,256]{1,0:T(8,128)(2,1)S(1)}, u32[]{:S(2)}, u32[]{:S(2)}) collective-permute-start(bf16[1696,256]{1,0:T(8,128)(2,1)S(1)} %constant_dynamic-update-slice_fusion.refs_6_.refs_10_.p0.refs_7_.refs_13_.refs_8_), channel_id=1, source_target_pairs={{0,2},{1,3},{2,0},{3,1},{4,6},{5,7},{6,4},{7,5},{8,10},{9,11},{10,... | collective-permute-start | bytes 2605064 | tf_op jit(solution)/shard_map/ppermute | solution.py:1348
  47.7 117.0 %all-gather.7.cloned.1.call-start = ((), (), s32[]{:S(2)}) async-start(), calls=%async_computation.1 | async-start | bytes 6537216 | tf_op jit(solution)/shard_map/all_gather | solution.py:1532
  48.4 287.2 %all-reduce.3.cloned.1.call-start = ((), (), s32[]{:S(2)}) async-start(), calls=%async_computation.2 | async-start | bytes 3440640 | tf_op jit(solution)/shard_map/psum | solution.py:1832
  59.8 21.0 %collective-permute-start.10 = (bf16[1536,128]{1,0:T(8,128)(2,1)S(1)}, bf16[1536,128]{1,0:T(8,128)(2,1)S(1)}, u32[]{:S(2)}, u32[]{:S(2)}) collective-permute-start(bf16[1536,128]{1,0:T(8,128)(2,1)S(1)} %pad_maximum_fusion.1.refs_6_.refs_14_.refs_17_.refs_13_), channel_id=1, source_target_pairs={{0,2},{1,3},{2,0},{3,1},{4,6},{5,7},{6,4},{7,5},{8,10},{9,11},{10,... | collective-permute-start | bytes 1179656 | tf_op jit(solution)/shard_map/ppermute | solution.py:1348
  72.6 18.6 %collective-permute-start.15 = (bf16[1536,128]{1,0:T(8,128)(2,1)S(1)}, bf16[1536,128]{1,0:T(8,128)(2,1)S(1)}, u32[]{:S(2)}, u32[]{:S(2)}) collective-permute-start(bf16[1536,128]{1,0:T(8,128)(2,1)S(1)} %pad_maximum_fusion.1.refs_6_.refs_14_.refs_17_.refs_13_), channel_id=1, source_target_pairs={{0,1},{1,0},{2,3},{3,2},{4,5},{5,4},{6,7},{7,6},{8,9},{9,8},{10,11... | collective-permute-start | bytes 1179656 | tf_op jit(solution)/shard_map/ppermute | solution.py:1348
  80.8 12.2 %collective-permute-start.16 = (bf16[1536,128]{1,0:T(8,128)(2,1)S(1)}, bf16[1536,128]{1,0:T(8,128)(2,1)S(1)}, u32[]{:S(2)}, u32[]{:S(2)}) collective-permute-start(bf16[1536,128]{1,0:T(8,128)(2,1)S(1)} %collective-permute-done.10.refs_8_.refs_16_.refs_19_.refs_15_), channel_id=1, source_target_pairs={{0,1},{1,0},{2,3},{3,2},{4,5},{5,4},{6,7},{7,6},{8,9},{9,8},{10,11... | collective-permute-start | bytes 1179656 | tf_op jit(solution)/shard_map/ppermute | solution.py:1348
  107.3 4.6 %collective-permute-start.20 = (f32[2,1024]{1,0:T(2,128)S(1)}, f32[2,1024]{1,0:T(2,128)S(1)}, u32[]{:S(2)}, u32[]{:S(2)}) collective-permute-start(f32[2,1024]{1,0:T(2,128)S(1)} %merge.8.refs_11_.refs_13_.refs_4_), channel_id=1, source_target_pairs={{0,16},{4,20},{8,24},{12,28},{16,0},{20,4},{24,8},{28,12},{1,17},{... | collective-permute-start | bytes 24584 | tf_op jit(solution)/shard_map/ppermute | solution.py:1358
  126.0 12.1 %collective-permute-start.25 = (bf16[2,4608,128]{2,1,0:T(8,128)(2,1)}, bf16[2,4608,128]{2,1,0:T(8,128)(2,1)S(1)}, u32[]{:S(2)}, u32[]{:S(2)}) collective-permute-start(bf16[2,4608,128]{2,1,0:T(8,128)(2,1)} %bitcast.109), channel_id=1, source_target_pairs={{0,1},{1,0},{2,3},{3,2},{4,5},{5,4},{6,7},{7,6},{8,9},{9,8},{10,11... | collective-permute-start | bytes 7077896 | tf_op jit(solution)/shard_map/ppermute | solution.py:1348
  155.5 13.0 %collective-permute-start.29 = (f32[2,512]{1,0:T(2,128)S(1)}, f32[2,512]{1,0:T(2,128)S(1)}, u32[]{:S(2)}, u32[]{:S(2)}) collective-permute-start(f32[2,512]{1,0:T(2,128)S(1)} %merge.10.refs_3_.sa5.refs_4_), channel_id=1, source_target_pairs={{0,16},{4,20},{8,24},{12,28},{16,0},{20,4},{24,8},{28,12},{1,17},{... | collective-permute-start | bytes 12296 | tf_op jit(solution)/shard_map/ppermute | solution.py:1358
  173.8 4.6 %collective-permute-start.32 = (f32[2,4,512]{2,1,0:T(4,128)S(1)}, f32[2,4,512]{2,1,0:T(4,128)S(1)}, u32[]{:S(2)}, u32[]{:S(2)}) collective-permute-start(f32[2,4,512]{2,1,0:T(4,128)S(1)} %get-tuple-element.233.refs_0_), channel_id=1, source_target_pairs={{0,12},{4,8},{8,4},{12,0},{16,28},{20,24},{24,20},{28,16},{1,13},{... | collective-permute-start | bytes 49160 | tf_op jit(solution)/shard_map/ppermute | solution.py:1358
  179.1 4.7 %collective-permute-start.33 = (f32[2,4,512]{2,1,0:T(4,128)S(1)}, f32[2,4,512]{2,1,0:T(4,128)S(1)}, u32[]{:S(2)}, u32[]{:S(2)}) collective-permute-start(f32[2,4,512]{2,1,0:T(4,128)S(1)} %merge.11.refs_4_.refs_5_), channel_id=1, source_target_pairs={{0,16},{4,20},{8,24},{12,28},{16,0},{20,4},{24,8},{28,12},{1,17},{... | collective-permute-start | bytes 49160 | tf_op jit(solution)/shard_map/ppermute | solution.py:1358
  190.4 4.6 %collective-permute-start.36 = (f32[2,3,512]{2,1,0:T(4,128)S(1)}, f32[2,3,512]{2,1,0:T(4,128)S(1)}, u32[]{:S(2)}, u32[]{:S(2)}) collective-permute-start(f32[2,3,512]{2,1,0:T(4,128)S(1)} %get-tuple-element.238.refs_0_), channel_id=1, source_target_pairs={{0,12},{4,8},{8,4},{12,0},{16,28},{20,24},{24,20},{28,16},{1,13},{... | collective-permute-start | bytes 36872 | tf_op jit(solution)/shard_map/ppermute | solution.py:1358
  195.0 4.7 %collective-permute-start.37 = (f32[2,3,512]{2,1,0:T(4,128)S(1)}, f32[2,3,512]{2,1,0:T(4,128)S(1)}, u32[]{:S(2)}, u32[]{:S(2)}) collective-permute-start(f32[2,3,512]{2,1,0:T(4,128)S(1)} %add.17.refs_8_), channel_id=1, source_target_pairs={{0,16},{4,20},{8,24},{12,28},{16,0},{20,4},{24,8},{28,12},{1,17},{... | collective-permute-start | bytes 36872 | tf_op jit(solution)/shard_map/ppermute | solution.py:1358
  206.3 40.8 %collective-permute-start.47 = (bf16[74,8,1024]{2,1,0:T(8,128)(2,1)S(1)}, bf16[74,8,1024]{2,1,0:T(8,128)(2,1)}, u32[]{:S(2)}, u32[]{:S(2)}) collective-permute-start(bf16[74,8,1024]{2,1,0:T(8,128)(2,1)S(1)} %back_short.1.refs_15_), channel_id=1, source_target_pairs={{0,1},{1,0},{2,3},{3,2},{4,5},{5,4},{6,7},{7,6},{8,9},{9,8},{10,11... | collective-permute-start | bytes 3637256 | tf_op jit(solution)/shard_map/ppermute | solution.py:1348
  210.4 5.9 %collective-permute-start.39 = (f32[2,512]{1,0:T(2,128)S(1)}, f32[2,512]{1,0:T(2,128)S(1)}, u32[]{:S(2)}, u32[]{:S(2)}) collective-permute-start(f32[2,512]{1,0:T(2,128)S(1)} %get-tuple-element.241.refs_0_), channel_id=1, source_target_pairs={{0,4},{4,0},{8,12},{12,8},{16,20},{20,16},{24,28},{28,24},{1,5},{5... | collective-permute-start | bytes 12296 | tf_op jit(solution)/shard_map/ppermute | solution.py:1358
  211.2 5.1 %collective-permute-start.40 = (f32[2,512]{1,0:T(2,128)S(1)}, f32[2,512]{1,0:T(2,128)S(1)}, u32[]{:S(2)}, u32[]{:S(2)}) collective-permute-start(f32[2,512]{1,0:T(2,128)S(1)} %get-tuple-element.241.refs_0_), channel_id=1, source_target_pairs={{0,8},{4,12},{8,0},{12,4},{16,24},{20,28},{24,16},{28,20},{1,9},{5... | collective-permute-start | bytes 12296 | tf_op jit(solution)/shard_map/ppermute | solution.py:1358
  235.2 4.8 %collective-permute-start.45 = (f32[2,512]{1,0:T(2,128)S(1)}, f32[2,512]{1,0:T(2,128)S(1)}, u32[]{:S(2)}, u32[]{:S(2)}) collective-permute-start(f32[2,512]{1,0:T(2,128)S(1)} %get-tuple-element.252.refs_0_), channel_id=1, source_target_pairs={{0,12},{4,8},{8,4},{12,0},{16,28},{20,24},{24,20},{28,16},{1,13},{... | collective-permute-start | bytes 12296 | tf_op jit(solution)/shard_map/ppermute | solution.py:1358
  240.0 6.4 %collective-permute-start.46 = (f32[2,512]{1,0:T(2,128)S(1)}, f32[2,512]{1,0:T(2,128)S(1)}, u32[]{:S(2)}, u32[]{:S(2)}) collective-permute-start(f32[2,512]{1,0:T(2,128)S(1)} %add.19.refs_9_), channel_id=1, source_target_pairs={{0,16},{4,20},{8,24},{12,28},{16,0},{20,4},{24,8},{28,12},{1,17},{... | collective-permute-start | bytes 12296 | tf_op jit(solution)/shard_map/ppermute | solution.py:1358
  246.4 18.6 %collective-permute-start.51 = (bf16[2304,128]{1,0:T(8,128)(2,1)S(1)}, bf16[2304,128]{1,0:T(8,128)(2,1)S(1)}, u32[]{:S(2)}, u32[]{:S(2)}) collective-permute-start(bf16[2304,128]{1,0:T(8,128)(2,1)S(1)} %get-tuple-element.261), channel_id=1, source_target_pairs={{0,4},{4,0},{8,12},{12,8},{16,20},{20,16},{24,28},{28,24},{1,5},{5... | collective-permute-start | bytes 1769480 | tf_op jit(solution)/shard_map/ppermute | solution.py:1409
  265.0 4.6 %collective-permute-start.52 = (f32[2,1024]{1,0:T(2,128)S(1)}, f32[2,1024]{1,0:T(2,128)S(1)}, u32[]{:S(2)}, u32[]{:S(2)}) collective-permute-start(f32[2,1024]{1,0:T(2,128)S(1)} %add.20.refs_7_), channel_id=1, source_target_pairs={{0,16},{4,20},{8,24},{12,28},{16,0},{20,4},{24,8},{28,12},{1,17},{... | collective-permute-start | bytes 24584 | tf_op jit(solution)/shard_map/ppermute | solution.py:1358
  269.6 18.3 %collective-permute-start.56 = (bf16[1152,128]{1,0:T(8,128)(2,1)S(1)}, bf16[1152,128]{1,0:T(8,128)(2,1)S(1)}, u32[]{:S(2)}, u32[]{:S(2)}) collective-permute-start(bf16[1152,128]{1,0:T(8,128)(2,1)S(1)} %get-tuple-element.277), channel_id=1, source_target_pairs={{0,8},{4,12},{8,0},{12,4},{16,24},{20,28},{24,16},{28,20},{1,9},{5... | collective-permute-start | bytes 884744 | tf_op jit(solution)/shard_map/ppermute | solution.py:1409
  279.8 7.4 %collective-permute-start.53 = (f32[2,256]{1,0:T(2,128)S(1)}, f32[2,256]{1,0:T(2,128)S(1)}, u32[]{:S(2)}, u32[]{:S(2)}) collective-permute-start(f32[2,256]{1,0:T(2,128)S(1)} %get-tuple-element.268.refs_0_), channel_id=1, source_target_pairs={{0,4},{4,0},{8,12},{12,8},{16,20},{20,16},{24,28},{28,24},{1,5},{5... | collective-permute-start | bytes 6152 | tf_op jit(solution)/shard_map/ppermute | solution.py:1358
  280.5 6.8 %collective-permute-start.54 = (f32[2,256]{1,0:T(2,128)S(1)}, f32[2,256]{1,0:T(2,128)S(1)}, u32[]{:S(2)}, u32[]{:S(2)}) collective-permute-start(f32[2,256]{1,0:T(2,128)S(1)} %get-tuple-element.268.refs_0_), channel_id=1, source_target_pairs={{0,8},{4,12},{8,0},{12,4},{16,24},{20,28},{24,16},{28,20},{1,9},{5... | collective-permute-start | bytes 6152 | tf_op jit(solution)/shard_map/ppermute | solution.py:1358
  282.1 5.1 %collective-permute-start.55 = (f32[2,256]{1,0:T(2,128)S(1)}, f32[2,256]{1,0:T(2,128)S(1)}, u32[]{:S(2)}, u32[]{:S(2)}) collective-permute-start(f32[2,256]{1,0:T(2,128)S(1)} %get-tuple-element.268.refs_0_), channel_id=1, source_target_pairs={{0,12},{4,8},{8,4},{12,0},{16,28},{20,24},{24,20},{28,16},{1,13},{... | collective-permute-start | bytes 6152 | tf_op jit(solution)/shard_map/ppermute | solution.py:1358
  287.2 26.1 %collective-permute-start.62 = (bf16[768,128]{1,0:T(8,128)(2,1)S(1)}, bf16[768,128]{1,0:T(8,128)(2,1)S(1)}, u32[]{:S(2)}, u32[]{:S(2)}) collective-permute-start(bf16[768,128]{1,0:T(8,128)(2,1)S(1)} %get-tuple-element.286), channel_id=1, source_target_pairs={{0,4},{4,0},{8,12},{12,8},{16,20},{20,16},{24,28},{28,24},{1,5},{5... | collective-permute-start | bytes 589832 | tf_op jit(solution)/shard_map/ppermute | solution.py:1409
  287.9 4.6 %collective-permute-start.57 = (f32[2,256]{1,0:T(2,128)S(1)}, f32[2,256]{1,0:T(2,128)S(1)}, u32[]{:S(2)}, u32[]{:S(2)}) collective-permute-start(f32[2,256]{1,0:T(2,128)S(1)} %add.21.refs_7_), channel_id=1, source_target_pairs={{0,16},{4,20},{8,24},{12,28},{16,0},{20,4},{24,8},{28,12},{1,17},{... | collective-permute-start | bytes 6152 | tf_op jit(solution)/shard_map/ppermute | solution.py:1358
  292.5 20.8 %collective-permute-start.61 = (bf16[576,128]{1,0:T(8,128)(2,1)S(1)}, bf16[576,128]{1,0:T(8,128)(2,1)S(1)}, u32[]{:S(2)}, u32[]{:S(2)}) collective-permute-start(bf16[576,128]{1,0:T(8,128)(2,1)S(1)} %get-tuple-element.285), channel_id=1, source_target_pairs={{0,16},{4,20},{8,24},{12,28},{16,0},{20,4},{24,8},{28,12},{1,17},{... | collective-permute-start | bytes 442376 | tf_op jit(solution)/shard_map/ppermute | solution.py:1409
  308.5 4.8 %collective-permute-start.60 = (f32[2,256]{1,0:T(2,128)S(1)}, f32[2,256]{1,0:T(2,128)S(1)}, u32[]{:S(2)}, u32[]{:S(2)}) collective-permute-start(f32[2,256]{1,0:T(2,128)S(1)} %get-tuple-element.284.refs_0_), channel_id=1, source_target_pairs={{0,12},{4,8},{8,4},{12,0},{16,28},{20,24},{24,20},{28,16},{1,13},{... | collective-permute-start | bytes 6152 | tf_op jit(solution)/shard_map/ppermute | solution.py:1358
  313.3 9.6 %collective-permute-start.63 = (f32[2,256]{1,0:T(2,128)S(1)}, f32[2,256]{1,0:T(2,128)S(1)}, u32[]{:S(2)}, u32[]{:S(2)}) collective-permute-start(f32[2,256]{1,0:T(2,128)S(1)} %add.22.refs_7_), channel_id=1, source_target_pairs={{0,16},{4,20},{8,24},{12,28},{16,0},{20,4},{24,8},{28,12},{1,17},{... | collective-permute-start | bytes 6152 | tf_op jit(solution)/shard_map/ppermute | solution.py:1358
  323.0 12.6 %collective-permute-start.64 = (bf16[832,128]{1,0:T(8,128)(2,1)S(1)}, bf16[832,128]{1,0:T(8,128)(2,1)S(1)}, u32[]{:S(2)}, u32[]{:S(2)}) collective-permute-start(bf16[832,128]{1,0:T(8,128)(2,1)S(1)} %get-tuple-element.303), channel_id=1, source_target_pairs={{0,4},{4,0},{8,12},{12,8},{16,20},{20,16},{24,28},{28,24},{1,5},{5... | collective-permute-start | bytes 638984 | tf_op jit(solution)/shard_map/ppermute | solution.py:1409
  324.7 10.9 %collective-permute-start.66 = (bf16[576,128]{1,0:T(8,128)(2,1)S(1)}, bf16[576,128]{1,0:T(8,128)(2,1)S(1)}, u32[]{:S(2)}, u32[]{:S(2)}) collective-permute-start(bf16[576,128]{1,0:T(8,128)(2,1)S(1)} %stride_2s.1.refs_0_), channel_id=1, source_target_pairs={{0,16},{4,20},{8,24},{12,28},{16,0},{20,4},{24,8},{28,12},{1,17},{... | collective-permute-start | bytes 442376 | tf_op jit(solution)/shard_map/ppermute | solution.py:1409
  327.5 6.2 %collective-permute-start.65 = (bf16[384,128]{1,0:T(8,128)(2,1)S(1)}, bf16[384,128]{1,0:T(8,128)(2,1)S(1)}, u32[]{:S(2)}, u32[]{:S(2)}) collective-permute-start(bf16[384,128]{1,0:T(8,128)(2,1)S(1)} %get-tuple-element.304), channel_id=1, source_target_pairs={{0,8},{4,12},{8,0},{12,4},{16,24},{20,28},{24,16},{28,20},{1,9},{5... | collective-permute-start | bytes 294920 | tf_op jit(solution)/shard_map/ppermute | solution.py:1409
  336.2 10.0 %collective-permute-start.73 = (bf16[1152,128]{1,0:T(8,128)(2,1)S(1)}, bf16[1152,128]{1,0:T(8,128)(2,1)S(1)}, u32[]{:S(2)}, u32[]{:S(2)}) collective-permute-start(bf16[1152,128]{1,0:T(8,128)(2,1)S(1)} %bitcast.71), channel_id=1, source_target_pairs={{0,8},{4,12},{8,0},{12,4},{16,24},{20,28},{24,16},{28,20},{1,9},{5... | collective-permute-start | bytes 884744 | tf_op jit(solution)/shard_map/ppermute | solution.py:1409
  336.8 8.1 %collective-permute-start.75 = (bf16[192,128]{1,0:T(8,128)(2,1)S(1)}, bf16[192,128]{1,0:T(8,128)(2,1)S(1)}, u32[]{:S(2)}, u32[]{:S(2)}) collective-permute-start(bf16[192,128]{1,0:T(8,128)(2,1)S(1)} %get-tuple-element.321), channel_id=1, source_target_pairs={{0,16},{4,20},{8,24},{12,28},{16,0},{20,4},{24,8},{28,12},{1,17},{... | collective-permute-start | bytes 147464 | tf_op jit(solution)/shard_map/ppermute | solution.py:1409
  340.5 7.2 %collective-permute-start.67 = (bf16[208,128]{1,0:T(8,128)(2,1)S(1)}, bf16[208,128]{1,0:T(8,128)(2,1)S(1)}, u32[]{:S(2)}, u32[]{:S(2)}) collective-permute-start(bf16[208,128]{1,0:T(8,128)(2,1)S(1)} %get-tuple-element.311), channel_id=1, source_target_pairs={{0,8},{4,12},{8,0},{12,4},{16,24},{20,28},{24,16},{28,20},{1,9},{5... | collective-permute-start | bytes 159752 | tf_op jit(solution)/shard_map/ppermute | solution.py:1409
  340.5 7.1 %collective-permute-start.68 = (bf16[208,128]{1,0:T(8,128)(2,1)S(1)}, bf16[208,128]{1,0:T(8,128)(2,1)S(1)}, u32[]{:S(2)}, u32[]{:S(2)}) collective-permute-start(bf16[208,128]{1,0:T(8,128)(2,1)S(1)} %get-tuple-element.312), channel_id=1, source_target_pairs={{0,16},{4,20},{8,24},{12,28},{16,0},{20,4},{24,8},{28,12},{1,17},{... | collective-permute-start | bytes 159752 | tf_op jit(solution)/shard_map/ppermute | solution.py:1409
  342.5 5.9 %collective-permute-start.69 = (bf16[208,128]{1,0:T(8,128)(2,1)S(1)}, bf16[208,128]{1,0:T(8,128)(2,1)S(1)}, u32[]{:S(2)}, u32[]{:S(2)}) collective-permute-start(bf16[208,128]{1,0:T(8,128)(2,1)S(1)} %get-tuple-element.313), channel_id=1, source_target_pairs={{0,24},{4,28},{8,16},{12,20},{16,8},{20,12},{24,0},{28,4},{1,25},{... | collective-permute-start | bytes 159752 | tf_op jit(solution)/shard_map/ppermute | solution.py:1409
  344.9 8.0 %collective-permute-start.76 = (bf16[192,128]{1,0:T(8,128)(2,1)S(1)}, bf16[192,128]{1,0:T(8,128)(2,1)S(1)}, u32[]{:S(2)}, u32[]{:S(2)}) collective-permute-start(bf16[192,128]{1,0:T(8,128)(2,1)S(1)} %mid_2s.1.refs_0_), channel_id=1, source_target_pairs={{0,16},{4,20},{8,24},{12,28},{16,0},{20,4},{24,8},{28,12},{1,17},{... | collective-permute-start | bytes 147464 | tf_op jit(solution)/shard_map/ppermute | solution.py:1409
  346.8 16.1 %collective-permute-start.74 = (bf16[2304,128]{1,0:T(8,128)(2,1)S(1)}, bf16[2304,128]{1,0:T(8,128)(2,1)S(1)}, u32[]{:S(2)}, u32[]{:S(2)}) collective-permute-start(bf16[2304,128]{1,0:T(8,128)(2,1)S(1)} %bitcast.69), channel_id=1, source_target_pairs={{0,4},{4,0},{8,12},{12,8},{16,20},{20,16},{24,28},{28,24},{1,5},{5... | collective-permute-start | bytes 1769480 | tf_op jit(solution)/shard_map/ppermute | solution.py:1409
  348.5 5.1 %collective-permute-start.70 = (bf16[208,128]{1,0:T(8,128)(2,1)S(1)}, bf16[208,128]{1,0:T(8,128)(2,1)S(1)}, u32[]{:S(2)}, u32[]{:S(2)}) collective-permute-start(bf16[208,128]{1,0:T(8,128)(2,1)S(1)} %last_1s.1.refs_0_), channel_id=1, source_target_pairs={{0,8},{4,12},{8,0},{12,4},{16,24},{20,28},{24,16},{28,20},{1,9},{5... | collective-permute-start | bytes 159752 | tf_op jit(solution)/shard_map/ppermute | solution.py:1409
  348.6 5.1 %collective-permute-start.71 = (bf16[208,128]{1,0:T(8,128)(2,1)S(1)}, bf16[208,128]{1,0:T(8,128)(2,1)S(1)}, u32[]{:S(2)}, u32[]{:S(2)}) collective-permute-start(bf16[208,128]{1,0:T(8,128)(2,1)S(1)} %last_1s.1.refs_0_), channel_id=1, source_target_pairs={{0,16},{4,20},{8,24},{12,28},{16,0},{20,4},{24,8},{28,12},{1,17},{... | collective-permute-start | bytes 159752 | tf_op jit(solution)/shard_map/ppermute | solution.py:1409
  351.5 6.0 %collective-permute-start.72 = (bf16[208,128]{1,0:T(8,128)(2,1)S(1)}, bf16[208,128]{1,0:T(8,128)(2,1)S(1)}, u32[]{:S(2)}, u32[]{:S(2)}) collective-permute-start(bf16[208,128]{1,0:T(8,128)(2,1)S(1)} %last_1s.1.refs_0_), channel_id=1, source_target_pairs={{0,24},{4,28},{8,16},{12,20},{16,8},{20,12},{24,0},{28,4},{1,25},{... | collective-permute-start | bytes 159752 | tf_op jit(solution)/shard_map/ppermute | solution.py:1409
  353.5 6.0 %collective-permute-start.77 = (bf16[384,128]{1,0:T(8,128)(2,1)S(1)}, bf16[384,128]{1,0:T(8,128)(2,1)S(1)}, u32[]{:S(2)}, u32[]{:S(2)}) collective-permute-start(bf16[384,128]{1,0:T(8,128)(2,1)S(1)} %bitcast.79), channel_id=1, source_target_pairs={{0,8},{4,12},{8,0},{12,4},{16,24},{20,28},{24,16},{28,20},{1,9},{5... | collective-permute-start | bytes 294920 | tf_op jit(solution)/shard_map/ppermute | solution.py:1409
  358.0 10.1 %collective-permute-start.79 = (bf16[832,128]{1,0:T(8,128)(2,1)S(1)}, bf16[832,128]{1,0:T(8,128)(2,1)S(1)}, u32[]{:S(2)}, u32[]{:S(2)}) collective-permute-start(bf16[832,128]{1,0:T(8,128)(2,1)S(1)} %bitcast.73), channel_id=1, source_target_pairs={{0,4},{4,0},{8,12},{12,8},{16,20},{20,16},{24,28},{28,24},{1,5},{5... | collective-permute-start | bytes 638984 | tf_op jit(solution)/shard_map/ppermute | solution.py:1409
  360.0 8.1 %collective-permute-start.78 = (bf16[768,128]{1,0:T(8,128)(2,1)S(1)}, bf16[768,128]{1,0:T(8,128)(2,1)S(1)}, u32[]{:S(2)}, u32[]{:S(2)}) collective-permute-start(bf16[768,128]{1,0:T(8,128)(2,1)S(1)} %bitcast.75), channel_id=1, source_target_pairs={{0,4},{4,0},{8,12},{12,8},{16,20},{20,16},{24,28},{28,24},{1,5},{5... | collective-permute-start | bytes 589832 | tf_op jit(solution)/shard_map/ppermute | solution.py:1409
  (70 other events, 448.7 us)
Sparse Core Ops, SparseCore 0:
  47.8 46.0 all-gather.4
  95.4 58.5 all-gather.6
  217.5 97.8 all-reduce.2

commit v2 on v1

--- a/solution.py
+++ b/solution.py
@@ -843,7 +843,7 @@
         acc = [jnp.zeros((VIEWS, chans), F32)] * 3
         for part, (lo, hi) in enumerate(spans):
             half = geo.parts[part][0] // 2
-            cot[lo:hi] = as_pix(cots[part][j][...].astype(F32))
+            cot[lo:hi] = as_pix(cots[part][j][...].astype(F32))[: hi - lo]
 
             def row(i, carry, part=part, lo=lo, half=half):
                 at = pl.ds(lo + i * half, half)
@@ -1177,7 +1177,7 @@
 
     zero = [jnp.zeros((VIEWS, 256), F32)] * 4
     big, small = geo.loop(body, [zero, zero], io)
-    sums = [jnp.broadcast_to(rows_sum(b * lives[0] + s * lives[1]), (8, 256)) for b, s in zip(big, small)]
+    sums = [jnp.broadcast_to(rows_sum(b * lives[0] + s * lives[1]), (16, 256)) for b, s in zip(big, small)]
     for j in range(4):
         part[...] = tn(devq[...], xs[j])
         out[:, 256 * j : 256 * j + 256] = jnp.concatenate([part[mine, :], sums[j]], axis=0).astype(BF16)
@@ -1294,7 +1294,8 @@
         for block in range(2):
             dmix[t, :, 128 * block : 128 * block + 128] = flat[at : at + 64]
             at += 64
-    fix = dev[64:65].astype(F32) * coef[1] + dev[0:64].astype(F32) * coef[2]
+    dev = dev[...].astype(F32)
+    fix = dev[64:65] * coef[1] + dev[0:64] * coef[2]
     for block in range(8):
         lanes = slice(128 * block, 128 * block + 128)
         dreduce[:, lanes] = flat[at : at + 64] * coef[0] - fix[:, lanes]
@@ -1514,7 +1515,12 @@
         return [v[:, 128 * b : 128 * b + 128] for b in range(v.shape[1] // 128)]
 
     w_mid = jnp.concatenate(blocks128(w_expand) + blocks128(w_narrow))
-    last_in = jnp.concatenate([w_short, w_widen, rows_of(cot_big), rows_of(cot_small)])
+    def whole_tiles(v):
+        return jnp.pad(v, ((0, -v.shape[0] % 16), (0, 0)))
+
+    cots = [whole_tiles(rows_of(v)) for v in (cot_big, cot_small)]
+    cot_rows = [v.shape[0] for v in cots]
+    last_in = jnp.concatenate([w_short, w_widen] + cots)
     wst = w_stride.reshape(-1, w_stride.shape[3])
     xb[3], xsm[2], w_mid, last_in, wst = after(xb[3], xsm[2], w_mid, last_in, wst)
     xsm = passed_on(xsm)
@@ -1636,19 +1642,19 @@
         "dev_products",
         k(k_dev_products),
         smem + flow("all", devq) + x_all,
-        [sds((m3 // 4 + 8, c3), BF16)],
+        [sds((m3 // 4 + 16, c3), BF16)],
         [pltpu.VMEM((128, c3 // 4), F32)],
         ahead=8,
     )
     a5, b5, (dev,) = sync_stats(st, cnt4, free={last: [dev]})
     a5, last_in, mids = after(a5, last_in, mids)
-    at_w, at_b, at_s = c3, c3 + m4, c3 + m4 + geo.qb * VIEWS
+    at_w, at_b, at_s = c3, c3 + m4, c3 + m4 + cot_rows[0]
 
     def from_chips(base, rows):
         return [(last_in, Flow("chip", base, (rows, c4q), j)) for j in range(2)]
 
     wsh, wwi = from_chips(0, c3), from_chips(at_w, m4)
-    cots = from_chips(at_b, geo.qb * VIEWS) + from_chips(at_s, geo.qs * VIEWS)
+    cots = from_chips(at_b, cot_rows[0]) + from_chips(at_s, cot_rows[1])
     side, st_side = run(
         "short",
         k(k_short),

time: 382 us -> 383 us (level)
  transfers between devices with their start and end apart: 83 -> 83, of which waited for: 49 -> 48; matrix products, arithmetic and copies ran while one was open for 2% -> 2% of each run, Pallas kernels for 38% -> 38%
where the time goes in v2:
time: 383 us; the launch traced here: 378 us
  Pallas kernels  158 us (41%)
  starting transfers between devices  96.2 us (25%)
  waiting for transfers between devices  88.4 us (23%)
  local copies, waits for them, and re-layouts  19 us (5%)
  between operations  14.8 us (4%)
    pallas_call x53, Pallas kernels, call(): pl.pallas_call(body, out_shape=out_shapes, in_specs=specs, out_specs=out_...  158 us
    ppermute x48, starting transfers between devices, peers(): out.append(lax.ppermute(v, 'img', [(i, i ^ m << shift) for i in range(ni)]))  62.7 us
    ppermute x48, waiting for transfers between devices, peers(): out.append(lax.ppermute(v, 'img', [(i, i ^ m << shift) for i in range(ni)]))  54.6 us
    ppermute x20, starting transfers between devices, to_peers(): out.append(lax.ppermute(parts[m if len(parts) > 1 else 0], 'img', perm))  26.9 us
    ppermute x12, waiting for transfers between devices, over_ch(): return lax.ppermute(v, 'ch', [(i, i ^ k) for i in range(nc)])  26.7 us
    unnamed x77, local copies, waits for them, and re-layouts  16.1 us
  transfers between devices with their start and end apart: 83, of which 48 were waited for; matrix products, arithmetic and copies ran while one was open for 2% of the time, Pallas kernels for 38%

profile of v2, /device:TPU:0, one launch (start us, length us, event | category | flops | bytes accessed | tf_op | source)
XLA Modules:
  0.0 378.3 jit_solution(16774993629717404828)
XLA Ops:
  7.8 2.6 collective-permute-start.1
  22.5 6.9 %collective-permute-done.1.refs_4_.refs_5_.refs_6_ = bf16[1568,256]{1,0:T(8,128)(2,1)} collective-permute-done((bf16[1568,256]{1,0:T(8,128)(2,1)}, bf16[1568,256]{1,0:T(8,128)(2,1)}, u32[]{:S(2)}, u32[]{:S(2)}) %collective-permute-start.1) | collective-permute-done | bytes 802848 | tf_op jit(solution)/shard_map/ppermute | solution.py:1349
  32.0 15.6 %collective-permute-done.3.refs_8_.refs_12_.p2.refs_9_.refs_15_.refs_10_ = bf16[1696,256]{1,0:T(8,128)(2,1)S(1)} collective-permute-done((bf16[1696,256]{1,0:T(8,128)(2,1)S(1)}, bf16[1696,256]{1,0:T(8,128)(2,1)S(1)}, u32[]{:S(2)}, u32[]{:S(2)}) %collective-permute-start.3) | collective-permute-done | bytes 868384 | tf_op jit(solution)/shard_map/ppermute | solution.py:1349
  53.1 6.7 %reduce.1 = (f32[296,8,256]{2,1,0:T(8,128)S(1)}, f32[2,256]{1,0:T(2,128)S(1)}) custom-call(s32[4]{0:T(128)S(1)} %get-tuple-element.184.refs_0_.me, f32[3]{0:T(128)S(1)} %get-tuple-element.186.refs_1_.refs_2_.refs_14_, bf16[1568,256]{1,0:T(8,128)(2,1)} %bitcast.105, bf16[1568,256]{1,0:T(8,128)(2,1)} %copy-done.21, ...), custom_call_target="tpu_custom_call" | custom-call | tf_op jit(solution)/shard_map/reduce/pallas_call | solution.py:316
  66.7 2.5 collective-permute-done.8.refs_3_
  69.9 2.7 collective-permute-start.9
  74.4 6.4 %mix.1 = (f32[296,8,256]{2,1,0:T(8,128)S(1)}, bf16[1792,768]{1,0:T(8,128)(2,1)}, bf16[960,768]{1,0:T(8,128)(2,1)}, f32[2,256]{1,0:T(2,128)S(1)}, bf16[2368,128]{1,0:T(8,128)(2,1)}, /*index=5*/f32[296,8,256]{2,1,0:T(8,128)}) custom-call(s32[4]{0:T(128)S(1)} %get-tuple-element.184.refs_0_.me, f32[3]{0:T(128)S(1)} %get-tuple-element.186.refs_1_.refs_2_.refs_14_, ...), custom_call_target="tpu_custom_call" | custom-call | tf_op jit(solution)/shard_map/mix/pallas_call | solution.py:316
  85.3 2.5 collective-permute-done.13.refs_3_
  88.5 2.7 collective-permute-start.14
  93.8 6.7 %expand.1 = (f32[296,8,1024]{2,1,0:T(8,128)S(1)}, bf16[2368,256]{1,0:T(8,128)(2,1)}, f32[2,1024]{1,0:T(2,128)S(1)}, f32[296,8,256]{2,1,0:T(8,128)}) custom-call(s32[4]{0:T(128)S(1)} %get-tuple-element.184.refs_0_.me, f32[3]{0:T(128)S(1)} %get-tuple-element.186.refs_1_.refs_2_.refs_14_, f32[296,8,256]{2,1,0:T(8,128)S(1)} %get-tuple-element.203.refs_2_, ...), custom_call_target="tpu_custom_call" | custom-call | tf_op jit(solution)/shard_map/expand/pallas_call | solution.py:316
  104.6 2.1 collective-permute-done.19.refs_3_
  107.4 2.6 collective-permute-start.20
  112.0 13.9 %narrow.1 = (f32[2,2,7,7,8,512]{5,4,3,2,1,0:T(8,128)}, f32[2,2,5,5,8,512]{5,4,3,2,1,0:T(8,128)}, bf16[2368,1024]{1,0:T(8,128)(2,1)}, bf16[592,1024]{1,0:T(8,128)...) custom-call(s32[4]{0:T(128)S(1)} %get-tuple-element.184.refs_0_.me, ...), custom_call_target="tpu_custom_call" | custom-call | tf_op jit(solution)/shard_map/narrow/pallas_call | solution.py:316
  130.4 2.5 collective-permute-done.23.refs_3_
  133.5 2.7 collective-permute-start.24
  139.5 9.1 %stride.1 = (f32[74,8,512]{2,1,0:T(8,128)S(1)}, bf16[9,592,512]{2,1,0:T(8,128)(2,1)}, f32[2,512]{1,0:T(2,128)S(1)}) custom-call(s32[4]{0:T(128)S(1)} %get-tuple-element.184.refs_0_.me, f32[3]{0:T(128)S(1)} %get-tuple-element.185.refs_1_.nf, f32[3]{0:T(128)S(1)} %get-tuple-element.186.refs_1_.refs_2_.refs_14_, ...), custom_call_target="tpu_custom_call" | custom-call | tf_op jit(solution)/shard_map/stride/pallas_call | solution.py:316
  152.8 2.1 collective-permute-done.28.refs_3_
  155.5 2.6 collective-permute-start.29
  158.2 6.5 %dev_products.1 = bf16[80,1024]{1,0:T(8,128)(2,1)} custom-call(s32[4]{0:T(128)S(1)} %get-tuple-element.184.refs_0_.me, bf16[2368,128]{1,0:T(8,128)(2,1)} %get-tuple-element.225.refs_1_, bf16[1568,256]{1,0:T(8,128)(2,1)} %bitcast.107, bf16[1568,256]{1,0:T(8,128)(2,1)} %copy-done.21, bf16[1568,256]{1,0:T(8,128)(2,1)} %collective-permute-done.1.refs_4_.refs_5_.refs_6_, ...), custom_call_target="tpu_custom_call" | custom-call | tf_op jit(solution)/shard_map/dev_products/pallas_call | solution.py:316
  164.7 3.8 %short.1 = (f32[2,74,8,512]{3,2,1,0:T(8,128)S(1)}, f32[2,2,512]{2,1,0:T(2,128)S(1)}) custom-call(s32[4]{0:T(128)S(1)} %get-tuple-element.184.refs_0_.me, f32[3]{0:T(128)S(1)} %get-tuple-element.185.refs_1_.nf, bf16[592,1024]{1,0:T(8,128)(2,1)S(1)} %get-tuple-element.229.refs_2_.mids, bf16[2,2144,512]{2,1,0:T(8,128)(2,1)} %bitcast.91, ...), custom_call_target="tpu_custom_call" | custom-call | tf_op jit(solution)/shard_map/short/pallas_call | solution.py:316
  168.5 2.8 widen.1
  176.0 2.5 collective-permute-done.32.refs_3_
  179.4 4.4 %collective-permute-done.33.refs_5_.refs_6_ = f32[2,4,512]{2,1,0:T(4,128)S(1)} collective-permute-done((f32[2,4,512]{2,1,0:T(4,128)S(1)}, f32[2,4,512]{2,1,0:T(4,128)S(1)}, u32[]{:S(2)}, u32[]{:S(2)}) %collective-permute-start.33) | collective-permute-done | bytes 16416 | tf_op jit(solution)/shard_map/ppermute | solution.py:1359
  183.8 4.9 %total.1 = (f32[49,8,512]{2,1,0:T(8,128)}, f32[25,8,512]{2,1,0:T(8,128)}, f32[2,74,8,512]{3,2,1,0:T(8,128)S(1)}, f32[2,3,512]{2,1,0:T(4,128)S(1)}) custom-call(s32[4]{0:T(128)S(1)} %get-tuple-element.184.refs_0_.me, f32[3]{0:T(128)S(1)} %get-tuple-element.185.refs_1_.nf, f32[2,74,8,512]{3,2,1,0:T(8,128)S(1)} %get-tuple-element.231.refs_2_.refs_3_, ...), custom_call_target="tpu_custom_call" | custom-call | tf_op jit(solution)/shard_map/total/pallas_call | solution.py:316
  193.0 2.0 collective-permute-done.36.refs_3_
  195.5 4.3 %collective-permute-done.37.refs_9_ = f32[2,3,512]{2,1,0:T(4,128)S(1)} collective-permute-done((f32[2,3,512]{2,1,0:T(4,128)S(1)}, f32[2,3,512]{2,1,0:T(4,128)S(1)}, u32[]{:S(2)}, u32[]{:S(2)}) %collective-permute-start.37) | collective-permute-done | bytes 12320 | tf_op jit(solution)/shard_map/ppermute | solution.py:1359
  199.7 3.0 back_wide.1
  202.8 3.6 back_short.1.refs_15_
  206.9 2.5 back_act5.1
  213.9 2.4 dw_wide.1
  217.8 4.2 %collective-permute-done.42.refs_8_ = f32[2,512]{1,0:T(2,128)S(1)} collective-permute-done((f32[2,512]{1,0:T(2,128)S(1)}, f32[2,512]{1,0:T(2,128)S(1)}, u32[]{:S(2)}, u32[]{:S(2)}) %collective-permute-start.42) | collective-permute-done | bytes 4128 | tf_op jit(solution)/shard_map/ppermute | solution.py:1359
  223.3 10.2 %back_stride.1 = (f32[2,2,7,7,8,512]{5,4,3,2,1,0:T(8,128)S(1)}, f32[2,2,5,5,8,512]{5,4,3,2,1,0:T(8,128)S(1)}, bf16[592,512]{1,0:T(8,128)(2,1)S(1)}, f32[2,512]{1,0:T(2,128)S(1)}, f32[2,512]{1,0:T(2,128)S(1)}) custom-call(s32[4]{0:T(128)S(1)} %get-tuple-element.184.refs_0_.me, f32[3]{0:T(128)S(1)} %get-tuple-element.185.refs_1_.nf, ...), custom_call_target="tpu_custom_call" | custom-call | tf_op jit(solution)/shard_map/back_stride/pallas_call | solution.py:316
  240.4 6.0 %dw_stride.1 = (bf16[2304,128]{1,0:T(8,128)(2,1)S(1)}, bf16[2304,128]{1,0:T(8,128)(2,1)S(1)}) custom-call(s32[4]{0:T(128)S(1)} %get-tuple-element.184.refs_0_.me, bf16[9,592,512]{2,1,0:T(8,128)(2,1)} %get-tuple-element.253.refs_1_, bf16[592,512]{1,0:T(8,128)(2,1)S(1)} %get-tuple-element.254.refs_2_), custom_call_target="tpu_custom_call" | custom-call | tf_op jit(solution)/shard_map/dw_stride/pallas_call | solution.py:316
  247.2 11.1 %back_narrow.1 = (bf16[2368,1024]{1,0:T(8,128)(2,1)S(1)}, bf16[2368,512]{1,0:T(8,128)(2,1)}, f32[2,1024]{1,0:T(2,128)S(1)}, f32[2,512]{1,0:T(2,128)S(1)}) custom-call(s32[4]{0:T(128)S(1)} %get-tuple-element.184.refs_0_.me, f32[3]{0:T(128)S(1)} %get-tuple-element.186.refs_1_.refs_2_.refs_14_, f32[2,2,7,7,8,512]{5,4,3,2,1,0:T(8,128)S(1)} %get-tuple-element.250.refs_2_, ...), custom_call_target="tpu_custom_call" | custom-call | tf_op jit(solution)/shard_map/back_narrow/pallas_call | solution.py:316
  265.0 2.7 collective-permute-start.52
  271.0 8.7 %back_expand.1 = (f32[296,8,256]{2,1,0:T(8,128)S(1)}, bf16[2368,256]{1,0:T(8,128)(2,1)}, bf16[2368,256]{1,0:T(8,128)(2,1)}, f32[2,256]{1,0:T(2,128)S(1)}, f32[2,1024]{1,0:T(2,128)S(1)}) custom-call(s32[4]{0:T(128)S(1)} %get-tuple-element.184.refs_0_.me, f32[3]{0:T(128)S(1)} %get-tuple-element.186.refs_1_.refs_2_.refs_14_, ...), custom_call_target="tpu_custom_call" | custom-call | tf_op jit(solution)/shard_map/back_expand/pallas_call | solution.py:316
  284.6 2.6 dw_mid.1
  288.1 2.5 collective-permute-start.57
  292.7 2.4 collective-permute-start.61
  295.1 11.4 %back_mix.1 = (f32[296,8,256]{2,1,0:T(8,128)}, bf16[2368,256]{1,0:T(8,128)(2,1)}, f32[2,256]{1,0:T(2,128)S(1)}, f32[2,256]{1,0:T(2,128)S(1)}, bf16[2368,128]{1,0:T(8,128)(2,1)}) custom-call(s32[4]{0:T(128)S(1)} %get-tuple-element.184.refs_0_.me, f32[3]{0:T(128)S(1)} %get-tuple-element.186.refs_1_.refs_2_.refs_14_, ...), custom_call_target="tpu_custom_call" | custom-call | tf_op jit(solution)/shard_map/back_mix/pallas_call | solution.py:316
  314.2 8.8 %dw_last.1 = (bf16[832,128]{1,0:T(8,128)(2,1)S(1)}, bf16[832,128]{1,0:T(8,128)(2,1)S(1)}) custom-call(s32[4]{0:T(128)S(1)} %get-tuple-element.184.refs_0_.me, bf16[1792,768]{1,0:T(8,128)(2,1)} %get-tuple-element.288.refs_1_, bf16[960,768]{1,0:T(8,128)(2,1)} %get-tuple-element.289.refs_2_, bf16[2368,256]{1,0:T(8,128)(2,1)} %get-tuple-element.290.refs_3_, ...), custom_call_target="tpu_custom_call" | custom-call | tf_op jit(solution)/shard_map/dw_last/pallas_call | solution.py:316
  325.1 2.9 collective-permute-start.66
  328.0 5.9 %back_reduce.1 = (f32[196,8,256]{2,1,0:T(8,128)}, f32[100,8,256]{2,1,0:T(8,128)}, f32[2,256]{1,0:T(2,128)S(1)}, f32[3,256]{1,0:T(4,128)S(1)}) custom-call(s32[4]{0:T(128)S(1)} %get-tuple-element.184.refs_0_.me, f32[3]{0:T(128)S(1)} %get-tuple-element.186.refs_1_.refs_2_.refs_14_, f32[296,8,256]{2,1,0:T(8,128)} %get-tuple-element.283.refs_2_, ...), custom_call_target="tpu_custom_call" | custom-call | tf_op jit(solution)/shard_map/back_reduce/pallas_call | solution.py:316
  337.2 2.8 collective-permute-start.75
  342.4 2.6 collective-permute-start.69
  348.5 3.2 collective-permute-start.71
  353.8 3.9 %collective-permute-done.72.refs_3_ = bf16[208,128]{1,0:T(8,128)(2,1)S(1)} collective-permute-done((bf16[208,128]{1,0:T(8,128)(2,1)S(1)}, bf16[208,128]{1,0:T(8,128)(2,1)S(1)}, u32[]{:S(2)}, u32[]{:S(2)}) %collective-permute-start.72) | collective-permute-done | bytes 53280 | tf_op jit(solution)/shard_map/ppermute | solution.py:1410
  363.9 4.4 %out_first.1 = (f32[2,256,512]{2,1,0:T(8,128)}, f32[4,256,512]{2,1,0:T(8,128)}, f32[2,2304,128]{2,1,0:T(8,128)}) custom-call(s32[4]{0:T(128)S(1)} %get-tuple-element.184.refs_0_.me, bf16[2,256,512]{2,1,0:T(8,128)(2,1)} %bitcast.115, bf16[4,256,512]{2,1,0:T(8,128)(2,1)} %bitcast.113, bf16[1,2304,128]{2,1,0:T(8,128)(2,1)} %bitcast.70, ...), custom_call_target="tpu_custom_call" | custom-call | tf_op jit(solution)/shard_map/out_first/pallas_call | solution.py:316
  (261 shorter events, 131.5 us)
Async XLA Ops:
  7.2 118.8 %all-gather.5.cloned.1.call-start = ((), (), s32[]{:S(2)}) async-start(), calls=%async_computation | async-start | bytes 3538944 | tf_op jit(solution)/shard_map/all_gather | solution.py:1537
  7.2 11.7 %collective-permute-start = (bf16[1568,256]{1,0:T(8,128)(2,1)}, bf16[1568,256]{1,0:T(8,128)(2,1)S(1)}, u32[]{:S(2)}, u32[]{:S(2)}) collective-permute-start(bf16[1568,256]{1,0:T(8,128)(2,1)} %bitcast.103), channel_id=1, source_target_pairs={{0,1},{1,0},{2,3},{3,2},{4,5},{5,4},{6,7},{7,6},{8,9},{9,8},{10,11... | collective-permute-start | bytes 2408456 | tf_op jit(solution)/shard_map/ppermute | solution.py:1349
  7.8 21.6 %collective-permute-start.1 = (bf16[1568,256]{1,0:T(8,128)(2,1)}, bf16[1568,256]{1,0:T(8,128)(2,1)}, u32[]{:S(2)}, u32[]{:S(2)}) collective-permute-start(bf16[1568,256]{1,0:T(8,128)(2,1)} %bitcast.104), channel_id=1, source_target_pairs={{0,2},{1,3},{2,0},{3,1},{4,6},{5,7},{6,4},{7,5},{8,10},{9,11},{10,... | collective-permute-start | bytes 2408456 | tf_op jit(solution)/shard_map/ppermute | solution.py:1349
  21.3 26.3 %collective-permute-start.3 = (bf16[1696,256]{1,0:T(8,128)(2,1)S(1)}, bf16[1696,256]{1,0:T(8,128)(2,1)S(1)}, u32[]{:S(2)}, u32[]{:S(2)}) collective-permute-start(bf16[1696,256]{1,0:T(8,128)(2,1)S(1)} %constant_dynamic-update-slice_fusion.refs_6_.refs_10_.p0.refs_7_.refs_13_.refs_8_), channel_id=1, source_target_pairs={{0,2},{1,3},{2,0},{3,1},{4,6},{5,7},{6,4},{7,5},{8,10},{9,11},{10,... | collective-permute-start | bytes 2605064 | tf_op jit(solution)/shard_map/ppermute | solution.py:1349
  47.7 117.0 %all-gather.7.cloned.1.call-start = ((), (), s32[]{:S(2)}) async-start(), calls=%async_computation.1 | async-start | bytes 6586368 | tf_op jit(solution)/shard_map/all_gather | solution.py:1538
  48.4 287.1 %all-reduce.5.cloned.1.call-start = ((), (), s32[]{:S(2)}) async-start(), calls=%async_computation.2 | async-start | bytes 3473408 | tf_op jit(solution)/shard_map/psum | solution.py:1838
  59.8 21.0 %collective-permute-start.10 = (bf16[1536,128]{1,0:T(8,128)(2,1)S(1)}, bf16[1536,128]{1,0:T(8,128)(2,1)S(1)}, u32[]{:S(2)}, u32[]{:S(2)}) collective-permute-start(bf16[1536,128]{1,0:T(8,128)(2,1)S(1)} %pad_maximum_fusion.refs_6_.refs_14_.refs_17_.refs_13_), channel_id=1, source_target_pairs={{0,2},{1,3},{2,0},{3,1},{4,6},{5,7},{6,4},{7,5},{8,10},{9,11},{10,... | collective-permute-start | bytes 1179656 | tf_op jit(solution)/shard_map/ppermute | solution.py:1349
  72.6 18.6 %collective-permute-start.15 = (bf16[1536,128]{1,0:T(8,128)(2,1)S(1)}, bf16[1536,128]{1,0:T(8,128)(2,1)S(1)}, u32[]{:S(2)}, u32[]{:S(2)}) collective-permute-start(bf16[1536,128]{1,0:T(8,128)(2,1)S(1)} %pad_maximum_fusion.refs_6_.refs_14_.refs_17_.refs_13_), channel_id=1, source_target_pairs={{0,1},{1,0},{2,3},{3,2},{4,5},{5,4},{6,7},{7,6},{8,9},{9,8},{10,11... | collective-permute-start | bytes 1179656 | tf_op jit(solution)/shard_map/ppermute | solution.py:1349
  80.8 12.2 %collective-permute-start.16 = (bf16[1536,128]{1,0:T(8,128)(2,1)S(1)}, bf16[1536,128]{1,0:T(8,128)(2,1)S(1)}, u32[]{:S(2)}, u32[]{:S(2)}) collective-permute-start(bf16[1536,128]{1,0:T(8,128)(2,1)S(1)} %collective-permute-done.10.refs_8_.refs_16_.refs_19_.refs_15_), channel_id=1, source_target_pairs={{0,1},{1,0},{2,3},{3,2},{4,5},{5,4},{6,7},{7,6},{8,9},{9,8},{10,11... | collective-permute-start | bytes 1179656 | tf_op jit(solution)/shard_map/ppermute | solution.py:1349
  107.4 4.6 %collective-permute-start.20 = (f32[2,1024]{1,0:T(2,128)S(1)}, f32[2,1024]{1,0:T(2,128)S(1)}, u32[]{:S(2)}, u32[]{:S(2)}) collective-permute-start(f32[2,1024]{1,0:T(2,128)S(1)} %merge.8.refs_11_.refs_13_.refs_4_), channel_id=1, source_target_pairs={{0,16},{4,20},{8,24},{12,28},{16,0},{20,4},{24,8},{28,12},{1,17},{... | collective-permute-start | bytes 24584 | tf_op jit(solution)/shard_map/ppermute | solution.py:1359
  126.0 12.2 %collective-permute-start.25 = (bf16[2,4608,128]{2,1,0:T(8,128)(2,1)}, bf16[2,4608,128]{2,1,0:T(8,128)(2,1)S(1)}, u32[]{:S(2)}, u32[]{:S(2)}) collective-permute-start(bf16[2,4608,128]{2,1,0:T(8,128)(2,1)} %bitcast.109), channel_id=1, source_target_pairs={{0,1},{1,0},{2,3},{3,2},{4,5},{5,4},{6,7},{7,6},{8,9},{9,8},{10,11... | collective-permute-start | bytes 7077896 | tf_op jit(solution)/shard_map/ppermute | solution.py:1349
  133.5 4.6 %collective-permute-start.24 = (f32[2,512]{1,0:T(2,128)S(1)}, f32[2,512]{1,0:T(2,128)S(1)}, u32[]{:S(2)}, u32[]{:S(2)}) collective-permute-start(f32[2,512]{1,0:T(2,128)S(1)} %merge.9.refs_5_.refs_11_.refs_6_), channel_id=1, source_target_pairs={{0,16},{4,20},{8,24},{12,28},{16,0},{20,4},{24,8},{28,12},{1,17},{... | collective-permute-start | bytes 12296 | tf_op jit(solution)/shard_map/ppermute | solution.py:1359
  155.5 13.0 %collective-permute-start.29 = (f32[2,512]{1,0:T(2,128)S(1)}, f32[2,512]{1,0:T(2,128)S(1)}, u32[]{:S(2)}, u32[]{:S(2)}) collective-permute-start(f32[2,512]{1,0:T(2,128)S(1)} %merge.10.refs_3_.sa5.refs_4_), channel_id=1, source_target_pairs={{0,16},{4,20},{8,24},{12,28},{16,0},{20,4},{24,8},{28,12},{1,17},{... | collective-permute-start | bytes 12296 | tf_op jit(solution)/shard_map/ppermute | solution.py:1359
  173.8 4.6 %collective-permute-start.32 = (f32[2,4,512]{2,1,0:T(4,128)S(1)}, f32[2,4,512]{2,1,0:T(4,128)S(1)}, u32[]{:S(2)}, u32[]{:S(2)}) collective-permute-start(f32[2,4,512]{2,1,0:T(4,128)S(1)} %get-tuple-element.233.refs_0_), channel_id=1, source_target_pairs={{0,12},{4,8},{8,4},{12,0},{16,28},{20,24},{24,20},{28,16},{1,13},{... | collective-permute-start | bytes 49160 | tf_op jit(solution)/shard_map/ppermute | solution.py:1359
  179.1 4.7 %collective-permute-start.33 = (f32[2,4,512]{2,1,0:T(4,128)S(1)}, f32[2,4,512]{2,1,0:T(4,128)S(1)}, u32[]{:S(2)}, u32[]{:S(2)}) collective-permute-start(f32[2,4,512]{2,1,0:T(4,128)S(1)} %merge.11.refs_4_.refs_5_), channel_id=1, source_target_pairs={{0,16},{4,20},{8,24},{12,28},{16,0},{20,4},{24,8},{28,12},{1,17},{... | collective-permute-start | bytes 49160 | tf_op jit(solution)/shard_map/ppermute | solution.py:1359
  190.4 4.6 %collective-permute-start.36 = (f32[2,3,512]{2,1,0:T(4,128)S(1)}, f32[2,3,512]{2,1,0:T(4,128)S(1)}, u32[]{:S(2)}, u32[]{:S(2)}) collective-permute-start(f32[2,3,512]{2,1,0:T(4,128)S(1)} %get-tuple-element.238.refs_0_), channel_id=1, source_target_pairs={{0,12},{4,8},{8,4},{12,0},{16,28},{20,24},{24,20},{28,16},{1,13},{... | collective-permute-start | bytes 36872 | tf_op jit(solution)/shard_map/ppermute | solution.py:1359
  195.0 4.7 %collective-permute-start.37 = (f32[2,3,512]{2,1,0:T(4,128)S(1)}, f32[2,3,512]{2,1,0:T(4,128)S(1)}, u32[]{:S(2)}, u32[]{:S(2)}) collective-permute-start(f32[2,3,512]{2,1,0:T(4,128)S(1)} %add.21.refs_8_), channel_id=1, source_target_pairs={{0,16},{4,20},{8,24},{12,28},{16,0},{20,4},{24,8},{28,12},{1,17},{... | collective-permute-start | bytes 36872 | tf_op jit(solution)/shard_map/ppermute | solution.py:1359
  206.4 40.8 %collective-permute-start.47 = (bf16[74,8,1024]{2,1,0:T(8,128)(2,1)S(1)}, bf16[74,8,1024]{2,1,0:T(8,128)(2,1)}, u32[]{:S(2)}, u32[]{:S(2)}) collective-permute-start(bf16[74,8,1024]{2,1,0:T(8,128)(2,1)S(1)} %back_short.1.refs_15_), channel_id=1, source_target_pairs={{0,1},{1,0},{2,3},{3,2},{4,5},{5,4},{6,7},{7,6},{8,9},{9,8},{10,11... | collective-permute-start | bytes 3637256 | tf_op jit(solution)/shard_map/ppermute | solution.py:1349
  210.4 5.9 %collective-permute-start.39 = (f32[2,512]{1,0:T(2,128)S(1)}, f32[2,512]{1,0:T(2,128)S(1)}, u32[]{:S(2)}, u32[]{:S(2)}) collective-permute-start(f32[2,512]{1,0:T(2,128)S(1)} %get-tuple-element.241.refs_0_), channel_id=1, source_target_pairs={{0,4},{4,0},{8,12},{12,8},{16,20},{20,16},{24,28},{28,24},{1,5},{5... | collective-permute-start | bytes 12296 | tf_op jit(solution)/shard_map/ppermute | solution.py:1359
  211.2 5.1 %collective-permute-start.40 = (f32[2,512]{1,0:T(2,128)S(1)}, f32[2,512]{1,0:T(2,128)S(1)}, u32[]{:S(2)}, u32[]{:S(2)}) collective-permute-start(f32[2,512]{1,0:T(2,128)S(1)} %get-tuple-element.241.refs_0_), channel_id=1, source_target_pairs={{0,8},{4,12},{8,0},{12,4},{16,24},{20,28},{24,16},{28,20},{1,9},{5... | collective-permute-start | bytes 12296 | tf_op jit(solution)/shard_map/ppermute | solution.py:1359
  235.2 4.8 %collective-permute-start.45 = (f32[2,512]{1,0:T(2,128)S(1)}, f32[2,512]{1,0:T(2,128)S(1)}, u32[]{:S(2)}, u32[]{:S(2)}) collective-permute-start(f32[2,512]{1,0:T(2,128)S(1)} %get-tuple-element.252.refs_0_), channel_id=1, source_target_pairs={{0,12},{4,8},{8,4},{12,0},{16,28},{20,24},{24,20},{28,16},{1,13},{... | collective-permute-start | bytes 12296 | tf_op jit(solution)/shard_map/ppermute | solution.py:1359
  240.1 6.3 %collective-permute-start.46 = (f32[2,512]{1,0:T(2,128)S(1)}, f32[2,512]{1,0:T(2,128)S(1)}, u32[]{:S(2)}, u32[]{:S(2)}) collective-permute-start(f32[2,512]{1,0:T(2,128)S(1)} %add.23.refs_9_), channel_id=1, source_target_pairs={{0,16},{4,20},{8,24},{12,28},{16,0},{20,4},{24,8},{28,12},{1,17},{... | collective-permute-start | bytes 12296 | tf_op jit(solution)/shard_map/ppermute | solution.py:1359
  246.4 18.6 %collective-permute-start.51 = (bf16[2304,128]{1,0:T(8,128)(2,1)S(1)}, bf16[2304,128]{1,0:T(8,128)(2,1)S(1)}, u32[]{:S(2)}, u32[]{:S(2)}) collective-permute-start(bf16[2304,128]{1,0:T(8,128)(2,1)S(1)} %get-tuple-element.261), channel_id=1, source_target_pairs={{0,4},{4,0},{8,12},{12,8},{16,20},{20,16},{24,28},{28,24},{1,5},{5... | collective-permute-start | bytes 1769480 | tf_op jit(solution)/shard_map/ppermute | solution.py:1410
  265.0 4.6 %collective-permute-start.52 = (f32[2,1024]{1,0:T(2,128)S(1)}, f32[2,1024]{1,0:T(2,128)S(1)}, u32[]{:S(2)}, u32[]{:S(2)}) collective-permute-start(f32[2,1024]{1,0:T(2,128)S(1)} %add.24.refs_7_), channel_id=1, source_target_pairs={{0,16},{4,20},{8,24},{12,28},{16,0},{20,4},{24,8},{28,12},{1,17},{... | collective-permute-start | bytes 24584 | tf_op jit(solution)/shard_map/ppermute | solution.py:1359
  269.6 18.4 %collective-permute-start.56 = (bf16[1152,128]{1,0:T(8,128)(2,1)S(1)}, bf16[1152,128]{1,0:T(8,128)(2,1)S(1)}, u32[]{:S(2)}, u32[]{:S(2)}) collective-permute-start(bf16[1152,128]{1,0:T(8,128)(2,1)S(1)} %get-tuple-element.277), channel_id=1, source_target_pairs={{0,8},{4,12},{8,0},{12,4},{16,24},{20,28},{24,16},{28,20},{1,9},{5... | collective-permute-start | bytes 884744 | tf_op jit(solution)/shard_map/ppermute | solution.py:1410
  279.7 7.4 %collective-permute-start.53 = (f32[2,256]{1,0:T(2,128)S(1)}, f32[2,256]{1,0:T(2,128)S(1)}, u32[]{:S(2)}, u32[]{:S(2)}) collective-permute-start(f32[2,256]{1,0:T(2,128)S(1)} %get-tuple-element.268.refs_0_), channel_id=1, source_target_pairs={{0,4},{4,0},{8,12},{12,8},{16,20},{20,16},{24,28},{28,24},{1,5},{5... | collective-permute-start | bytes 6152 | tf_op jit(solution)/shard_map/ppermute | solution.py:1359
  280.6 6.6 %collective-permute-start.54 = (f32[2,256]{1,0:T(2,128)S(1)}, f32[2,256]{1,0:T(2,128)S(1)}, u32[]{:S(2)}, u32[]{:S(2)}) collective-permute-start(f32[2,256]{1,0:T(2,128)S(1)} %get-tuple-element.268.refs_0_), channel_id=1, source_target_pairs={{0,8},{4,12},{8,0},{12,4},{16,24},{20,28},{24,16},{28,20},{1,9},{5... | collective-permute-start | bytes 6152 | tf_op jit(solution)/shard_map/ppermute | solution.py:1359
  282.4 4.8 %collective-permute-start.55 = (f32[2,256]{1,0:T(2,128)S(1)}, f32[2,256]{1,0:T(2,128)S(1)}, u32[]{:S(2)}, u32[]{:S(2)}) collective-permute-start(f32[2,256]{1,0:T(2,128)S(1)} %get-tuple-element.268.refs_0_), channel_id=1, source_target_pairs={{0,12},{4,8},{8,4},{12,0},{16,28},{20,24},{24,20},{28,16},{1,13},{... | collective-permute-start | bytes 6152 | tf_op jit(solution)/shard_map/ppermute | solution.py:1359
  287.2 26.3 %collective-permute-start.62 = (bf16[768,128]{1,0:T(8,128)(2,1)S(1)}, bf16[768,128]{1,0:T(8,128)(2,1)S(1)}, u32[]{:S(2)}, u32[]{:S(2)}) collective-permute-start(bf16[768,128]{1,0:T(8,128)(2,1)S(1)} %get-tuple-element.286), channel_id=1, source_target_pairs={{0,4},{4,0},{8,12},{12,8},{16,20},{20,16},{24,28},{28,24},{1,5},{5... | collective-permute-start | bytes 589832 | tf_op jit(solution)/shard_map/ppermute | solution.py:1410
  288.1 4.6 %collective-permute-start.57 = (f32[2,256]{1,0:T(2,128)S(1)}, f32[2,256]{1,0:T(2,128)S(1)}, u32[]{:S(2)}, u32[]{:S(2)}) collective-permute-start(f32[2,256]{1,0:T(2,128)S(1)} %add.25.refs_7_), channel_id=1, source_target_pairs={{0,16},{4,20},{8,24},{12,28},{16,0},{20,4},{24,8},{28,12},{1,17},{... | collective-permute-start | bytes 6152 | tf_op jit(solution)/shard_map/ppermute | solution.py:1359
  292.7 20.8 %collective-permute-start.61 = (bf16[576,128]{1,0:T(8,128)(2,1)S(1)}, bf16[576,128]{1,0:T(8,128)(2,1)S(1)}, u32[]{:S(2)}, u32[]{:S(2)}) collective-permute-start(bf16[576,128]{1,0:T(8,128)(2,1)S(1)} %get-tuple-element.285), channel_id=1, source_target_pairs={{0,16},{4,20},{8,24},{12,28},{16,0},{20,4},{24,8},{28,12},{1,17},{... | collective-permute-start | bytes 442376 | tf_op jit(solution)/shard_map/ppermute | solution.py:1410
  313.5 9.6 %collective-permute-start.63 = (f32[2,256]{1,0:T(2,128)S(1)}, f32[2,256]{1,0:T(2,128)S(1)}, u32[]{:S(2)}, u32[]{:S(2)}) collective-permute-start(f32[2,256]{1,0:T(2,128)S(1)} %add.26.refs_7_), channel_id=1, source_target_pairs={{0,16},{4,20},{8,24},{12,28},{16,0},{20,4},{24,8},{28,12},{1,17},{... | collective-permute-start | bytes 6152 | tf_op jit(solution)/shard_map/ppermute | solution.py:1359
  323.1 12.4 %collective-permute-start.64 = (bf16[832,128]{1,0:T(8,128)(2,1)S(1)}, bf16[832,128]{1,0:T(8,128)(2,1)S(1)}, u32[]{:S(2)}, u32[]{:S(2)}) collective-permute-start(bf16[832,128]{1,0:T(8,128)(2,1)S(1)} %get-tuple-element.303), channel_id=1, source_target_pairs={{0,4},{4,0},{8,12},{12,8},{16,20},{20,16},{24,28},{28,24},{1,5},{5... | collective-permute-start | bytes 638984 | tf_op jit(solution)/shard_map/ppermute | solution.py:1410
  325.1 10.4 %collective-permute-start.66 = (bf16[576,128]{1,0:T(8,128)(2,1)S(1)}, bf16[576,128]{1,0:T(8,128)(2,1)S(1)}, u32[]{:S(2)}, u32[]{:S(2)}) collective-permute-start(bf16[576,128]{1,0:T(8,128)(2,1)S(1)} %stride_2s.1.refs_0_), channel_id=1, source_target_pairs={{0,16},{4,20},{8,24},{12,28},{16,0},{20,4},{24,8},{28,12},{1,17},{... | collective-permute-start | bytes 442376 | tf_op jit(solution)/shard_map/ppermute | solution.py:1410
  328.0 5.9 %collective-permute-start.65 = (bf16[384,128]{1,0:T(8,128)(2,1)S(1)}, bf16[384,128]{1,0:T(8,128)(2,1)S(1)}, u32[]{:S(2)}, u32[]{:S(2)}) collective-permute-start(bf16[384,128]{1,0:T(8,128)(2,1)S(1)} %get-tuple-element.304), channel_id=1, source_target_pairs={{0,8},{4,12},{8,0},{12,4},{16,24},{20,28},{24,16},{28,20},{1,9},{5... | collective-permute-start | bytes 294920 | tf_op jit(solution)/shard_map/ppermute | solution.py:1410
  336.1 10.0 %collective-permute-start.73 = (bf16[1152,128]{1,0:T(8,128)(2,1)S(1)}, bf16[1152,128]{1,0:T(8,128)(2,1)S(1)}, u32[]{:S(2)}, u32[]{:S(2)}) collective-permute-start(bf16[1152,128]{1,0:T(8,128)(2,1)S(1)} %bitcast.71), channel_id=1, source_target_pairs={{0,8},{4,12},{8,0},{12,4},{16,24},{20,28},{24,16},{28,20},{1,9},{5... | collective-permute-start | bytes 884744 | tf_op jit(solution)/shard_map/ppermute | solution.py:1410
  337.2 7.9 %collective-permute-start.75 = (bf16[192,128]{1,0:T(8,128)(2,1)S(1)}, bf16[192,128]{1,0:T(8,128)(2,1)S(1)}, u32[]{:S(2)}, u32[]{:S(2)}) collective-permute-start(bf16[192,128]{1,0:T(8,128)(2,1)S(1)} %get-tuple-element.321), channel_id=1, source_target_pairs={{0,16},{4,20},{8,24},{12,28},{16,0},{20,4},{24,8},{28,12},{1,17},{... | collective-permute-start | bytes 147464 | tf_op jit(solution)/shard_map/ppermute | solution.py:1410
  340.6 7.2 %collective-permute-start.67 = (bf16[208,128]{1,0:T(8,128)(2,1)S(1)}, bf16[208,128]{1,0:T(8,128)(2,1)S(1)}, u32[]{:S(2)}, u32[]{:S(2)}) collective-permute-start(bf16[208,128]{1,0:T(8,128)(2,1)S(1)} %get-tuple-element.311), channel_id=1, source_target_pairs={{0,8},{4,12},{8,0},{12,4},{16,24},{20,28},{24,16},{28,20},{1,9},{5... | collective-permute-start | bytes 159752 | tf_op jit(solution)/shard_map/ppermute | solution.py:1410
  340.7 7.2 %collective-permute-start.68 = (bf16[208,128]{1,0:T(8,128)(2,1)S(1)}, bf16[208,128]{1,0:T(8,128)(2,1)S(1)}, u32[]{:S(2)}, u32[]{:S(2)}) collective-permute-start(bf16[208,128]{1,0:T(8,128)(2,1)S(1)} %get-tuple-element.312), channel_id=1, source_target_pairs={{0,16},{4,20},{8,24},{12,28},{16,0},{20,4},{24,8},{28,12},{1,17},{... | collective-permute-start | bytes 159752 | tf_op jit(solution)/shard_map/ppermute | solution.py:1410
  342.4 5.9 %collective-permute-start.69 = (bf16[208,128]{1,0:T(8,128)(2,1)S(1)}, bf16[208,128]{1,0:T(8,128)(2,1)S(1)}, u32[]{:S(2)}, u32[]{:S(2)}) collective-permute-start(bf16[208,128]{1,0:T(8,128)(2,1)S(1)} %get-tuple-element.313), channel_id=1, source_target_pairs={{0,24},{4,28},{8,16},{12,20},{16,8},{20,12},{24,0},{28,4},{1,25},{... | collective-permute-start | bytes 159752 | tf_op jit(solution)/shard_map/ppermute | solution.py:1410
  345.1 7.8 %collective-permute-start.76 = (bf16[192,128]{1,0:T(8,128)(2,1)S(1)}, bf16[192,128]{1,0:T(8,128)(2,1)S(1)}, u32[]{:S(2)}, u32[]{:S(2)}) collective-permute-start(bf16[192,128]{1,0:T(8,128)(2,1)S(1)} %mid_2s.1.refs_0_), channel_id=1, source_target_pairs={{0,16},{4,20},{8,24},{12,28},{16,0},{20,4},{24,8},{28,12},{1,17},{... | collective-permute-start | bytes 147464 | tf_op jit(solution)/shard_map/ppermute | solution.py:1410
  346.7 16.3 %collective-permute-start.74 = (bf16[2304,128]{1,0:T(8,128)(2,1)S(1)}, bf16[2304,128]{1,0:T(8,128)(2,1)S(1)}, u32[]{:S(2)}, u32[]{:S(2)}) collective-permute-start(bf16[2304,128]{1,0:T(8,128)(2,1)S(1)} %bitcast.69), channel_id=1, source_target_pairs={{0,4},{4,0},{8,12},{12,8},{16,20},{20,16},{24,28},{28,24},{1,5},{5... | collective-permute-start | bytes 1769480 | tf_op jit(solution)/shard_map/ppermute | solution.py:1410
  348.4 5.1 %collective-permute-start.70 = (bf16[208,128]{1,0:T(8,128)(2,1)S(1)}, bf16[208,128]{1,0:T(8,128)(2,1)S(1)}, u32[]{:S(2)}, u32[]{:S(2)}) collective-permute-start(bf16[208,128]{1,0:T(8,128)(2,1)S(1)} %last_1s.1.refs_0_), channel_id=1, source_target_pairs={{0,8},{4,12},{8,0},{12,4},{16,24},{20,28},{24,16},{28,20},{1,9},{5... | collective-permute-start | bytes 159752 | tf_op jit(solution)/shard_map/ppermute | solution.py:1410
  348.5 5.3 %collective-permute-start.71 = (bf16[208,128]{1,0:T(8,128)(2,1)S(1)}, bf16[208,128]{1,0:T(8,128)(2,1)S(1)}, u32[]{:S(2)}, u32[]{:S(2)}) collective-permute-start(bf16[208,128]{1,0:T(8,128)(2,1)S(1)} %last_1s.1.refs_0_), channel_id=1, source_target_pairs={{0,16},{4,20},{8,24},{12,28},{16,0},{20,4},{24,8},{28,12},{1,17},{... | collective-permute-start | bytes 159752 | tf_op jit(solution)/shard_map/ppermute | solution.py:1410
  351.7 6.0 %collective-permute-start.72 = (bf16[208,128]{1,0:T(8,128)(2,1)S(1)}, bf16[208,128]{1,0:T(8,128)(2,1)S(1)}, u32[]{:S(2)}, u32[]{:S(2)}) collective-permute-start(bf16[208,128]{1,0:T(8,128)(2,1)S(1)} %last_1s.1.refs_0_), channel_id=1, source_target_pairs={{0,24},{4,28},{8,16},{12,20},{16,8},{20,12},{24,0},{28,4},{1,25},{... | collective-permute-start | bytes 159752 | tf_op jit(solution)/shard_map/ppermute | solution.py:1410
  353.4 6.1 %collective-permute-start.77 = (bf16[384,128]{1,0:T(8,128)(2,1)S(1)}, bf16[384,128]{1,0:T(8,128)(2,1)S(1)}, u32[]{:S(2)}, u32[]{:S(2)}) collective-permute-start(bf16[384,128]{1,0:T(8,128)(2,1)S(1)} %bitcast.79), channel_id=1, source_target_pairs={{0,8},{4,12},{8,0},{12,4},{16,24},{20,28},{24,16},{28,20},{1,9},{5... | collective-permute-start | bytes 294920 | tf_op jit(solution)/shard_map/ppermute | solution.py:1410
  358.2 10.1 %collective-permute-start.79 = (bf16[832,128]{1,0:T(8,128)(2,1)S(1)}, bf16[832,128]{1,0:T(8,128)(2,1)S(1)}, u32[]{:S(2)}, u32[]{:S(2)}) collective-permute-start(bf16[832,128]{1,0:T(8,128)(2,1)S(1)} %bitcast.73), channel_id=1, source_target_pairs={{0,4},{4,0},{8,12},{12,8},{16,20},{20,16},{24,28},{28,24},{1,5},{5... | collective-permute-start | bytes 638984 | tf_op jit(solution)/shard_map/ppermute | solution.py:1410
  360.1 8.3 %collective-permute-start.78 = (bf16[768,128]{1,0:T(8,128)(2,1)S(1)}, bf16[768,128]{1,0:T(8,128)(2,1)S(1)}, u32[]{:S(2)}, u32[]{:S(2)}) collective-permute-start(bf16[768,128]{1,0:T(8,128)(2,1)S(1)} %bitcast.75), channel_id=1, source_target_pairs={{0,4},{4,0},{8,12},{12,8},{16,20},{20,16},{24,28},{28,24},{1,5},{5... | collective-permute-start | bytes 589832 | tf_op jit(solution)/shard_map/ppermute | solution.py:1410
  (70 other events, 444.6 us)
Sparse Core Ops, SparseCore 0:
  47.8 46.0 all-gather.4
  95.4 58.9 all-gather.6
  217.5 98.4 all-reduce.4

commit v3 on v2

--- a/solution.py
+++ b/solution.py
@@ -1814,6 +1814,7 @@
             out("rows", (geo.rows, 128), BF16),
         ],
         [pltpu.VMEM(wb_shape, BF16), pltpu.VMEM(ws_shape, BF16)],
+        ahead=8,
     )
     came = stride_train.received + mid_train.received
     stride_train.advance()

time: 383 us -> 382 us (level)
  no operation moved by 1% of the time
where the time goes in v3:
time: 382 us; the launch traced here: 377 us
  Pallas kernels  157 us (41%)
  starting transfers between devices  96.3 us (25%)
  waiting for transfers between devices  88.3 us (23%)
  local copies, waits for them, and re-layouts  19 us (5%)
  between operations  14.8 us (4%)
    pallas_call x53, Pallas kernels, call(): pl.pallas_call(body, out_shape=out_shapes, in_specs=specs, out_specs=out_...  157 us
    ppermute x48, starting transfers between devices, peers(): out.append(lax.ppermute(v, 'img', [(i, i ^ m << shift) for i in range(ni)]))  62.7 us
    ppermute x48, waiting for transfers between devices, peers(): out.append(lax.ppermute(v, 'img', [(i, i ^ m << shift) for i in range(ni)]))  54.7 us
    ppermute x20, starting transfers between devices, to_peers(): out.append(lax.ppermute(parts[m if len(parts) > 1 else 0], 'img', perm))  27 us
    ppermute x12, waiting for transfers between devices, over_ch(): return lax.ppermute(v, 'ch', [(i, i ^ k) for i in range(nc)])  26.7 us
    unnamed x77, local copies, waits for them, and re-layouts  16.1 us
  transfers between devices with their start and end apart: 83, of which 48 were waited for; matrix products, arithmetic and copies ran while one was open for 2% of the time, Pallas kernels for 38%

profile of v3, /device:TPU:0, one launch (start us, length us, event | category | flops | bytes accessed | tf_op | source)
XLA Modules:
  0.0 377.4 jit_solution(15233827485478830598)
XLA Ops:
  7.8 2.6 collective-permute-start.1
  22.5 6.9 %collective-permute-done.1.refs_4_.refs_5_.refs_6_ = bf16[1568,256]{1,0:T(8,128)(2,1)} collective-permute-done((bf16[1568,256]{1,0:T(8,128)(2,1)}, bf16[1568,256]{1,0:T(8,128)(2,1)}, u32[]{:S(2)}, u32[]{:S(2)}) %collective-permute-start.1) | collective-permute-done | bytes 802848 | tf_op jit(solution)/shard_map/ppermute | solution.py:1349
  32.0 15.6 %collective-permute-done.3.refs_8_.refs_12_.p2.refs_9_.refs_15_.refs_10_ = bf16[1696,256]{1,0:T(8,128)(2,1)S(1)} collective-permute-done((bf16[1696,256]{1,0:T(8,128)(2,1)S(1)}, bf16[1696,256]{1,0:T(8,128)(2,1)S(1)}, u32[]{:S(2)}, u32[]{:S(2)}) %collective-permute-start.3) | collective-permute-done | bytes 868384 | tf_op jit(solution)/shard_map/ppermute | solution.py:1349
  53.1 6.7 %reduce.1 = (f32[296,8,256]{2,1,0:T(8,128)S(1)}, f32[2,256]{1,0:T(2,128)S(1)}) custom-call(s32[4]{0:T(128)S(1)} %get-tuple-element.184.refs_0_.me, f32[3]{0:T(128)S(1)} %get-tuple-element.186.refs_1_.refs_2_.refs_14_, bf16[1568,256]{1,0:T(8,128)(2,1)} %bitcast.105, bf16[1568,256]{1,0:T(8,128)(2,1)} %copy-done.21, ...), custom_call_target="tpu_custom_call" | custom-call | tf_op jit(solution)/shard_map/reduce/pallas_call | solution.py:316
  66.7 2.5 collective-permute-done.8.refs_3_
  69.9 2.7 collective-permute-start.9
  74.4 6.4 %mix.1 = (f32[296,8,256]{2,1,0:T(8,128)S(1)}, bf16[1792,768]{1,0:T(8,128)(2,1)}, bf16[960,768]{1,0:T(8,128)(2,1)}, f32[2,256]{1,0:T(2,128)S(1)}, bf16[2368,128]{1,0:T(8,128)(2,1)}, /*index=5*/f32[296,8,256]{2,1,0:T(8,128)}) custom-call(s32[4]{0:T(128)S(1)} %get-tuple-element.184.refs_0_.me, f32[3]{0:T(128)S(1)} %get-tuple-element.186.refs_1_.refs_2_.refs_14_, ...), custom_call_target="tpu_custom_call" | custom-call | tf_op jit(solution)/shard_map/mix/pallas_call | solution.py:316
  85.3 2.5 collective-permute-done.13.refs_3_
  88.5 2.7 collective-permute-start.14
  93.8 6.7 %expand.1 = (f32[296,8,1024]{2,1,0:T(8,128)S(1)}, bf16[2368,256]{1,0:T(8,128)(2,1)}, f32[2,1024]{1,0:T(2,128)S(1)}, f32[296,8,256]{2,1,0:T(8,128)}) custom-call(s32[4]{0:T(128)S(1)} %get-tuple-element.184.refs_0_.me, f32[3]{0:T(128)S(1)} %get-tuple-element.186.refs_1_.refs_2_.refs_14_, f32[296,8,256]{2,1,0:T(8,128)S(1)} %get-tuple-element.203.refs_2_, ...), custom_call_target="tpu_custom_call" | custom-call | tf_op jit(solution)/shard_map/expand/pallas_call | solution.py:316
  104.6 2.1 collective-permute-done.19.refs_3_
  107.4 2.6 collective-permute-start.20
  112.0 13.9 %narrow.1 = (f32[2,2,7,7,8,512]{5,4,3,2,1,0:T(8,128)}, f32[2,2,5,5,8,512]{5,4,3,2,1,0:T(8,128)}, bf16[2368,1024]{1,0:T(8,128)(2,1)}, bf16[592,1024]{1,0:T(8,128)...) custom-call(s32[4]{0:T(128)S(1)} %get-tuple-element.184.refs_0_.me, ...), custom_call_target="tpu_custom_call" | custom-call | tf_op jit(solution)/shard_map/narrow/pallas_call | solution.py:316
  130.4 2.5 collective-permute-done.23.refs_3_
  133.5 2.7 collective-permute-start.24
  139.5 9.1 %stride.1 = (f32[74,8,512]{2,1,0:T(8,128)S(1)}, bf16[9,592,512]{2,1,0:T(8,128)(2,1)}, f32[2,512]{1,0:T(2,128)S(1)}) custom-call(s32[4]{0:T(128)S(1)} %get-tuple-element.184.refs_0_.me, f32[3]{0:T(128)S(1)} %get-tuple-element.185.refs_1_.nf, f32[3]{0:T(128)S(1)} %get-tuple-element.186.refs_1_.refs_2_.refs_14_, ...), custom_call_target="tpu_custom_call" | custom-call | tf_op jit(solution)/shard_map/stride/pallas_call | solution.py:316
  152.8 2.1 collective-permute-done.28.refs_3_
  155.5 2.6 collective-permute-start.29
  158.2 6.5 %dev_products.1 = bf16[80,1024]{1,0:T(8,128)(2,1)} custom-call(s32[4]{0:T(128)S(1)} %get-tuple-element.184.refs_0_.me, bf16[2368,128]{1,0:T(8,128)(2,1)} %get-tuple-element.225.refs_1_, bf16[1568,256]{1,0:T(8,128)(2,1)} %bitcast.107, bf16[1568,256]{1,0:T(8,128)(2,1)} %copy-done.21, bf16[1568,256]{1,0:T(8,128)(2,1)} %collective-permute-done.1.refs_4_.refs_5_.refs_6_, ...), custom_call_target="tpu_custom_call" | custom-call | tf_op jit(solution)/shard_map/dev_products/pallas_call | solution.py:316
  164.7 3.8 %short.1 = (f32[2,74,8,512]{3,2,1,0:T(8,128)S(1)}, f32[2,2,512]{2,1,0:T(2,128)S(1)}) custom-call(s32[4]{0:T(128)S(1)} %get-tuple-element.184.refs_0_.me, f32[3]{0:T(128)S(1)} %get-tuple-element.185.refs_1_.nf, bf16[592,1024]{1,0:T(8,128)(2,1)S(1)} %get-tuple-element.229.refs_2_.mids, bf16[2,2144,512]{2,1,0:T(8,128)(2,1)} %bitcast.91, ...), custom_call_target="tpu_custom_call" | custom-call | tf_op jit(solution)/shard_map/short/pallas_call | solution.py:316
  168.5 2.8 widen.1
  176.0 2.5 collective-permute-done.32.refs_3_
  179.4 4.4 %collective-permute-done.33.refs_5_.refs_6_ = f32[2,4,512]{2,1,0:T(4,128)S(1)} collective-permute-done((f32[2,4,512]{2,1,0:T(4,128)S(1)}, f32[2,4,512]{2,1,0:T(4,128)S(1)}, u32[]{:S(2)}, u32[]{:S(2)}) %collective-permute-start.33) | collective-permute-done | bytes 16416 | tf_op jit(solution)/shard_map/ppermute | solution.py:1359
  183.8 4.9 %total.1 = (f32[49,8,512]{2,1,0:T(8,128)}, f32[25,8,512]{2,1,0:T(8,128)}, f32[2,74,8,512]{3,2,1,0:T(8,128)S(1)}, f32[2,3,512]{2,1,0:T(4,128)S(1)}) custom-call(s32[4]{0:T(128)S(1)} %get-tuple-element.184.refs_0_.me, f32[3]{0:T(128)S(1)} %get-tuple-element.185.refs_1_.nf, f32[2,74,8,512]{3,2,1,0:T(8,128)S(1)} %get-tuple-element.231.refs_2_.refs_3_, ...), custom_call_target="tpu_custom_call" | custom-call | tf_op jit(solution)/shard_map/total/pallas_call | solution.py:316
  195.5 4.3 %collective-permute-done.37.refs_9_ = f32[2,3,512]{2,1,0:T(4,128)S(1)} collective-permute-done((f32[2,3,512]{2,1,0:T(4,128)S(1)}, f32[2,3,512]{2,1,0:T(4,128)S(1)}, u32[]{:S(2)}, u32[]{:S(2)}) %collective-permute-start.37) | collective-permute-done | bytes 12320 | tf_op jit(solution)/shard_map/ppermute | solution.py:1359
  199.7 3.0 back_wide.1
  202.8 3.6 back_short.1.refs_15_
  206.9 2.5 back_act5.1
  213.9 2.4 dw_wide.1
  217.8 4.2 %collective-permute-done.42.refs_8_ = f32[2,512]{1,0:T(2,128)S(1)} collective-permute-done((f32[2,512]{1,0:T(2,128)S(1)}, f32[2,512]{1,0:T(2,128)S(1)}, u32[]{:S(2)}, u32[]{:S(2)}) %collective-permute-start.42) | collective-permute-done | bytes 4128 | tf_op jit(solution)/shard_map/ppermute | solution.py:1359
  223.3 10.2 %back_stride.1 = (f32[2,2,7,7,8,512]{5,4,3,2,1,0:T(8,128)S(1)}, f32[2,2,5,5,8,512]{5,4,3,2,1,0:T(8,128)S(1)}, bf16[592,512]{1,0:T(8,128)(2,1)S(1)}, f32[2,512]{1,0:T(2,128)S(1)}, f32[2,512]{1,0:T(2,128)S(1)}) custom-call(s32[4]{0:T(128)S(1)} %get-tuple-element.184.refs_0_.me, f32[3]{0:T(128)S(1)} %get-tuple-element.185.refs_1_.nf, ...), custom_call_target="tpu_custom_call" | custom-call | tf_op jit(solution)/shard_map/back_stride/pallas_call | solution.py:316
  240.4 6.0 %dw_stride.1 = (bf16[2304,128]{1,0:T(8,128)(2,1)S(1)}, bf16[2304,128]{1,0:T(8,128)(2,1)S(1)}) custom-call(s32[4]{0:T(128)S(1)} %get-tuple-element.184.refs_0_.me, bf16[9,592,512]{2,1,0:T(8,128)(2,1)} %get-tuple-element.253.refs_1_, bf16[592,512]{1,0:T(8,128)(2,1)S(1)} %get-tuple-element.254.refs_2_), custom_call_target="tpu_custom_call" | custom-call | tf_op jit(solution)/shard_map/dw_stride/pallas_call | solution.py:316
  247.2 11.1 %back_narrow.1 = (bf16[2368,1024]{1,0:T(8,128)(2,1)S(1)}, bf16[2368,512]{1,0:T(8,128)(2,1)}, f32[2,1024]{1,0:T(2,128)S(1)}, f32[2,512]{1,0:T(2,128)S(1)}) custom-call(s32[4]{0:T(128)S(1)} %get-tuple-element.184.refs_0_.me, f32[3]{0:T(128)S(1)} %get-tuple-element.186.refs_1_.refs_2_.refs_14_, f32[2,2,7,7,8,512]{5,4,3,2,1,0:T(8,128)S(1)} %get-tuple-element.250.refs_2_, ...), custom_call_target="tpu_custom_call" | custom-call | tf_op jit(solution)/shard_map/back_narrow/pallas_call | solution.py:316
  265.0 2.7 collective-permute-start.52
  271.0 8.7 %back_expand.1 = (f32[296,8,256]{2,1,0:T(8,128)S(1)}, bf16[2368,256]{1,0:T(8,128)(2,1)}, bf16[2368,256]{1,0:T(8,128)(2,1)}, f32[2,256]{1,0:T(2,128)S(1)}, f32[2,1024]{1,0:T(2,128)S(1)}) custom-call(s32[4]{0:T(128)S(1)} %get-tuple-element.184.refs_0_.me, f32[3]{0:T(128)S(1)} %get-tuple-element.186.refs_1_.refs_2_.refs_14_, ...), custom_call_target="tpu_custom_call" | custom-call | tf_op jit(solution)/shard_map/back_expand/pallas_call | solution.py:316
  284.6 2.6 dw_mid.1
  288.1 2.5 collective-permute-start.57
  292.7 2.4 collective-permute-start.61
  295.1 10.4 %back_mix.1 = (f32[296,8,256]{2,1,0:T(8,128)}, bf16[2368,256]{1,0:T(8,128)(2,1)}, f32[2,256]{1,0:T(2,128)S(1)}, f32[2,256]{1,0:T(2,128)S(1)}, bf16[2368,128]{1,0:T(8,128)(2,1)}) custom-call(s32[4]{0:T(128)S(1)} %get-tuple-element.184.refs_0_.me, f32[3]{0:T(128)S(1)} %get-tuple-element.186.refs_1_.refs_2_.refs_14_, ...), custom_call_target="tpu_custom_call" | custom-call | tf_op jit(solution)/shard_map/back_mix/pallas_call | solution.py:316
  313.2 8.8 %dw_last.1 = (bf16[832,128]{1,0:T(8,128)(2,1)S(1)}, bf16[832,128]{1,0:T(8,128)(2,1)S(1)}) custom-call(s32[4]{0:T(128)S(1)} %get-tuple-element.184.refs_0_.me, bf16[1792,768]{1,0:T(8,128)(2,1)} %get-tuple-element.288.refs_1_, bf16[960,768]{1,0:T(8,128)(2,1)} %get-tuple-element.289.refs_2_, bf16[2368,256]{1,0:T(8,128)(2,1)} %get-tuple-element.290.refs_3_, ...), custom_call_target="tpu_custom_call" | custom-call | tf_op jit(solution)/shard_map/dw_last/pallas_call | solution.py:316
  322.1 2.2 collective-permute-start.64
  324.2 2.9 collective-permute-start.66
  327.1 5.9 %back_reduce.1 = (f32[196,8,256]{2,1,0:T(8,128)}, f32[100,8,256]{2,1,0:T(8,128)}, f32[2,256]{1,0:T(2,128)S(1)}, f32[3,256]{1,0:T(4,128)S(1)}) custom-call(s32[4]{0:T(128)S(1)} %get-tuple-element.184.refs_0_.me, f32[3]{0:T(128)S(1)} %get-tuple-element.186.refs_1_.refs_2_.refs_14_, f32[296,8,256]{2,1,0:T(8,128)} %get-tuple-element.283.refs_2_, ...), custom_call_target="tpu_custom_call" | custom-call | tf_op jit(solution)/shard_map/back_reduce/pallas_call | solution.py:316
  336.3 2.6 collective-permute-start.75
  341.4 2.7 collective-permute-start.69
  347.4 3.2 collective-permute-start.71
  352.8 3.9 %collective-permute-done.72.refs_3_ = bf16[208,128]{1,0:T(8,128)(2,1)S(1)} collective-permute-done((bf16[208,128]{1,0:T(8,128)(2,1)S(1)}, bf16[208,128]{1,0:T(8,128)(2,1)S(1)}, u32[]{:S(2)}, u32[]{:S(2)}) %collective-permute-start.72) | collective-permute-done | bytes 53280 | tf_op jit(solution)/shard_map/ppermute | solution.py:1410
  362.9 4.4 %out_first.1 = (f32[2,256,512]{2,1,0:T(8,128)}, f32[4,256,512]{2,1,0:T(8,128)}, f32[2,2304,128]{2,1,0:T(8,128)}) custom-call(s32[4]{0:T(128)S(1)} %get-tuple-element.184.refs_0_.me, bf16[2,256,512]{2,1,0:T(8,128)(2,1)} %bitcast.115, bf16[4,256,512]{2,1,0:T(8,128)(2,1)} %bitcast.113, bf16[1,2304,128]{2,1,0:T(8,128)(2,1)} %bitcast.70, ...), custom_call_target="tpu_custom_call" | custom-call | tf_op jit(solution)/shard_map/out_first/pallas_call | solution.py:316
  (261 shorter events, 131.4 us)
Async XLA Ops:
  7.2 118.8 %all-gather.5.cloned.1.call-start = ((), (), s32[]{:S(2)}) async-start(), calls=%async_computation | async-start | bytes 3538944 | tf_op jit(solution)/shard_map/all_gather | solution.py:1537
  7.2 11.7 %collective-permute-start = (bf16[1568,256]{1,0:T(8,128)(2,1)}, bf16[1568,256]{1,0:T(8,128)(2,1)S(1)}, u32[]{:S(2)}, u32[]{:S(2)}) collective-permute-start(bf16[1568,256]{1,0:T(8,128)(2,1)} %bitcast.103), channel_id=1, source_target_pairs={{0,1},{1,0},{2,3},{3,2},{4,5},{5,4},{6,7},{7,6},{8,9},{9,8},{10,11... | collective-permute-start | bytes 2408456 | tf_op jit(solution)/shard_map/ppermute | solution.py:1349
  7.8 21.6 %collective-permute-start.1 = (bf16[1568,256]{1,0:T(8,128)(2,1)}, bf16[1568,256]{1,0:T(8,128)(2,1)}, u32[]{:S(2)}, u32[]{:S(2)}) collective-permute-start(bf16[1568,256]{1,0:T(8,128)(2,1)} %bitcast.104), channel_id=1, source_target_pairs={{0,2},{1,3},{2,0},{3,1},{4,6},{5,7},{6,4},{7,5},{8,10},{9,11},{10,... | collective-permute-start | bytes 2408456 | tf_op jit(solution)/shard_map/ppermute | solution.py:1349
  21.3 26.3 %collective-permute-start.3 = (bf16[1696,256]{1,0:T(8,128)(2,1)S(1)}, bf16[1696,256]{1,0:T(8,128)(2,1)S(1)}, u32[]{:S(2)}, u32[]{:S(2)}) collective-permute-start(bf16[1696,256]{1,0:T(8,128)(2,1)S(1)} %constant_dynamic-update-slice_fusion.refs_6_.refs_10_.p0.refs_7_.refs_13_.refs_8_), channel_id=1, source_target_pairs={{0,2},{1,3},{2,0},{3,1},{4,6},{5,7},{6,4},{7,5},{8,10},{9,11},{10,... | collective-permute-start | bytes 2605064 | tf_op jit(solution)/shard_map/ppermute | solution.py:1349
  47.7 117.0 %all-gather.7.cloned.1.call-start = ((), (), s32[]{:S(2)}) async-start(), calls=%async_computation.1 | async-start | bytes 6586368 | tf_op jit(solution)/shard_map/all_gather | solution.py:1538
  48.4 286.0 %all-reduce.5.cloned.1.call-start = ((), (), s32[]{:S(2)}) async-start(), calls=%async_computation.2 | async-start | bytes 3473408 | tf_op jit(solution)/shard_map/psum | solution.py:1839
  59.8 21.0 %collective-permute-start.10 = (bf16[1536,128]{1,0:T(8,128)(2,1)S(1)}, bf16[1536,128]{1,0:T(8,128)(2,1)S(1)}, u32[]{:S(2)}, u32[]{:S(2)}) collective-permute-start(bf16[1536,128]{1,0:T(8,128)(2,1)S(1)} %pad_maximum_fusion.refs_6_.refs_14_.refs_17_.refs_13_), channel_id=1, source_target_pairs={{0,2},{1,3},{2,0},{3,1},{4,6},{5,7},{6,4},{7,5},{8,10},{9,11},{10,... | collective-permute-start | bytes 1179656 | tf_op jit(solution)/shard_map/ppermute | solution.py:1349
  72.6 18.6 %collective-permute-start.15 = (bf16[1536,128]{1,0:T(8,128)(2,1)S(1)}, bf16[1536,128]{1,0:T(8,128)(2,1)S(1)}, u32[]{:S(2)}, u32[]{:S(2)}) collective-permute-start(bf16[1536,128]{1,0:T(8,128)(2,1)S(1)} %pad_maximum_fusion.refs_6_.refs_14_.refs_17_.refs_13_), channel_id=1, source_target_pairs={{0,1},{1,0},{2,3},{3,2},{4,5},{5,4},{6,7},{7,6},{8,9},{9,8},{10,11... | collective-permute-start | bytes 1179656 | tf_op jit(solution)/shard_map/ppermute | solution.py:1349
  80.8 12.2 %collective-permute-start.16 = (bf16[1536,128]{1,0:T(8,128)(2,1)S(1)}, bf16[1536,128]{1,0:T(8,128)(2,1)S(1)}, u32[]{:S(2)}, u32[]{:S(2)}) collective-permute-start(bf16[1536,128]{1,0:T(8,128)(2,1)S(1)} %collective-permute-done.10.refs_8_.refs_16_.refs_19_.refs_15_), channel_id=1, source_target_pairs={{0,1},{1,0},{2,3},{3,2},{4,5},{5,4},{6,7},{7,6},{8,9},{9,8},{10,11... | collective-permute-start | bytes 1179656 | tf_op jit(solution)/shard_map/ppermute | solution.py:1349
  107.4 4.6 %collective-permute-start.20 = (f32[2,1024]{1,0:T(2,128)S(1)}, f32[2,1024]{1,0:T(2,128)S(1)}, u32[]{:S(2)}, u32[]{:S(2)}) collective-permute-start(f32[2,1024]{1,0:T(2,128)S(1)} %merge.8.refs_11_.refs_13_.refs_4_), channel_id=1, source_target_pairs={{0,16},{4,20},{8,24},{12,28},{16,0},{20,4},{24,8},{28,12},{1,17},{... | collective-permute-start | bytes 24584 | tf_op jit(solution)/shard_map/ppermute | solution.py:1359
  126.0 12.2 %collective-permute-start.25 = (bf16[2,4608,128]{2,1,0:T(8,128)(2,1)}, bf16[2,4608,128]{2,1,0:T(8,128)(2,1)S(1)}, u32[]{:S(2)}, u32[]{:S(2)}) collective-permute-start(bf16[2,4608,128]{2,1,0:T(8,128)(2,1)} %bitcast.109), channel_id=1, source_target_pairs={{0,1},{1,0},{2,3},{3,2},{4,5},{5,4},{6,7},{7,6},{8,9},{9,8},{10,11... | collective-permute-start | bytes 7077896 | tf_op jit(solution)/shard_map/ppermute | solution.py:1349
  133.5 4.6 %collective-permute-start.24 = (f32[2,512]{1,0:T(2,128)S(1)}, f32[2,512]{1,0:T(2,128)S(1)}, u32[]{:S(2)}, u32[]{:S(2)}) collective-permute-start(f32[2,512]{1,0:T(2,128)S(1)} %merge.9.refs_5_.refs_11_.refs_6_), channel_id=1, source_target_pairs={{0,16},{4,20},{8,24},{12,28},{16,0},{20,4},{24,8},{28,12},{1,17},{... | collective-permute-start | bytes 12296 | tf_op jit(solution)/shard_map/ppermute | solution.py:1359
  155.5 13.0 %collective-permute-start.29 = (f32[2,512]{1,0:T(2,128)S(1)}, f32[2,512]{1,0:T(2,128)S(1)}, u32[]{:S(2)}, u32[]{:S(2)}) collective-permute-start(f32[2,512]{1,0:T(2,128)S(1)} %merge.10.refs_3_.sa5.refs_4_), channel_id=1, source_target_pairs={{0,16},{4,20},{8,24},{12,28},{16,0},{20,4},{24,8},{28,12},{1,17},{... | collective-permute-start | bytes 12296 | tf_op jit(solution)/shard_map/ppermute | solution.py:1359
  173.8 4.6 %collective-permute-start.32 = (f32[2,4,512]{2,1,0:T(4,128)S(1)}, f32[2,4,512]{2,1,0:T(4,128)S(1)}, u32[]{:S(2)}, u32[]{:S(2)}) collective-permute-start(f32[2,4,512]{2,1,0:T(4,128)S(1)} %get-tuple-element.233.refs_0_), channel_id=1, source_target_pairs={{0,12},{4,8},{8,4},{12,0},{16,28},{20,24},{24,20},{28,16},{1,13},{... | collective-permute-start | bytes 49160 | tf_op jit(solution)/shard_map/ppermute | solution.py:1359
  179.1 4.7 %collective-permute-start.33 = (f32[2,4,512]{2,1,0:T(4,128)S(1)}, f32[2,4,512]{2,1,0:T(4,128)S(1)}, u32[]{:S(2)}, u32[]{:S(2)}) collective-permute-start(f32[2,4,512]{2,1,0:T(4,128)S(1)} %merge.11.refs_4_.refs_5_), channel_id=1, source_target_pairs={{0,16},{4,20},{8,24},{12,28},{16,0},{20,4},{24,8},{28,12},{1,17},{... | collective-permute-start | bytes 49160 | tf_op jit(solution)/shard_map/ppermute | solution.py:1359
  190.4 4.6 %collective-permute-start.36 = (f32[2,3,512]{2,1,0:T(4,128)S(1)}, f32[2,3,512]{2,1,0:T(4,128)S(1)}, u32[]{:S(2)}, u32[]{:S(2)}) collective-permute-start(f32[2,3,512]{2,1,0:T(4,128)S(1)} %get-tuple-element.238.refs_0_), channel_id=1, source_target_pairs={{0,12},{4,8},{8,4},{12,0},{16,28},{20,24},{24,20},{28,16},{1,13},{... | collective-permute-start | bytes 36872 | tf_op jit(solution)/shard_map/ppermute | solution.py:1359
  195.0 4.7 %collective-permute-start.37 = (f32[2,3,512]{2,1,0:T(4,128)S(1)}, f32[2,3,512]{2,1,0:T(4,128)S(1)}, u32[]{:S(2)}, u32[]{:S(2)}) collective-permute-start(f32[2,3,512]{2,1,0:T(4,128)S(1)} %add.21.refs_8_), channel_id=1, source_target_pairs={{0,16},{4,20},{8,24},{12,28},{16,0},{20,4},{24,8},{28,12},{1,17},{... | collective-permute-start | bytes 36872 | tf_op jit(solution)/shard_map/ppermute | solution.py:1359
  206.4 40.8 %collective-permute-start.47 = (bf16[74,8,1024]{2,1,0:T(8,128)(2,1)S(1)}, bf16[74,8,1024]{2,1,0:T(8,128)(2,1)}, u32[]{:S(2)}, u32[]{:S(2)}) collective-permute-start(bf16[74,8,1024]{2,1,0:T(8,128)(2,1)S(1)} %back_short.1.refs_15_), channel_id=1, source_target_pairs={{0,1},{1,0},{2,3},{3,2},{4,5},{5,4},{6,7},{7,6},{8,9},{9,8},{10,11... | collective-permute-start | bytes 3637256 | tf_op jit(solution)/shard_map/ppermute | solution.py:1349
  210.4 5.9 %collective-permute-start.39 = (f32[2,512]{1,0:T(2,128)S(1)}, f32[2,512]{1,0:T(2,128)S(1)}, u32[]{:S(2)}, u32[]{:S(2)}) collective-permute-start(f32[2,512]{1,0:T(2,128)S(1)} %get-tuple-element.241.refs_0_), channel_id=1, source_target_pairs={{0,4},{4,0},{8,12},{12,8},{16,20},{20,16},{24,28},{28,24},{1,5},{5... | collective-permute-start | bytes 12296 | tf_op jit(solution)/shard_map/ppermute | solution.py:1359
  211.2 5.1 %collective-permute-start.40 = (f32[2,512]{1,0:T(2,128)S(1)}, f32[2,512]{1,0:T(2,128)S(1)}, u32[]{:S(2)}, u32[]{:S(2)}) collective-permute-start(f32[2,512]{1,0:T(2,128)S(1)} %get-tuple-element.241.refs_0_), channel_id=1, source_target_pairs={{0,8},{4,12},{8,0},{12,4},{16,24},{20,28},{24,16},{28,20},{1,9},{5... | collective-permute-start | bytes 12296 | tf_op jit(solution)/shard_map/ppermute | solution.py:1359
  235.2 4.8 %collective-permute-start.45 = (f32[2,512]{1,0:T(2,128)S(1)}, f32[2,512]{1,0:T(2,128)S(1)}, u32[]{:S(2)}, u32[]{:S(2)}) collective-permute-start(f32[2,512]{1,0:T(2,128)S(1)} %get-tuple-element.252.refs_0_), channel_id=1, source_target_pairs={{0,12},{4,8},{8,4},{12,0},{16,28},{20,24},{24,20},{28,16},{1,13},{... | collective-permute-start | bytes 12296 | tf_op jit(solution)/shard_map/ppermute | solution.py:1359
  240.1 6.3 %collective-permute-start.46 = (f32[2,512]{1,0:T(2,128)S(1)}, f32[2,512]{1,0:T(2,128)S(1)}, u32[]{:S(2)}, u32[]{:S(2)}) collective-permute-start(f32[2,512]{1,0:T(2,128)S(1)} %add.23.refs_9_), channel_id=1, source_target_pairs={{0,16},{4,20},{8,24},{12,28},{16,0},{20,4},{24,8},{28,12},{1,17},{... | collective-permute-start | bytes 12296 | tf_op jit(solution)/shard_map/ppermute | solution.py:1359
  246.4 18.6 %collective-permute-start.51 = (bf16[2304,128]{1,0:T(8,128)(2,1)S(1)}, bf16[2304,128]{1,0:T(8,128)(2,1)S(1)}, u32[]{:S(2)}, u32[]{:S(2)}) collective-permute-start(bf16[2304,128]{1,0:T(8,128)(2,1)S(1)} %get-tuple-element.261), channel_id=1, source_target_pairs={{0,4},{4,0},{8,12},{12,8},{16,20},{20,16},{24,28},{28,24},{1,5},{5... | collective-permute-start | bytes 1769480 | tf_op jit(solution)/shard_map/ppermute | solution.py:1410
  265.0 4.6 %collective-permute-start.52 = (f32[2,1024]{1,0:T(2,128)S(1)}, f32[2,1024]{1,0:T(2,128)S(1)}, u32[]{:S(2)}, u32[]{:S(2)}) collective-permute-start(f32[2,1024]{1,0:T(2,128)S(1)} %add.24.refs_7_), channel_id=1, source_target_pairs={{0,16},{4,20},{8,24},{12,28},{16,0},{20,4},{24,8},{28,12},{1,17},{... | collective-permute-start | bytes 24584 | tf_op jit(solution)/shard_map/ppermute | solution.py:1359
  269.6 18.4 %collective-permute-start.56 = (bf16[1152,128]{1,0:T(8,128)(2,1)S(1)}, bf16[1152,128]{1,0:T(8,128)(2,1)S(1)}, u32[]{:S(2)}, u32[]{:S(2)}) collective-permute-start(bf16[1152,128]{1,0:T(8,128)(2,1)S(1)} %get-tuple-element.277), channel_id=1, source_target_pairs={{0,8},{4,12},{8,0},{12,4},{16,24},{20,28},{24,16},{28,20},{1,9},{5... | collective-permute-start | bytes 884744 | tf_op jit(solution)/shard_map/ppermute | solution.py:1410
  279.7 7.4 %collective-permute-start.53 = (f32[2,256]{1,0:T(2,128)S(1)}, f32[2,256]{1,0:T(2,128)S(1)}, u32[]{:S(2)}, u32[]{:S(2)}) collective-permute-start(f32[2,256]{1,0:T(2,128)S(1)} %get-tuple-element.268.refs_0_), channel_id=1, source_target_pairs={{0,4},{4,0},{8,12},{12,8},{16,20},{20,16},{24,28},{28,24},{1,5},{5... | collective-permute-start | bytes 6152 | tf_op jit(solution)/shard_map/ppermute | solution.py:1359
  280.6 6.6 %collective-permute-start.54 = (f32[2,256]{1,0:T(2,128)S(1)}, f32[2,256]{1,0:T(2,128)S(1)}, u32[]{:S(2)}, u32[]{:S(2)}) collective-permute-start(f32[2,256]{1,0:T(2,128)S(1)} %get-tuple-element.268.refs_0_), channel_id=1, source_target_pairs={{0,8},{4,12},{8,0},{12,4},{16,24},{20,28},{24,16},{28,20},{1,9},{5... | collective-permute-start | bytes 6152 | tf_op jit(solution)/shard_map/ppermute | solution.py:1359
  282.4 4.8 %collective-permute-start.55 = (f32[2,256]{1,0:T(2,128)S(1)}, f32[2,256]{1,0:T(2,128)S(1)}, u32[]{:S(2)}, u32[]{:S(2)}) collective-permute-start(f32[2,256]{1,0:T(2,128)S(1)} %get-tuple-element.268.refs_0_), channel_id=1, source_target_pairs={{0,12},{4,8},{8,4},{12,0},{16,28},{20,24},{24,20},{28,16},{1,13},{... | collective-permute-start | bytes 6152 | tf_op jit(solution)/shard_map/ppermute | solution.py:1359
  287.2 25.3 %collective-permute-start.62 = (bf16[768,128]{1,0:T(8,128)(2,1)S(1)}, bf16[768,128]{1,0:T(8,128)(2,1)S(1)}, u32[]{:S(2)}, u32[]{:S(2)}) collective-permute-start(bf16[768,128]{1,0:T(8,128)(2,1)S(1)} %get-tuple-element.286), channel_id=1, source_target_pairs={{0,4},{4,0},{8,12},{12,8},{16,20},{20,16},{24,28},{28,24},{1,5},{5... | collective-permute-start | bytes 589832 | tf_op jit(solution)/shard_map/ppermute | solution.py:1410
  288.1 4.6 %collective-permute-start.57 = (f32[2,256]{1,0:T(2,128)S(1)}, f32[2,256]{1,0:T(2,128)S(1)}, u32[]{:S(2)}, u32[]{:S(2)}) collective-permute-start(f32[2,256]{1,0:T(2,128)S(1)} %add.25.refs_7_), channel_id=1, source_target_pairs={{0,16},{4,20},{8,24},{12,28},{16,0},{20,4},{24,8},{28,12},{1,17},{... | collective-permute-start | bytes 6152 | tf_op jit(solution)/shard_map/ppermute | solution.py:1359
  292.7 19.8 %collective-permute-start.61 = (bf16[576,128]{1,0:T(8,128)(2,1)S(1)}, bf16[576,128]{1,0:T(8,128)(2,1)S(1)}, u32[]{:S(2)}, u32[]{:S(2)}) collective-permute-start(bf16[576,128]{1,0:T(8,128)(2,1)S(1)} %get-tuple-element.285), channel_id=1, source_target_pairs={{0,16},{4,20},{8,24},{12,28},{16,0},{20,4},{24,8},{28,12},{1,17},{... | collective-permute-start | bytes 442376 | tf_op jit(solution)/shard_map/ppermute | solution.py:1410
  312.5 9.6 %collective-permute-start.63 = (f32[2,256]{1,0:T(2,128)S(1)}, f32[2,256]{1,0:T(2,128)S(1)}, u32[]{:S(2)}, u32[]{:S(2)}) collective-permute-start(f32[2,256]{1,0:T(2,128)S(1)} %add.26.refs_7_), channel_id=1, source_target_pairs={{0,16},{4,20},{8,24},{12,28},{16,0},{20,4},{24,8},{28,12},{1,17},{... | collective-permute-start | bytes 6152 | tf_op jit(solution)/shard_map/ppermute | solution.py:1359
  322.1 12.4 %collective-permute-start.64 = (bf16[832,128]{1,0:T(8,128)(2,1)S(1)}, bf16[832,128]{1,0:T(8,128)(2,1)S(1)}, u32[]{:S(2)}, u32[]{:S(2)}) collective-permute-start(bf16[832,128]{1,0:T(8,128)(2,1)S(1)} %get-tuple-element.303), channel_id=1, source_target_pairs={{0,4},{4,0},{8,12},{12,8},{16,20},{20,16},{24,28},{28,24},{1,5},{5... | collective-permute-start | bytes 638984 | tf_op jit(solution)/shard_map/ppermute | solution.py:1410
  324.2 10.2 %collective-permute-start.66 = (bf16[576,128]{1,0:T(8,128)(2,1)S(1)}, bf16[576,128]{1,0:T(8,128)(2,1)S(1)}, u32[]{:S(2)}, u32[]{:S(2)}) collective-permute-start(bf16[576,128]{1,0:T(8,128)(2,1)S(1)} %stride_2s.1.refs_0_), channel_id=1, source_target_pairs={{0,16},{4,20},{8,24},{12,28},{16,0},{20,4},{24,8},{28,12},{1,17},{... | collective-permute-start | bytes 442376 | tf_op jit(solution)/shard_map/ppermute | solution.py:1410
  327.1 5.9 %collective-permute-start.65 = (bf16[384,128]{1,0:T(8,128)(2,1)S(1)}, bf16[384,128]{1,0:T(8,128)(2,1)S(1)}, u32[]{:S(2)}, u32[]{:S(2)}) collective-permute-start(bf16[384,128]{1,0:T(8,128)(2,1)S(1)} %get-tuple-element.304), channel_id=1, source_target_pairs={{0,8},{4,12},{8,0},{12,4},{16,24},{20,28},{24,16},{28,20},{1,9},{5... | collective-permute-start | bytes 294920 | tf_op jit(solution)/shard_map/ppermute | solution.py:1410
  335.0 10.0 %collective-permute-start.73 = (bf16[1152,128]{1,0:T(8,128)(2,1)S(1)}, bf16[1152,128]{1,0:T(8,128)(2,1)S(1)}, u32[]{:S(2)}, u32[]{:S(2)}) collective-permute-start(bf16[1152,128]{1,0:T(8,128)(2,1)S(1)} %bitcast.71), channel_id=1, source_target_pairs={{0,8},{4,12},{8,0},{12,4},{16,24},{20,28},{24,16},{28,20},{1,9},{5... | collective-permute-start | bytes 884744 | tf_op jit(solution)/shard_map/ppermute | solution.py:1410
  336.3 7.7 %collective-permute-start.75 = (bf16[192,128]{1,0:T(8,128)(2,1)S(1)}, bf16[192,128]{1,0:T(8,128)(2,1)S(1)}, u32[]{:S(2)}, u32[]{:S(2)}) collective-permute-start(bf16[192,128]{1,0:T(8,128)(2,1)S(1)} %get-tuple-element.321), channel_id=1, source_target_pairs={{0,16},{4,20},{8,24},{12,28},{16,0},{20,4},{24,8},{28,12},{1,17},{... | collective-permute-start | bytes 147464 | tf_op jit(solution)/shard_map/ppermute | solution.py:1410
  339.6 7.2 %collective-permute-start.67 = (bf16[208,128]{1,0:T(8,128)(2,1)S(1)}, bf16[208,128]{1,0:T(8,128)(2,1)S(1)}, u32[]{:S(2)}, u32[]{:S(2)}) collective-permute-start(bf16[208,128]{1,0:T(8,128)(2,1)S(1)} %get-tuple-element.311), channel_id=1, source_target_pairs={{0,8},{4,12},{8,0},{12,4},{16,24},{20,28},{24,16},{28,20},{1,9},{5... | collective-permute-start | bytes 159752 | tf_op jit(solution)/shard_map/ppermute | solution.py:1410
  339.7 7.1 %collective-permute-start.68 = (bf16[208,128]{1,0:T(8,128)(2,1)S(1)}, bf16[208,128]{1,0:T(8,128)(2,1)S(1)}, u32[]{:S(2)}, u32[]{:S(2)}) collective-permute-start(bf16[208,128]{1,0:T(8,128)(2,1)S(1)} %get-tuple-element.312), channel_id=1, source_target_pairs={{0,16},{4,20},{8,24},{12,28},{16,0},{20,4},{24,8},{28,12},{1,17},{... | collective-permute-start | bytes 159752 | tf_op jit(solution)/shard_map/ppermute | solution.py:1410
  341.4 5.9 %collective-permute-start.69 = (bf16[208,128]{1,0:T(8,128)(2,1)S(1)}, bf16[208,128]{1,0:T(8,128)(2,1)S(1)}, u32[]{:S(2)}, u32[]{:S(2)}) collective-permute-start(bf16[208,128]{1,0:T(8,128)(2,1)S(1)} %get-tuple-element.313), channel_id=1, source_target_pairs={{0,24},{4,28},{8,16},{12,20},{16,8},{20,12},{24,0},{28,4},{1,25},{... | collective-permute-start | bytes 159752 | tf_op jit(solution)/shard_map/ppermute | solution.py:1410
  344.1 7.7 %collective-permute-start.76 = (bf16[192,128]{1,0:T(8,128)(2,1)S(1)}, bf16[192,128]{1,0:T(8,128)(2,1)S(1)}, u32[]{:S(2)}, u32[]{:S(2)}) collective-permute-start(bf16[192,128]{1,0:T(8,128)(2,1)S(1)} %mid_2s.1.refs_0_), channel_id=1, source_target_pairs={{0,16},{4,20},{8,24},{12,28},{16,0},{20,4},{24,8},{28,12},{1,17},{... | collective-permute-start | bytes 147464 | tf_op jit(solution)/shard_map/ppermute | solution.py:1410
  345.7 16.4 %collective-permute-start.74 = (bf16[2304,128]{1,0:T(8,128)(2,1)S(1)}, bf16[2304,128]{1,0:T(8,128)(2,1)S(1)}, u32[]{:S(2)}, u32[]{:S(2)}) collective-permute-start(bf16[2304,128]{1,0:T(8,128)(2,1)S(1)} %bitcast.69), channel_id=1, source_target_pairs={{0,4},{4,0},{8,12},{12,8},{16,20},{20,16},{24,28},{28,24},{1,5},{5... | collective-permute-start | bytes 1769480 | tf_op jit(solution)/shard_map/ppermute | solution.py:1410
  347.4 5.1 %collective-permute-start.70 = (bf16[208,128]{1,0:T(8,128)(2,1)S(1)}, bf16[208,128]{1,0:T(8,128)(2,1)S(1)}, u32[]{:S(2)}, u32[]{:S(2)}) collective-permute-start(bf16[208,128]{1,0:T(8,128)(2,1)S(1)} %last_1s.1.refs_0_), channel_id=1, source_target_pairs={{0,8},{4,12},{8,0},{12,4},{16,24},{20,28},{24,16},{28,20},{1,9},{5... | collective-permute-start | bytes 159752 | tf_op jit(solution)/shard_map/ppermute | solution.py:1410
  347.4 5.4 %collective-permute-start.71 = (bf16[208,128]{1,0:T(8,128)(2,1)S(1)}, bf16[208,128]{1,0:T(8,128)(2,1)S(1)}, u32[]{:S(2)}, u32[]{:S(2)}) collective-permute-start(bf16[208,128]{1,0:T(8,128)(2,1)S(1)} %last_1s.1.refs_0_), channel_id=1, source_target_pairs={{0,16},{4,20},{8,24},{12,28},{16,0},{20,4},{24,8},{28,12},{1,17},{... | collective-permute-start | bytes 159752 | tf_op jit(solution)/shard_map/ppermute | solution.py:1410
  350.7 6.0 %collective-permute-start.72 = (bf16[208,128]{1,0:T(8,128)(2,1)S(1)}, bf16[208,128]{1,0:T(8,128)(2,1)S(1)}, u32[]{:S(2)}, u32[]{:S(2)}) collective-permute-start(bf16[208,128]{1,0:T(8,128)(2,1)S(1)} %last_1s.1.refs_0_), channel_id=1, source_target_pairs={{0,24},{4,28},{8,16},{12,20},{16,8},{20,12},{24,0},{28,4},{1,25},{... | collective-permute-start | bytes 159752 | tf_op jit(solution)/shard_map/ppermute | solution.py:1410
  352.4 6.1 %collective-permute-start.77 = (bf16[384,128]{1,0:T(8,128)(2,1)S(1)}, bf16[384,128]{1,0:T(8,128)(2,1)S(1)}, u32[]{:S(2)}, u32[]{:S(2)}) collective-permute-start(bf16[384,128]{1,0:T(8,128)(2,1)S(1)} %bitcast.79), channel_id=1, source_target_pairs={{0,8},{4,12},{8,0},{12,4},{16,24},{20,28},{24,16},{28,20},{1,9},{5... | collective-permute-start | bytes 294920 | tf_op jit(solution)/shard_map/ppermute | solution.py:1410
  357.3 10.1 %collective-permute-start.79 = (bf16[832,128]{1,0:T(8,128)(2,1)S(1)}, bf16[832,128]{1,0:T(8,128)(2,1)S(1)}, u32[]{:S(2)}, u32[]{:S(2)}) collective-permute-start(bf16[832,128]{1,0:T(8,128)(2,1)S(1)} %bitcast.73), channel_id=1, source_target_pairs={{0,4},{4,0},{8,12},{12,8},{16,20},{20,16},{24,28},{28,24},{1,5},{5... | collective-permute-start | bytes 638984 | tf_op jit(solution)/shard_map/ppermute | solution.py:1410
  359.1 8.3 %collective-permute-start.78 = (bf16[768,128]{1,0:T(8,128)(2,1)S(1)}, bf16[768,128]{1,0:T(8,128)(2,1)S(1)}, u32[]{:S(2)}, u32[]{:S(2)}) collective-permute-start(bf16[768,128]{1,0:T(8,128)(2,1)S(1)} %bitcast.75), channel_id=1, source_target_pairs={{0,4},{4,0},{8,12},{12,8},{16,20},{20,16},{24,28},{28,24},{1,5},{5... | collective-permute-start | bytes 589832 | tf_op jit(solution)/shard_map/ppermute | solution.py:1410
  (70 other events, 444.7 us)
Sparse Core Ops, SparseCore 0:
  47.8 46.0 all-gather.4
  95.4 58.9 all-gather.6
  217.5 98.4 all-reduce.4
